TPU v7x, 32 devices: a whole 2x2x4 slice. The times are simulated.
32 devices in a mesh: region: 16 (over z, y, core), sub: 2 (over x).
Axes of the slice: x: 2, y: 2, z: 4, core: 2. Of those that a mesh axis runs over, the one named last changes fastest.
Arguments:
- sources: bfloat16 [32, 2048, 1280], P(('region', 'sub')), may hold values from -6 to 6
- coupling: bfloat16 [32, 2048, 2048], P(('region', 'sub')), may hold values from -0.0625 to 0.0625
- self_term: float32 [32, 2048], P(('region', 'sub')), may hold values from 0.25 to 1
- history: float32 [32, 4, 8, 640], P(('region', 'sub')), may hold values from -6 to 6
- line_nodes: int32 [32, 4, 8], P(('region', 'sub')), may hold values from -1 to 2047, as said below
- line_admit: float32 [32, 4, 8], P(('region', 'sub')), may hold values from 0 to 1, as said below
- term_region: int32 [8192, 1], P(('region', 'sub')), may hold values from 0 to 15; in each aligned block of 256 rows (0 to 255, 256 to 511, ...) at most 32 rows name the same one
- old_samples: bfloat16 [8192, 1280], P(('region', 'sub')), may hold values from -6 to 6
- prior_phasor: float32 [8192, 2, 128], P(('region', 'sub')), may hold values from -6 to 6
Outputs:
- next_history: float32 [32, 4, 8, 640], P(('region', 'sub'))
- node_voltages: bfloat16 [32, 2048, 1280], P(('region', 'sub'))
- phasors: float32 [16384, 2, 2, 128], P(('region', 'sub'))
Inputs may be any that keep to these rules, and one draw needn't show every extreme that they name: line_nodes[a, d, k] is -1 for an empty slot and for every slot of a direction with no subsystem; each subsystem has lines to each of its up to 4 neighbours in the directions of the steps, 1 to 8 lines a pair, in the first slots; [a, d, k] and the slot k of the opposite direction at the neighbour are both -1 or are the two ends of one line; some pair uses all 8 slots. line_admit is equal at the two ends of a line; it is 0 exactly where line_nodes is -1, else 0.25 or more. `term_region`: among the 256 terminals of one subsystem at most 32 name the same region, and in every draw some region is named by exactly 32 of one subsystem's terminals.
All inputs are finite; a program needn't handle non-finite values.
Results may differ from a plain program's by a relative error of at most 0.003.
Values sent between devices are 32-bit elements; how exact they have to be, the bound alone decides.
No kernel may reach another device: no remote copies, remote signals or barrier semaphores. Data moves between devices by JAX's collectives and lax.ppermute only.
A program may use at most 128 MiB of HBM per device.

v0:
```python
import math

import jax
import jax.numpy as jnp
from jax import lax
from jax.sharding import PartitionSpec as P

NODES = 2048
NEIGH = 4
LPP = 8
DELAY = 40
SPANS = 2
SCEN = 16
TERM_DEV = 256
BINS = 8
DFT_LEN = 2048


def shifted(shard, axis, by):
    length = lax.axis_size(axis)
    pairs = [(i, i + by) for i in range(length) if 0 <= i + by < length]
    return lax.ppermute(shard, axis, pairs)


def fit_table():
    step_index = jnp.arange(SPANS * DELAY, dtype=jnp.int32)
    harmonic = jnp.arange(1, BINS + 1, dtype=jnp.int32)
    product = step_index[:, None] * harmonic[None, :] % DFT_LEN
    angles = product.astype(jnp.float32) * (2.0 * math.pi / DFT_LEN)
    norm_scale = 1.0 / math.sqrt(DFT_LEN)
    twiddle = jnp.stack([jnp.cos(angles), -jnp.sin(angles)], axis=1) * norm_scale
    span_ends = (jnp.arange(SPANS, dtype=jnp.int32) + 1) * DELAY
    reached = (step_index[:, None] < span_ends[None, :]).astype(jnp.float32)
    same_scen = jnp.eye(SCEN, dtype=jnp.float32)
    table = jnp.einsum("uj,uch,st->usjcht", reached, twiddle, same_scen)
    return table.reshape(SPANS * DELAY * SCEN, SPANS * 2 * BINS * SCEN)


def phasor_fit(differences, prior):
    row_count = differences.shape[0]
    running = jnp.dot(
        differences,
        fit_table(),
        precision=lax.Precision.HIGHEST,
        preferred_element_type=jnp.float32,
    )
    return running.reshape(row_count, SPANS, 2, BINS * SCEN) + prior[:, None]


def send_lines(outgoing):
    from_lower_sub = shifted(outgoing[1], "sub", 1)
    from_upper_sub = shifted(outgoing[0], "sub", -1)
    from_lower_region = shifted(outgoing[3], "region", 1)
    from_upper_region = shifted(outgoing[2], "region", -1)
    return jnp.stack([from_lower_sub, from_upper_sub, from_lower_region, from_upper_region], axis=0)


def body(
    sources,
    coupling,
    self_term,
    history,
    line_nodes,
    line_admit,
    term_region,
    old_samples,
    prior_phasor,
):
    source_block = sources[0]
    matrix = coupling[0]
    self_gain = self_term[0][:, None]
    incoming = history[0]
    span_cols = DELAY * SCEN
    end_nodes = line_nodes[0].reshape(-1)
    admit_col = line_admit[0].reshape(-1, 1)
    live_slot = end_nodes >= 0
    target_rows = jnp.where(live_slot, end_nodes, NODES)
    pick_rows = jnp.where(live_slot, end_nodes, 0)
    pieces = []
    node_pieces = []
    for span_index in range(SPANS):
        low = span_index * span_cols
        span_src = source_block[:, low : low + span_cols]
        line_rows = incoming.reshape(NEIGH * LPP, span_cols)
        injection = (
            jnp.zeros((NODES, span_cols), jnp.float32)
            .at[target_rows]
            .add(line_rows, mode="drop")
            .astype(jnp.bfloat16)
        )
        source_part = jnp.dot(matrix, span_src, preferred_element_type=jnp.float32)
        voltages = source_part + jnp.dot(matrix, injection, preferred_element_type=jnp.float32)
        voltages = voltages + self_gain * (
            span_src.astype(jnp.float32) + injection.astype(jnp.float32)
        )
        pieces.append(voltages[:TERM_DEV])
        node_pieces.append(voltages.astype(jnp.bfloat16))
        line_volts = voltages[pick_rows]
        outgoing = jnp.where(live_slot[:, None], 2.0 * admit_col * line_volts - line_rows, 0.0)
        incoming = send_lines(outgoing.reshape(NEIGH, LPP, span_cols))
    next_history = incoming[None]
    node_voltages = jnp.concatenate(node_pieces, axis=1)[None]
    waveforms = jnp.concatenate(pieces, axis=1)
    differences = waveforms - old_samples.astype(jnp.float32)
    region_count = lax.axis_size("region")
    capacity = max(2, 2 * TERM_DEV // region_count)
    regions = term_region[:, 0]
    onehot = (regions[:, None] == jnp.arange(region_count, dtype=jnp.int32)[None, :]).astype(
        jnp.int32
    )
    rank_in = jnp.cumsum(onehot, axis=0) - onehot
    slot_index = jnp.sum(rank_in * onehot, axis=1)
    dest_row = regions * capacity + slot_index
    slot_ids = jnp.arange(region_count * capacity, dtype=jnp.int32)
    pack_table = (slot_ids[:, None] == dest_row[None, :]).astype(jnp.float32)
    fitted = phasor_fit(differences, prior_phasor)
    flat = fitted.reshape(fitted.shape[0], -1)
    packed = jnp.dot(
        pack_table, flat, precision=lax.Precision.HIGHEST, preferred_element_type=jnp.float32
    )
    result = lax.all_to_all(
        packed.reshape((region_count, capacity) + fitted.shape[1:]),
        "region",
        split_axis=0,
        concat_axis=0,
        tiled=True,
    )
    phasors = result.reshape(region_count * capacity, SPANS, 2, BINS * SCEN)
    return (next_history, node_voltages, phasors)


def solution(mesh):
    return jax.shard_map(
        body,
        mesh=mesh,
        in_specs=(
            P(("region", "sub"), None, None),
            P(("region", "sub"), None, None),
            P(("region", "sub"), None),
            P(("region", "sub"), None, None, None),
            P(("region", "sub"), None, None),
            P(("region", "sub"), None, None),
            P(("region", "sub"), None),
            P(("region", "sub"), None),
            P(("region", "sub"), None, None),
        ),
        out_specs=(
            P(("region", "sub"), None, None, None),
            P(("region", "sub"), None, None),
            P(("region", "sub"), None, None, None),
        ),
        check_vma=False,
    )
```

profile of v0, /device:TPU:10, one launch (start us, length us, event | category | flops | bytes accessed | tf_op | source)
XLA Modules:
  0.0 184.3 jit_solution(4719080472505791524)
XLA Ops:
  2.1 8.0 %copy.36 = bf16[1,2048,1280]{1,2,0:T(8,128)(2,1)} copy(bf16[1,2048,1280]{2,1,0:T(8,128)(2,1)} %param.9) | data formatting | bytes 10485760 | tf_op args[0]
  10.6 3.4 %scatter_custom_fusion = f32[2048,640]{1,0:T(8,128)} fusion(s32[32]{0:T(128)S(1)} %get-tuple-element.23, f32[]{:T(128)} %constant.15.clone.1, f32[1,4,8,640]{3,2,1,0:T(8,128)S(1)} %copy-done.2), kind=kCustom, calls=%fused_computation.22 | custom fusion | flops 20480 | bytes 5324804 | tf_op jit(solution)/shard_map/scatter-add | solution.py:88
  14.0 5.1 %copy.37 = bf16[2048,640]{0,1:T(8,128)(2,1)} copy(f32[2048,640]{1,0:T(8,128)} %scatter_custom_fusion) | data formatting | bytes 7864320 | tf_op jit(solution)/shard_map/scatter-add | solution.py:88
  19.1 11.3 %fusion.4 = f32[2048,640]{0,1:T(8,128)} fusion(bf16[1,2048,2048]{2,1,0:T(8,128)(2,1)} %param.10, bf16[2048,1280]{0,1:T(8,128)(2,1)} %bitcast.108), kind=kOutput, calls=%fused_computation.9 | convolution fusion | flops 5368709120 | bytes 16252928 | tf_op jit(solution)/shard_map/dot_general | solution.py:91
  30.4 13.8 %fusion.60 = (bf16[2048,640]{0,1:T(8,128)(2,1)}, f32[2048,640]{0,1:T(8,128)}) fusion(bf16[2048,640]{0,1:T(8,128)(2,1)} %copy.37, bf16[2048,1280]{0,1:T(8,128)(2,1)S(1)} %bitcast.113, f32[2048]{0:T(1024)S(1)} %bitcast.123, f32[2048,640]{0,1:T(8,128)} %fusion.4, bf16[1,2048,2048]{2,1,0:T(8,128)(2,1)} %param.10), kind=kOutput, calls=%fused_computation.88 | convolution fusion | flops 5377884160 | bytes 29368320 | tf_op jit(solution)/shard_map/dot_general | solution.py:92
  44.1 5.9 %copy.38 = f32[2048,640]{1,0:T(8,128)} copy(f32[2048,640]{0,1:T(8,128)} %get-tuple-element.27) | data formatting | bytes 10485760 | tf_op jit(solution)/shard_map/add | solution.py:93
  50.3 3.1 %gather_fusion = f32[32,640]{1,0:T(8,128)S(1)} fusion(f32[2048,640]{1,0:T(8,128)} %copy.38, s32[1024]{0:T(1024)S(1)} %pad_clamp_fusion), kind=kCustom, calls=%fused_computation | custom fusion | bytes 163968 | tf_op jit(solution)/shard_map/gather | solution.py:98
  54.1 2.7 %collective-permute-start.3 = (f32[8,640]{1,0:T(8,128)}, f32[8,640]{1,0:T(8,128)}, u32[]{:S(2)}, u32[]{:S(2)}) collective-permute-start(f32[8,640]{1,0:T(8,128)} %get-tuple-element.17), channel_id=1, source_target_pairs={{2,0},{4,2},{6,4},{8,6},{10,8},{12,10},{14,12},{16,14},{18,16},{20... | collective-permute-start | bytes 61448 | tf_op jit(solution)/shard_map/ppermute | solution.py:22
  56.9 1.3 collective-permute-start
  58.2 5.7 %collective-permute-start.1 = (f32[8,640]{1,0:T(8,128)}, f32[8,640]{1,0:T(8,128)}, u32[]{:S(2)}, u32[]{:S(2)}) collective-permute-start(f32[8,640]{1,0:T(8,128)} %get-tuple-element.19), channel_id=1, source_target_pairs={{1,0},{3,2},{5,4},{7,6},{9,8},{11,10},{13,12},{15,14},{17,16},{19,... | collective-permute-start | bytes 61448 | tf_op jit(solution)/shard_map/ppermute | solution.py:22
  63.9 2.2 %collective-permute-start.2 = (f32[8,640]{1,0:T(8,128)}, f32[8,640]{1,0:T(8,128)}, u32[]{:S(2)}, u32[]{:S(2)}) collective-permute-start(f32[8,640]{1,0:T(8,128)} %get-tuple-element.18), channel_id=1, source_target_pairs={{0,2},{2,4},{4,6},{6,8},{8,10},{10,12},{12,14},{14,16},{16,18},{18... | collective-permute-start | bytes 61448 | tf_op jit(solution)/shard_map/ppermute | solution.py:22
  66.1 11.1 %fusion.6 = f32[2048,640]{0,1:T(8,128)} fusion(bf16[1,2048,2048]{2,1,0:T(8,128)(2,1)} %param.10, bf16[2048,1280]{0,1:T(8,128)(2,1)} %bitcast.109), kind=kOutput, calls=%fused_computation.11 | convolution fusion | flops 5368709120 | bytes 16252928 | tf_op jit(solution)/shard_map/dot_general | solution.py:91
  79.3 9.7 %multiply_bitcast_fusion = f32[80,16,2,2,8,16]{5,4,3,2,1,0:T(8,128)} fusion(f32[16,16]{1,0:T(8,128)S(1)} %fusion.46, f32[80,2,8,2]{2,1,3,0:T(2,128)S(1)} %broadcast_multiply_fusion), kind=kLoop, calls=%fused_computation.4 | loop fusion | flops 655360 | bytes 2632704 | tf_op jit(solution)/shard_map/uj,uch,st->usjcht/transpose | solution.py:35
  89.0 1.1 slice.79
  90.1 18.2 %reshape.255 = f32[1280,512]{1,0:T(8,128)} reshape(f32[80,16,2,2,8,16]{5,4,3,2,1,0:T(8,128)} %multiply_bitcast_fusion) | data formatting | bytes 5242880 | tf_op jit(solution)/shard_map/reshape | solution.py:36
  108.3 2.1 %copy.53 = f32[512,1280]{1,0:T(8,128)S(1)} copy(f32[512,1280]{0,1:T(8,128)} %bitcast.107) | data formatting | bytes 5242880 | tf_op jit(solution)/shard_map/dot_general | solution.py:41
  110.5 2.2 %copy.42 = bf16[256,1280]{0,1:T(8,128)(2,1)} copy(bf16[256,1280]{1,0:T(8,128)(2,1)} %param.16) | data formatting | bytes 1310720 | tf_op args[7]
  113.8 3.7 %scatter_custom_fusion.1 = f32[2048,640]{1,0:T(8,128)} fusion(s32[32]{0:T(128)} %copy-done.9, f32[]{:T(128)} %constant.15.clone.1, f32[1,8,640]{2,1,0:T(8,128)} %bitcast.10, f32[]{:T(128)} %constant.46, f32[1,8,640]{2,1,0:T(8,128)} %bitcast.9, f32[1,8,640]{2,1,0:T(8,128)} %bitcast.8, f32[1,8,640]{2,1,0:T(8,128)} %bitcast.7), kind=kCustom, calls=%fused_computation.20 | custom fusion | flops 81920 | bytes 5325824 | tf_op jit(solution)/shard_map/scatter-add | solution.py:88
  117.5 5.0 %copy.39 = bf16[2048,640]{0,1:T(8,128)(2,1)} copy(f32[2048,640]{1,0:T(8,128)} %scatter_custom_fusion.1) | data formatting | bytes 7864320 | tf_op jit(solution)/shard_map/scatter-add | solution.py:88
  122.5 12.9 %fusion.59 = (bf16[2048,640]{0,1:T(8,128)(2,1)}, f32[2048,640]{0,1:T(8,128)S(1)}) fusion(bf16[2048,640]{0,1:T(8,128)(2,1)} %copy.39, bf16[2048,1280]{0,1:T(8,128)(2,1)} %bitcast.110, f32[2048]{0:T(1024)} %bitcast.122, f32[2048,640]{0,1:T(8,128)} %fusion.6, bf16[1,2048,2048]{2,1,0:T(8,128)(2,1)} %param.10), kind=kOutput, calls=%fused_computation.87 | convolution fusion | flops 5377884160 | bytes 29368320 | tf_op jit(solution)/shard_map/dot_general | solution.py:92
  135.5 2.3 %fusion.31 = f32[2,2,128,256,1]{3,2,1,0,4:T(8,128)S(1)} fusion(f32[2,2,128,1280]{3,2,1,0:T(8,128)S(1)} %bitcast.106, f32[256,640]{0,1:T(8,128)S(1)} %slice.80, f32[256,640]{0,1:T(8,128)S(1)} %slice.79, bf16[256,1280]{0,1:T(8,128)(2,1)S(1)} %copy-done.1, f32[256,2,128]{0,2,1:T(8,128)S(1)} %copy.46), kind=kOutput, calls=%fused_computation.33 | convolution fusion | flops 2014380032 | bytes 5373952 | tf_op jit(solution)/shard_map/dot_general | solution.py:41
  137.8 1.6 fusion.34
  139.4 6.5 %all-to-all-start = ((f32[16,32,2,2,128]{4,1,3,2,0:T(8,128)}), f32[16,32,2,2,128]{4,1,3,2,0:T(8,128)S(1)}, u32[]{:S(2)}, u32[]{:S(2)}) async-start(f32[16,32,2,2,128]{4,1,3,2,0:T(8,128)} %fusion.34), calls=%async_computation | async-start | bytes 2097152 | tf_op jit(solution)/shard_map/all_to_all | solution.py:121
  146.0 5.9 %copy.40 = f32[2048,640]{1,0:T(8,128)} copy(f32[2048,640]{0,1:T(8,128)} %copy-done) | data formatting | bytes 10485760 | tf_op jit(solution)/shard_map/add | solution.py:93
  151.9 3.1 %gather_fusion.1 = f32[32,640]{1,0:T(8,128)S(1)} fusion(f32[2048,640]{1,0:T(8,128)} %copy.40, s32[1024]{0:T(1024)S(1)} %pad_clamp_fusion), kind=kCustom, calls=%fused_computation.1 | custom fusion | bytes 163968 | tf_op jit(solution)/shard_map/gather | solution.py:98
  155.9 1.3 collective-permute-start.4
  157.2 4.5 %collective-permute-start.5 = (f32[8,640]{1,0:T(8,128)S(1)}, f32[8,640]{1,0:T(8,128)S(1)}, u32[]{:S(2)}, u32[]{:S(2)}) collective-permute-start(f32[8,640]{1,0:T(8,128)S(1)} %get-tuple-element.15), channel_id=1, source_target_pairs={{1,0},{3,2},{5,4},{7,6},{9,8},{11,10},{13,12},{15,14},{17,16},{19,... | collective-permute-start | bytes 61448 | tf_op jit(solution)/shard_map/ppermute | solution.py:22
  161.8 1.9 %collective-permute-start.6 = (f32[8,640]{1,0:T(8,128)S(1)}, f32[8,640]{1,0:T(8,128)S(1)}, u32[]{:S(2)}, u32[]{:S(2)}) collective-permute-start(f32[8,640]{1,0:T(8,128)S(1)} %get-tuple-element.14), channel_id=1, source_target_pairs={{0,2},{2,4},{4,6},{6,8},{8,10},{10,12},{12,14},{14,16},{16,18},{18... | collective-permute-start | bytes 61448 | tf_op jit(solution)/shard_map/ppermute | solution.py:22
  163.7 4.5 %collective-permute-start.7 = (f32[8,640]{1,0:T(8,128)S(1)}, f32[8,640]{1,0:T(8,128)S(1)}, u32[]{:S(2)}, u32[]{:S(2)}) collective-permute-start(f32[8,640]{1,0:T(8,128)S(1)} %get-tuple-element.13), channel_id=1, source_target_pairs={{2,0},{4,2},{6,4},{8,6},{10,8},{12,10},{14,12},{16,14},{18,16},{20... | collective-permute-start | bytes 61448 | tf_op jit(solution)/shard_map/ppermute | solution.py:22
  168.2 5.7 %maximum_bitcast_fusion = bf16[1,2048,1280]{1,2,0:T(8,128)(2,1)} fusion(bf16[2048,640]{0,1:T(8,128)(2,1)} %get-tuple-element.24, bf16[2048,640]{0,1:T(8,128)(2,1)} %get-tuple-element.26), kind=kLoop, calls=%fused_computation.13 | loop fusion | flops 10485760 | bytes 10485760 | tf_op jit(solution)/shard_map/broadcast_in_dim | solution.py:102
  173.9 7.9 %copy.48 = bf16[1,2048,1280]{2,1,0:T(8,128)(2,1)} copy(bf16[1,2048,1280]{1,2,0:T(8,128)(2,1)} %maximum_bitcast_fusion) | data formatting | bytes 10485760
  182.5 1.8 copy.49
  (65 shorter events, 7.6 us)
Async XLA Ops:
  2.1 8.5 %copy-start.2 = (f32[1,4,8,640]{3,2,1,0:T(8,128)S(1)}, f32[1,4,8,640]{3,2,1,0:T(8,128)}, u32[]{:S(2)}) copy-start(f32[1,4,8,640]{3,2,1,0:T(8,128)} %param.12) | copy-start | bytes 245764
  10.1 0.5 copy-start.9
  14.0 16.3 %slice-start = ((s8[5242880]{0:T(1024)(128)(4,1)}), s8[1048576]{0:T(1024)(128)(4,1)S(1)}, s32[]{:S(2)}) async-start(s8[5242880]{0:T(1024)(128)(4,1)} %bitcast.111), calls=%async_computation.1 | async-start | bytes 2097152
  19.1 11.3 %slice-start.1 = ((s8[5242880]{0:T(1024)(128)(4,1)}), s8[4194304]{0:T(1024)(128)(4,1)S(1)}, s32[]{:S(2)}) async-start(s8[5242880]{0:T(1024)(128)(4,1)} %bitcast.111), calls=%async_computation.2 | async-start | bytes 8388608
  19.1 11.3 %copy-start.8 = (f32[1,2048]{1,0:T(1,128)S(1)}, f32[1,2048]{1,0:T(1,128)}, u32[]{:S(2)}) copy-start(f32[1,2048]{1,0:T(1,128)} %param.11) | copy-start | bytes 24580
  44.1 5.9 %copy-start.7 = (f32[1,4,8]{2,1,0:T(4,128)S(1)}, f32[1,4,8]{2,1,0:T(4,128)}, u32[]{:S(2)}) copy-start(f32[1,4,8]{2,1,0:T(4,128)} %param.14) | copy-start | bytes 388
  50.3 27.0 %copy-start.5 = (pred[32]{0:T(512)(128)(4,1)}, pred[32]{0:T(512)(128)(4,1)S(1)}, u32[]{:S(2)}) copy-start(pred[32]{0:T(512)(128)(4,1)S(1)} %ge.23) | copy-start | bytes 100
  54.1 59.6 %collective-permute-start.3 = (f32[8,640]{1,0:T(8,128)}, f32[8,640]{1,0:T(8,128)}, u32[]{:S(2)}, u32[]{:S(2)}) collective-permute-start(f32[8,640]{1,0:T(8,128)} %get-tuple-element.17), channel_id=1, source_target_pairs={{2,0},{4,2},{6,4},{8,6},{10,8},{12,10},{14,12},{16,14},{18,16},{20... | collective-permute-start | bytes 61448 | tf_op jit(solution)/shard_map/ppermute | solution.py:22
  56.9 56.9 %collective-permute-start = (f32[8,640]{1,0:T(8,128)}, f32[8,640]{1,0:T(8,128)}, u32[]{:S(2)}, u32[]{:S(2)}) collective-permute-start(f32[8,640]{1,0:T(8,128)} %get-tuple-element.16), channel_id=1, source_target_pairs={{0,1},{2,3},{4,5},{6,7},{8,9},{10,11},{12,13},{14,15},{16,17},{18,... | collective-permute-start | bytes 61448 | tf_op jit(solution)/shard_map/ppermute | solution.py:22
  58.2 55.6 %collective-permute-start.1 = (f32[8,640]{1,0:T(8,128)}, f32[8,640]{1,0:T(8,128)}, u32[]{:S(2)}, u32[]{:S(2)}) collective-permute-start(f32[8,640]{1,0:T(8,128)} %get-tuple-element.19), channel_id=1, source_target_pairs={{1,0},{3,2},{5,4},{7,6},{9,8},{11,10},{13,12},{15,14},{17,16},{19,... | collective-permute-start | bytes 61448 | tf_op jit(solution)/shard_map/ppermute | solution.py:22
  63.9 13.7 %copy-start.3 = (s32[256,1]{0,1:T(1,128)S(1)}, s32[256,1]{0,1:T(1,128)}, u32[]{:S(2)}) copy-start(s32[256,1]{0,1:T(1,128)} %param.15) | copy-start | bytes 3076
  63.9 49.9 %collective-permute-start.2 = (f32[8,640]{1,0:T(8,128)}, f32[8,640]{1,0:T(8,128)}, u32[]{:S(2)}, u32[]{:S(2)}) collective-permute-start(f32[8,640]{1,0:T(8,128)} %get-tuple-element.18), channel_id=1, source_target_pairs={{0,2},{2,4},{4,6},{6,8},{8,10},{10,12},{12,14},{14,16},{16,18},{18... | collective-permute-start | bytes 61448 | tf_op jit(solution)/shard_map/ppermute | solution.py:22
  122.5 13.0 %copy-start.1 = (bf16[256,1280]{0,1:T(8,128)(2,1)S(1)}, bf16[256,1280]{0,1:T(8,128)(2,1)}, u32[]{:S(2)}) copy-start(bf16[256,1280]{0,1:T(8,128)(2,1)} %copy.42) | copy-start | bytes 1966084
  135.4 2.4 %copy-start = (f32[2048,640]{0,1:T(8,128)}, f32[2048,640]{0,1:T(8,128)S(1)}, u32[]{:S(2)}) copy-start(f32[2048,640]{0,1:T(8,128)S(1)} %get-tuple-element.25) | copy-start | bytes 15728644
  135.4 2.4 %copy-start.4 = (s32[256]{0:T(256)S(1)}, s32[256]{0:T(256)}, u32[]{:S(2)}) copy-start(s32[256]{0:T(256)} %multiply_add_fusion.1) | copy-start | bytes 3076
  139.4 43.0 %all-to-all-start = ((f32[16,32,2,2,128]{4,1,3,2,0:T(8,128)}), f32[16,32,2,2,128]{4,1,3,2,0:T(8,128)S(1)}, u32[]{:S(2)}, u32[]{:S(2)}) async-start(f32[16,32,2,2,128]{4,1,3,2,0:T(8,128)} %fusion.34), calls=%async_computation | async-start | bytes 2097152 | tf_op jit(solution)/shard_map/all_to_all | solution.py:121
  146.0 9.1 %copy-start.6 = (pred[32]{0:T(512)(128)(4,1)S(1)}, pred[32]{0:T(512)(128)(4,1)}, u32[]{:S(2)}) copy-start(pred[32]{0:T(512)(128)(4,1)} %copy-done.5) | copy-start | bytes 100
  155.9 25.9 %collective-permute-start.4 = (f32[8,640]{1,0:T(8,128)S(1)}, f32[8,640]{1,0:T(8,128)S(1)}, u32[]{:S(2)}, u32[]{:S(2)}) collective-permute-start(f32[8,640]{1,0:T(8,128)S(1)} %get-tuple-element.12), channel_id=1, source_target_pairs={{0,1},{2,3},{4,5},{6,7},{8,9},{10,11},{12,13},{14,15},{16,17},{18,... | collective-permute-start | bytes 61448 | tf_op jit(solution)/shard_map/ppermute | solution.py:22
  157.2 24.6 %collective-permute-start.5 = (f32[8,640]{1,0:T(8,128)S(1)}, f32[8,640]{1,0:T(8,128)S(1)}, u32[]{:S(2)}, u32[]{:S(2)}) collective-permute-start(f32[8,640]{1,0:T(8,128)S(1)} %get-tuple-element.15), channel_id=1, source_target_pairs={{1,0},{3,2},{5,4},{7,6},{9,8},{11,10},{13,12},{15,14},{17,16},{19,... | collective-permute-start | bytes 61448 | tf_op jit(solution)/shard_map/ppermute | solution.py:22
  161.8 20.0 %collective-permute-start.6 = (f32[8,640]{1,0:T(8,128)S(1)}, f32[8,640]{1,0:T(8,128)S(1)}, u32[]{:S(2)}, u32[]{:S(2)}) collective-permute-start(f32[8,640]{1,0:T(8,128)S(1)} %get-tuple-element.14), channel_id=1, source_target_pairs={{0,2},{2,4},{4,6},{6,8},{8,10},{10,12},{12,14},{14,16},{16,18},{18... | collective-permute-start | bytes 61448 | tf_op jit(solution)/shard_map/ppermute | solution.py:22
  163.7 18.1 %collective-permute-start.7 = (f32[8,640]{1,0:T(8,128)S(1)}, f32[8,640]{1,0:T(8,128)S(1)}, u32[]{:S(2)}, u32[]{:S(2)}) collective-permute-start(f32[8,640]{1,0:T(8,128)S(1)} %get-tuple-element.13), channel_id=1, source_target_pairs={{2,0},{4,2},{6,4},{8,6},{10,8},{12,10},{14,12},{16,14},{18,16},{20... | collective-permute-start | bytes 61448 | tf_op jit(solution)/shard_map/ppermute | solution.py:22
where the time goes:
time: 186 us; the launch traced here: 184 us
  local copies, waits for them, and re-layouts  73 us (39%)
  matrix products  53 us (28%)
  starting transfers between devices  30.8 us (17%)
  other arithmetic  26.5 us (14%)
    dot_general x2, matrix products, body(): jnp.dot(matrix, injection, preferred_element_type=jnp.float32)  26.7 us
    ppermute x8, starting transfers between devices, shifted(): return lax.ppermute(shard, axis, pairs)  24.3 us
    dot_general x2, matrix products, body(): source_part = jnp.dot(matrix, span_src, preferred_element_type=jnp.float32)  22.4 us
    unnamed x29, local copies, waits for them, and re-layouts  21.4 us
    reshape x1, local copies, waits for them, and re-layouts, fit_table(): return table.reshape(SPANS * DELAY * SCEN, SPANS * 2 * BINS * SCEN)  18.2 us
    add x2, local copies, waits for them, and re-layouts, body(): voltages + self_gain * (span_src.astype(jnp.float32) + injection.astype(j...  11.8 us
    scatter-add x2, local copies, waits for them, and re-layouts, body(): injection = jnp.zeros((NODES, span_cols), jnp.float32).at[target_rows].ad...  10 us
    transpose x1, other arithmetic, fit_table(): table = jnp.einsum('uj,uch,st->usjcht', reached, twiddle, same_scen)  9.72 us
  transfers between devices with their start and end apart: 9, of which 0 were waited for; matrix products, arithmetic and copies ran while one was open for 39% of the time, Pallas kernels for 0%

commit v1 on v0

v1 whole, which is shorter than its diff:
```python
import functools
import math

import jax
import jax.numpy as jnp
import numpy as np
from jax import lax
from jax.experimental import pallas as pl
from jax.experimental.pallas import tpu as pltpu
from jax.sharding import PartitionSpec as P

NODES = 2048
NEIGH = 4
LPP = 8
DELAY = 40
SPANS = 2
SCEN = 16
TERM_DEV = 256
BINS = 8
DFT_LEN = 2048

LINES = NEIGH * LPP
COLS = DELAY * SCEN
LANES = 128
PHASOR = 2 * BINS * SCEN
ROWS = 256
VMEM_LIMIT = 24 * 1024 * 1024

F32 = jnp.float32
BF16 = jnp.bfloat16


def fit_tables():
    step = np.arange(SPANS * DELAY)
    harmonic = np.arange(1, BINS + 1)
    angles = (step[:, None] * harmonic[None, :] % DFT_LEN) * (2.0 * math.pi / DFT_LEN)
    twiddle = np.stack([np.cos(angles), -np.sin(angles)], axis=1) / math.sqrt(DFT_LEN)
    table = np.einsum("uch,st->uscht", twiddle, np.eye(SCEN))
    table = table.reshape(SPANS * COLS, PHASOR).astype(np.float32)
    high = table.astype(jnp.bfloat16)
    low = (table - high.astype(np.float32)).astype(jnp.bfloat16)
    return np.concatenate([high, low], axis=1)


def dot(left, right):
    return jnp.dot(left, right, preferred_element_type=F32)


def split(value):
    high = value.astype(BF16)
    return high, (value - high.astype(F32)).astype(BF16)


def fit(values, table):
    high, low = split(values)
    both = dot(high, table)
    return both[:, :PHASOR] + both[:, PHASOR:] + dot(low, table[:, :PHASOR])


def iota(shape, axis):
    return lax.broadcasted_iota(jnp.int32, shape, axis)


def slot_vectors(nodes_ref):
    lane = iota((1, LANES), 1)
    row_id = iota((LINES, 1), 0)
    along = jnp.full((1, LANES), -1, jnp.int32)
    down = jnp.full((LINES, 1), -1, jnp.int32)
    for slot in range(LINES):
        node = nodes_ref[slot // LPP, slot % LPP]
        hit = (lane == slot) | (lane == slot + LINES) | (lane == slot + 2 * LINES)
        along = jnp.where(hit, node, along)
        down = jnp.where(row_id == slot, node, down)
    return along, down


def slot_column(value_ref):
    row_id = iota((LINES, 1), 0)
    down = jnp.zeros((LINES, 1), F32)
    for slot in range(LINES):
        down = jnp.where(row_id == slot, value_ref[slot // LPP, slot % LPP], down)
    return down


def first_slots(along, down):
    lane = iota((LINES, LANES), 1)
    row_id = iota((LINES, LANES), 0)
    same = (down == along) & (down >= 0)
    before = jnp.where(same & (row_id < lane % LINES), 1, 0)
    first_along = (jnp.sum(before, axis=0, keepdims=True) == 0) & (along >= 0)
    after = jnp.where(same & (lane < row_id), 1, 0)
    first_down = (jnp.sum(after, axis=1, keepdims=True) == 0) & (down >= 0)
    return first_along, first_down


def injected(lines, along, down):
    same = ((down == along) & (down >= 0))[:, :LINES]
    pick = jnp.where(same, 1.0, 0.0).astype(BF16)
    high = lines.astype(BF16)
    mid, low = split(lines - high.astype(F32))
    total = dot(pick, high) + (dot(pick, mid) + dot(pick, low))
    return total.astype(BF16)


def one_hot(along, rows, offset=0):
    lane = iota((1, LANES), 1)
    wanted = jnp.where(lane < LINES, along, -1)
    return jnp.where(iota((rows, LANES), 0) + offset == wanted, 1.0, 0.0).astype(BF16)


def three_times(rows):
    width = rows.shape[1]
    return jnp.concatenate([rows, rows, rows, jnp.zeros((LANES - 3 * LINES, width), rows.dtype)], axis=0)


def column_of(row):
    size = row.shape[1]
    eye = iota((size, size), 0) == iota((size, size), 1)
    return jnp.sum(jnp.where(eye, row, 0.0), axis=1, keepdims=True)


def small_left(gathered, self_col, along, first_along, offset):
    rows = gathered.shape[0]
    lane = iota((1, LANES), 1)
    high, low = split(self_col)
    here = (iota((rows, LANES), 0) + offset == along) & first_along & (lane >= LINES)
    weight = jnp.where(lane < 2 * LINES, high.astype(F32), low.astype(F32))
    return (gathered + jnp.where(here, weight, 0.0)).astype(BF16)


def outgoing_of(volts, lines, admit_ref, down):
    value = 2.0 * slot_column(admit_ref) * volts - lines
    return jnp.where(down >= 0, value, 0.0)


def send_out(outgoing, place_ref, sub_ref, near_ref, far_ref):
    odd_region = place_ref[0] == 1
    odd_sub = place_ref[1] == 1
    lower_sub, upper_sub = outgoing[:LPP], outgoing[LPP : 2 * LPP]
    lower, upper = outgoing[2 * LPP : 3 * LPP], outgoing[3 * LPP :]
    sub_ref[...] = jnp.where(odd_sub, lower_sub, upper_sub)
    near_ref[...] = jnp.where(odd_region, lower, upper)
    far_ref[...] = jnp.where(odd_region, upper, lower)


def lines_kernel(
    place_ref, nodes_ref, admit_ref, self_ref, history_ref, coupling_ref, sources_ref,
    sub_ref, near_ref, far_ref, rows_ref, inj_ref,
    src_buf, blocks, src_sem, block_sem,
):
    chunks = 4
    depth = NODES // chunks

    def src_copy(part):
        rows = pl.ds(part * depth, depth)
        return pltpu.make_async_copy(
            sources_ref.at[0, rows, pl.ds(0, COLS)], src_buf.at[rows], src_sem.at[part]
        )

    def block_copy(slot):
        node = jnp.maximum(nodes_ref[slot // LPP, slot % LPP], 0)
        start = pl.multiple_of((node // 16) * 16, 16)
        return pltpu.make_async_copy(
            coupling_ref.at[0, pl.ds(start, 16)], blocks.at[pl.ds(slot * 16, 16)], block_sem.at[slot]
        )

    for slot in range(LINES):
        block_copy(slot).start()
    for part in range(chunks):
        src_copy(part).start()

    along, down = slot_vectors(nodes_ref)
    first_along, first_down = first_slots(along, down)
    lines = history_ref[0].reshape(LINES, COLS)
    total = injected(lines, along, down)
    injection = jnp.where(first_down, total, jnp.zeros_like(total))
    inj_ref[...] = injection
    at_node = jnp.maximum(down, 0)
    choose = jnp.where(
        iota((LINES, LINES * 16), 1) == iota((LINES, LINES * 16), 0) * 16 + at_node % 16, 1.0, 0.0
    ).astype(BF16)
    own_row = iota((LINES, NODES), 1) == at_node
    own = jnp.where(own_row, 1.0, 0.0).astype(BF16)
    self_col = jnp.sum(jnp.where(own_row, self_ref[...], 0.0), axis=1, keepdims=True)
    hot = one_hot(along, NODES)

    for slot in range(LINES):
        block_copy(slot).wait()
    rows = dot(choose, blocks[...]).astype(BF16)
    rows_ref[...] = rows
    gathered = dot(rows, hot)
    volts = dot(gathered.astype(BF16)[:, :LINES], injection)
    left = jnp.concatenate([rows, own], axis=0)
    picked = jnp.zeros((2 * LINES, COLS), F32)
    for part in range(chunks):
        src_copy(part).wait()
        span = slice(part * depth, (part + 1) * depth)
        picked = picked + dot(left[:, span], src_buf[span, :])
    volts = volts + picked[:LINES] + self_col * (picked[LINES:] + total.astype(F32))
    send_out(outgoing_of(volts, lines, admit_ref, down), place_ref, sub_ref, near_ref, far_ref)


def terminals_kernel(
    capacity, slots,
    nodes_ref, self_ref, rows_ref, inj_ref, region_ref, prior_ref, old_ref, table_ref,
    coupling_ref, sources_ref,
    packed_ref, left_ref, gathered_ref, base_ref,
    src_buf, left_buf, src_sem, left_sem,
):
    chunks = 8
    depth = NODES // chunks

    def src_copy(part):
        rows = pl.ds(part * depth, depth)
        return pltpu.make_async_copy(
            sources_ref.at[0, rows], src_buf.at[rows], src_sem.at[part]
        )

    left_copy = pltpu.make_async_copy(
        coupling_ref.at[0, pl.ds(0, TERM_DEV)], left_buf.at[pl.ds(0, TERM_DEV)], left_sem
    )
    left_copy.start()
    for part in range(chunks):
        src_copy(part).start()

    along, down = slot_vectors(nodes_ref)
    first_along, _ = first_slots(along, down)
    at_node = jnp.maximum(down, 0)
    own_row = iota((LINES, NODES), 1) == at_node
    left_buf[TERM_DEV : TERM_DEV + LINES, :] = rows_ref[...]
    left_buf[TERM_DEV + LINES :, :] = jnp.where(own_row, 1.0, 0.0).astype(BF16)
    line_self = jnp.sum(jnp.where(own_row, self_ref[...], 0.0), axis=1, keepdims=True)
    term_self = column_of(self_ref[:, :TERM_DEV])
    hot = one_hot(along, NODES)

    region_row = region_ref[...]
    region_col = column_of(region_row.astype(F32)).astype(jnp.int32)
    earlier = iota((TERM_DEV, TERM_DEV), 0) < iota((TERM_DEV, TERM_DEV), 1)
    rank = jnp.sum(
        jnp.where((region_col == region_row) & earlier, 1, 0), axis=0, keepdims=True
    )
    dest = region_row * capacity + rank
    pack = jnp.where(iota((slots, TERM_DEV), 0) == dest, 1.0, 0.0).astype(BF16)

    left_copy.wait()
    gathered = dot(left_buf[: TERM_DEV + LINES, :], hot)
    gathered_ref[...] = gathered[TERM_DEV:].astype(BF16)
    small = small_left(gathered[:TERM_DEV], term_self, along, first_along, 0)
    left_ref[...] = dot(pack, small).astype(BF16)
    total = jnp.zeros((TERM_DEV + 2 * LINES, SPANS * COLS), F32)
    for part in range(chunks):
        src_copy(part).wait()
        span = slice(part * depth, (part + 1) * depth)
        total = total + dot(left_buf[:, span], src_buf[span, :])
    lines_at = total[TERM_DEV : TERM_DEV + LINES, COLS:]
    base_ref[...] = lines_at + line_self * total[TERM_DEV + LINES :, COLS:]
    volts = total[:TERM_DEV] + term_self * src_buf[:TERM_DEV, :].astype(F32)
    differences = volts - old_ref[...].astype(F32)
    from_lines = dot(small, three_times(inj_ref[...]))
    running = prior_ref[...].reshape(TERM_DEV, 2, LANES)
    running = jnp.concatenate([running[:, 0], running[:, 1]], axis=1)
    for span_index in range(SPANS):
        cols = slice(span_index * COLS, (span_index + 1) * COLS)
        values = differences[:, cols]
        if span_index == 0:
            values = values + from_lines
        running = running + fit(values, table_ref[cols, :])
        high, low = split(running)
        filled = dot(pack, high) + dot(pack, low)
        for part in range(2):
            packed_ref[pl.ds(2 * span_index + part, slots, stride=4), :] = filled[
                :, part * LANES : (part + 1) * LANES
            ]


def second_kernel(
    slots,
    place_ref, nodes_ref, admit_ref, self_ref, from_sub_ref, from_near_ref, from_far_ref,
    base_ref, gathered_ref, left_ref, table_ref, packed_in_ref,
    packed_ref, sub_ref, near_ref, far_ref, inj_ref,
):
    along, down = slot_vectors(nodes_ref)
    _, first_down = first_slots(along, down)
    odd_region = place_ref[0] == 1
    odd_sub = place_ref[1] == 1
    from_sub, near, far = from_sub_ref[...], from_near_ref[...], from_far_ref[...]
    none = jnp.zeros_like(from_sub)
    lines = jnp.concatenate(
        [
            jnp.where(odd_sub, from_sub, none),
            jnp.where(odd_sub, none, from_sub),
            jnp.where(odd_region, near, far),
            jnp.where(odd_region, far, near),
        ],
        axis=0,
    )
    total = injected(lines, along, down)
    injection = jnp.where(first_down, total, jnp.zeros_like(total))
    inj_ref[...] = injection
    both = dot(injection, table_ref[...])
    spectrum = both[:, :PHASOR] + both[:, PHASOR:]
    high, low = split(spectrum)
    left = left_ref[...]
    change = dot(left, three_times(high)) + dot(left, three_times(low))
    for row in range(2):
        rows = pl.ds(row, slots, stride=4)
        packed_ref[rows, :] = packed_in_ref[rows, :]
    for part in range(2):
        rows = pl.ds(2 + part, slots, stride=4)
        packed_ref[rows, :] = packed_in_ref[rows, :] + change[:, part * LANES : (part + 1) * LANES]
    own_row = iota((LINES, NODES), 1) == jnp.maximum(down, 0)
    self_col = jnp.sum(jnp.where(own_row, self_ref[...], 0.0), axis=1, keepdims=True)
    volts = base_ref[...] + dot(gathered_ref[:, :LINES], injection) + self_col * total.astype(F32)
    send_out(outgoing_of(volts, lines, admit_ref, down), place_ref, sub_ref, near_ref, far_ref)


def nodes_kernel(
    nodes_ref, self_ref, inj0_ref, inj1_ref, coupling_ref, sources_ref, volts_ref,
    hot_buf, small_buf,
):
    step = pl.program_id(0)
    along, down = slot_vectors(nodes_ref)
    first_along, _ = first_slots(along, down)

    @pl.when(step == 0)
    def _():
        hot_buf[...] = one_hot(along, NODES)
        rows = jnp.concatenate([inj0_ref[...], inj1_ref[...]], axis=1)
        small_buf[...] = three_times(rows)

    start = pl.multiple_of(step * ROWS, ROWS)
    matrix = coupling_ref[0]
    gathered = dot(matrix, hot_buf[...])
    self_col = column_of(self_ref[:, pl.ds(start, ROWS)])
    small = small_left(gathered, self_col, along, first_along, start)
    total = dot(matrix, sources_ref[0]) + dot(small, small_buf[...])
    total = total + self_col * sources_ref[0, pl.ds(start, ROWS), :].astype(F32)
    volts_ref[0] = total.astype(BF16)


def vmem(*shape_dtype):
    return pl.BlockSpec(memory_space=pltpu.VMEM)


VM = pl.BlockSpec(memory_space=pltpu.VMEM)
SM = pl.BlockSpec(memory_space=pltpu.SMEM)
ANY = pl.BlockSpec(memory_space=pl.ANY)


def struct(shape, dtype):
    return jax.ShapeDtypeStruct(shape, dtype)


def params():
    return pltpu.CompilerParams(vmem_limit_bytes=VMEM_LIMIT)


def exchange(sub, near, far):
    subs = lax.axis_size("sub")
    regions = lax.axis_size("region")

    def swap(block, axis, size, first):
        pairs = []
        for low in range(first, size - 1, 2):
            pairs += [(low, low + 1), (low + 1, low)]
        return lax.ppermute(block, axis, pairs)

    return (
        swap(near, "region", regions, 0),
        swap(sub, "sub", subs, 0),
        swap(far, "region", regions, 1),
    )


def body(
    sources,
    coupling,
    self_term,
    history,
    line_nodes,
    line_admit,
    term_region,
    old_samples,
    prior_phasor,
):
    region_count = lax.axis_size("region")
    capacity = max(2, 2 * TERM_DEV // region_count)
    slots = region_count * capacity
    odd_region = lax.axis_index("region") % 2
    odd_sub = lax.axis_index("sub") % 2
    place = jnp.stack([odd_region, odd_sub]).astype(jnp.int32)
    nodes = line_nodes[0]
    admit = line_admit[0]
    tables = fit_tables()
    block = struct((LPP, COLS), F32)

    sub, near, far, rows, inj0 = pl.pallas_call(
        lines_kernel,
        out_shape=[block, block, block, struct((LINES, NODES), BF16), struct((LINES, COLS), BF16)],
        in_specs=[SM, SM, SM, VM, VM, ANY, ANY],
        out_specs=[VM] * 5,
        scratch_shapes=[
            pltpu.VMEM((NODES, COLS), BF16),
            pltpu.VMEM((LINES * 16, NODES), BF16),
            pltpu.SemaphoreType.DMA((4,)),
            pltpu.SemaphoreType.DMA((LINES,)),
        ],
        compiler_params=params(),
        name="lines",
    )(place, nodes, admit, self_term, history, coupling, sources)

    from_near, from_sub, from_far = exchange(sub, near, far)

    packed, left, gathered, base = pl.pallas_call(
        functools.partial(terminals_kernel, capacity, slots),
        out_shape=[
            struct((slots * 4, LANES), F32),
            struct((slots, LANES), BF16),
            struct((LINES, LANES), BF16),
            struct((LINES, COLS), F32),
        ],
        in_specs=[SM, VM, VM, VM, VM, VM, VM, VM, ANY, ANY],
        out_specs=[VM] * 4,
        scratch_shapes=[
            pltpu.VMEM((NODES, SPANS * COLS), BF16),
            pltpu.VMEM((TERM_DEV + 2 * LINES, NODES), BF16),
            pltpu.SemaphoreType.DMA((8,)),
            pltpu.SemaphoreType.DMA,
        ],
        compiler_params=params(),
        name="terminals",
    )(
        nodes, self_term, rows, inj0, term_region.reshape(1, TERM_DEV),
        prior_phasor.reshape(TERM_DEV * 2, LANES), old_samples, tables, coupling, sources,
    )

    packed, sub, near, far, inj1 = pl.pallas_call(
        functools.partial(second_kernel, slots),
        out_shape=[
            struct((slots * 4, LANES), F32), block, block, block, struct((LINES, COLS), BF16)
        ],
        in_specs=[SM, SM, SM] + [VM] * 9,
        out_specs=[VM] * 5,
        input_output_aliases={11: 0},
        compiler_params=params(),
        name="second",
    )(
        place, nodes, admit, self_term, from_sub, from_near, from_far,
        base, gathered, left, tables[COLS:], packed,
    )

    result = lax.all_to_all(
        packed.reshape(region_count, capacity * 4, LANES),
        "region",
        split_axis=0,
        concat_axis=0,
        tiled=True,
    )
    phasors = result.reshape(slots, SPANS, 2, LANES)

    from_near, from_sub, from_far = exchange(sub, near, far)
    none = jnp.zeros_like(from_sub)
    next_history = jnp.stack(
        [
            jnp.where(odd_sub == 1, from_sub, none),
            jnp.where(odd_sub == 1, none, from_sub),
            jnp.where(odd_region == 1, from_near, from_far),
            jnp.where(odd_region == 1, from_far, from_near),
        ],
        axis=0,
    )[None]

    node_voltages = pl.pallas_call(
        nodes_kernel,
        grid=(NODES // ROWS,),
        out_shape=struct((1, NODES, SPANS * COLS), BF16),
        in_specs=[
            SM, VM, VM, VM,
            pl.BlockSpec((1, ROWS, NODES), lambda i: (0, i, 0)),
            pl.BlockSpec((1, NODES, SPANS * COLS), lambda i: (0, 0, 0), pipeline_mode=pl.Buffered(1)),
        ],
        out_specs=pl.BlockSpec((1, ROWS, SPANS * COLS), lambda i: (0, i, 0)),
        scratch_shapes=[
            pltpu.VMEM((NODES, LANES), BF16),
            pltpu.VMEM((LANES, SPANS * COLS), BF16),
        ],
        compiler_params=params(),
        cost_estimate=pl.CostEstimate(
            flops=2 * NODES * NODES * SPANS * COLS, bytes_accessed=20_000_000, transcendentals=0
        ),
        name="nodes",
    )(nodes, self_term, inj0, inj1, coupling, sources)
    return (next_history, node_voltages, phasors)


def solution(mesh):
    return jax.shard_map(
        body,
        mesh=mesh,
        in_specs=(
            P(("region", "sub"), None, None),
            P(("region", "sub"), None, None),
            P(("region", "sub"), None),
            P(("region", "sub"), None, None, None),
            P(("region", "sub"), None, None),
            P(("region", "sub"), None, None),
            P(("region", "sub"), None),
            P(("region", "sub"), None),
            P(("region", "sub"), None, None),
        ),
        out_specs=(
            P(("region", "sub"), None, None, None),
            P(("region", "sub"), None, None),
            P(("region", "sub"), None, None, None),
        ),
        check_vma=False,
    )
```

time: 186 us -> 79.3 us (0.43)
  the two profiles are of different devices: /device:TPU:10 before, /device:TPU:1 now
where the time goes in v1:
time: 79.3 us; the launch traced here: 78.7 us
  Pallas kernels  42.6 us (54%)
  local copies, waits for them, and re-layouts  19 us (24%)
  starting transfers between devices  15.5 us (20%)
  between operations  0.81 us (1%)
    pallas_call x1, Pallas kernels, body(): pl.pallas_call(nodes_kernel, grid=(NODES // ROWS,), out_shape=struct((1,...  22.5 us
    unnamed x35, local copies, waits for them, and re-layouts  19 us
    pallas_call x1, Pallas kernels, body(): pl.pallas_call(functools.partial(terminals_kernel, capacity, slots), out_...  11 us
    ppermute x6, starting transfers between devices, swap(): return lax.ppermute(block, axis, pairs)  10.2 us
    pallas_call x1, Pallas kernels, body(): pl.pallas_call(lines_kernel, out_shape=[block, block, block, struct((LINE...  6.03 us
    all_to_all x1, starting transfers between devices, body(): lax.all_to_all(packed.reshape(region_count, capacity * 4, LANES), 'region...  5.33 us
    pallas_call x1, Pallas kernels, body(): pl.pallas_call(functools.partial(second_kernel, slots), out_shape=[struct...  3.05 us
  transfers between devices with their start and end apart: 7, of which 0 were waited for; matrix products, arithmetic and copies ran while one was open for 1% of the time, Pallas kernels for 43%

profile of v1, /device:TPU:1, one launch (start us, length us, event | category | flops | bytes accessed | tf_op | source)
XLA Modules:
  0.0 78.7 jit_solution(5919831507010080780)
XLA Ops:
  0.6 0.1 pad_add_fusion.place_ref
  0.7 3.4 %copy-done = bf16[1,2048,2048]{2,1,0:T(8,128)(2,1)S(1)} copy-done((bf16[1,2048,2048]{2,1,0:T(8,128)(2,1)S(1)}, bf16[1,2048,2048]{2,1,0:T(8,128)(2,1)}, u32[]{:S(2)}) %copy-start) | copy-done | bytes 8388632
  4.1 2.5 %copy-done.3 = bf16[1,2048,1280]{2,1,0:T(8,128)(2,1)S(1)} copy-done((bf16[1,2048,1280]{2,1,0:T(8,128)(2,1)S(1)}, bf16[1,2048,1280]{2,1,0:T(8,128)(2,1)}, u32[]{:S(2)}) %copy-start.3) | copy-done | bytes 5242904
  6.6 0.9 %copy-done.10 = f32[1,4,8,640]{3,2,1,0:T(8,128)S(1)} copy-done((f32[1,4,8,640]{3,2,1,0:T(8,128)S(1)}, f32[1,4,8,640]{3,2,1,0:T(8,128)}, u32[]{:S(2)}) %copy-start.10) | copy-done | bytes 81944
  7.5 0.7 copy-done.11
  8.2 0.7 copy-done.13
  8.9 0.7 copy-done.15
  9.5 6.0 %lines.1 = (f32[8,640]{1,0:T(8,128)S(1)}, f32[8,640]{1,0:T(8,128)S(1)}, f32[8,640]{1,0:T(8,128)S(1)}, bf16[32,2048]{1,0:T(8,128)(2,1)S(1)}, bf16[32,640]{1,0:T(8,128)(2,1)S(1)}) custom-call(s32[2]{0:T(128)S(1)} %pad_add_fusion.place_ref, s32[4,8]{1,0:T(4,128)S(1)} %bitcast.19, f32[4,8]{1,0:T(4,128)S(1)} %bitcast.23, f32[1,2048]{1,0:T(1,128)S(1)} %copy-done.11, ...), custom_call_target="tpu_custom_call" | custom-call | tf_op jit(solution)/shard_map/lines/pallas_call | solution.py:397
  15.6 2.1 %collective-permute-start = (f32[8,640]{1,0:T(8,128)S(1)}, f32[8,640]{1,0:T(8,128)S(1)}, u32[]{:S(2)}, u32[]{:S(2)}) collective-permute-start(f32[8,640]{1,0:T(8,128)S(1)} %get-tuple-element.17), channel_id=1, source_target_pairs={{0,1},{1,0},{2,3},{3,2},{4,5},{5,4},{6,7},{7,6},{8,9},{9,8},{10,11... | collective-permute-start | bytes 61448 | tf_op jit(solution)/shard_map/ppermute | solution.py:366
  17.7 1.0 %collective-permute-start.1 = (f32[8,640]{1,0:T(8,128)S(1)}, f32[8,640]{1,0:T(8,128)S(1)}, u32[]{:S(2)}, u32[]{:S(2)}) collective-permute-start(f32[8,640]{1,0:T(8,128)S(1)} %get-tuple-element.18), channel_id=1, source_target_pairs={{0,2},{2,0},{4,6},{6,4},{8,10},{10,8},{12,14},{14,12},{16,18},{18,... | collective-permute-start | bytes 61448 | tf_op jit(solution)/shard_map/ppermute | solution.py:366
  18.7 3.0 %collective-permute-start.2 = (f32[8,640]{1,0:T(8,128)S(1)}, f32[8,640]{1,0:T(8,128)S(1)}, u32[]{:S(2)}, u32[]{:S(2)}) collective-permute-start(f32[8,640]{1,0:T(8,128)S(1)} %get-tuple-element.19), channel_id=1, source_target_pairs={{2,4},{4,2},{6,8},{8,6},{10,12},{12,10},{14,16},{16,14},{18,20},{2... | collective-permute-start | bytes 61448 | tf_op jit(solution)/shard_map/ppermute | solution.py:366
  21.7 0.0 copy-start.6
  21.7 1.3 %copy-done.6 = bf16[1280,512]{1,0:T(8,128)(2,1)S(1)} copy-done((bf16[1280,512]{1,0:T(8,128)(2,1)S(1)}, bf16[1280,512]{1,0:T(8,128)(2,1)}, u32[]{:S(2)}) %copy-start.6) | copy-done | bytes 1310744
  23.0 1.1 %copy-done.7 = bf16[256,1280]{1,0:T(8,128)(2,1)S(1)} copy-done((bf16[256,1280]{1,0:T(8,128)(2,1)S(1)}, bf16[256,1280]{1,0:T(8,128)(2,1)}, u32[]{:S(2)}) %copy-start.7) | copy-done | bytes 655384
  24.1 0.9 %copy-done.9 = f32[256,2,128]{2,1,0:T(2,128)S(1)} copy-done((f32[256,2,128]{2,1,0:T(2,128)S(1)}, f32[256,2,128]{2,1,0:T(2,128)}, u32[]{:S(2)}) %copy-start.9) | copy-done | bytes 262168
  25.1 11.0 %terminals.1 = (f32[2048,128]{1,0:T(8,128)}, bf16[512,128]{1,0:T(8,128)(2,1)S(1)}, bf16[32,128]{1,0:T(8,128)(2,1)S(1)}, f32[32,640]{1,0:T(8,128)S(1)}) custom-call(s32[4,8]{1,0:T(4,128)S(1)} %bitcast.20, f32[1,2048]{1,0:T(1,128)S(1)} %copy-done.11, bf16[32,2048]{1,0:T(8,128)(2,1)S(1)} %get-tuple-element.20.rows_ref, ...), custom_call_target="tpu_custom_call" | custom-call | tf_op jit(solution)/shard_map/terminals/pallas_call | solution.py:414
  36.1 0.0 collective-permute-done.from_sub_ref
  36.1 0.0 collective-permute-done.2.from_far_ref
  36.1 3.0 %second.1 = (f32[2048,128]{1,0:T(8,128)}, f32[8,640]{1,0:T(8,128)S(1)}, f32[8,640]{1,0:T(8,128)S(1)}, f32[8,640]{1,0:T(8,128)S(1)}, bf16[32,640]{1,0:T(8,128)(2,1)S(1)}) custom-call(s32[2]{0:T(128)S(1)} %pad_add_fusion.place_ref, s32[4,8]{1,0:T(4,128)S(1)} %bitcast.21, f32[4,8]{1,0:T(4,128)S(1)} %bitcast.24, ...), custom_call_target="tpu_custom_call", output_to_operand_aliasing={{0}: (11, {})} | custom-call | tf_op jit(solution)/shard_map/second/pallas_call | solution.py:437
  39.2 5.3 %all-to-all-start = ((f32[16,128,128]{2,1,0:T(8,128)}), f32[16,128,128]{2,1,0:T(8,128)S(1)}, u32[]{:S(2)}, u32[]{:S(2)}) async-start(f32[16,128,128]{2,1,0:T(8,128)} %bitcast.11), calls=%async_computation | async-start | bytes 2097152 | tf_op jit(solution)/shard_map/all_to_all | solution.py:452
  44.5 0.3 collective-permute-start.3
  44.8 0.5 collective-permute-start.4
  45.2 3.4 %collective-permute-start.5 = (f32[8,640]{1,0:T(8,128)S(1)}, f32[8,640]{1,0:T(8,128)S(1)}, u32[]{:S(2)}, u32[]{:S(2)}) collective-permute-start(f32[8,640]{1,0:T(8,128)S(1)} %get-tuple-element.28), channel_id=1, source_target_pairs={{2,4},{4,2},{6,8},{8,6},{10,12},{12,10},{14,16},{16,14},{18,20},{2... | collective-permute-start | bytes 61448 | tf_op jit(solution)/shard_map/ppermute | solution.py:366
  48.6 0.0 copy-start.2
  48.6 3.4 %copy-done.2 = bf16[1,2048,2048]{2,1,0:T(8,128)(2,1)S(1)} copy-done((bf16[1,2048,2048]{2,1,0:T(8,128)(2,1)S(1)}, bf16[1,2048,2048]{2,1,0:T(8,128)(2,1)}, u32[]{:S(2)}) %copy-start.2) | copy-done | bytes 8388632
  52.0 2.5 %copy-done.5 = bf16[1,2048,1280]{2,1,0:T(8,128)(2,1)S(1)} copy-done((bf16[1,2048,1280]{2,1,0:T(8,128)(2,1)S(1)}, bf16[1,2048,1280]{2,1,0:T(8,128)(2,1)}, u32[]{:S(2)}) %copy-start.5) | copy-done | bytes 5242904
  54.5 22.5 %nodes.1 = bf16[1,2048,1280]{2,1,0:T(8,128)(2,1)} custom-call(s32[4,8]{1,0:T(4,128)S(1)} %bitcast.22, f32[1,2048]{1,0:T(1,128)S(1)} %copy-done.12, bf16[32,640]{1,0:T(8,128)(2,1)S(1)} %get-tuple-element.21.inj_ref.inj0_ref, bf16[32,640]{1,0:T(8,128)(2,1)S(1)} %get-tuple-element.29.inj1_ref, bf16[1,2048,2048]{2,1,0:T(8,128)(2,1)S(1)} %copy-done.2, ...), custom_call_target="tpu_custom_call" | custom-call | flops 10737418240 | bytes 20000000 | tf_op jit(solution)/shard_map/nodes/pallas_call | solution.py:473
  77.0 0.0 collective-permute-done.3
  77.0 0.0 collective-permute-done.4
  77.0 0.0 collective-permute-done.5
  77.1 0.6 maximum_bitcast_fusion
  77.7 1.0 %copy.17 = f32[512,2,2,128]{3,2,1,0:T(2,128)} copy(f32[512,2,2,128]{3,2,1,0:T(2,128)S(1)} %bitcast.26) | data formatting | bytes 2097152
  (25 shorter events, 0.1 us)
Async XLA Ops:
  0.7 3.4 %copy-start = (bf16[1,2048,2048]{2,1,0:T(8,128)(2,1)S(1)}, bf16[1,2048,2048]{2,1,0:T(8,128)(2,1)}, u32[]{:S(2)}) copy-start(bf16[1,2048,2048]{2,1,0:T(8,128)(2,1)} %coupling_ref.5) | copy-start | bytes 25165828
  4.1 2.5 %copy-start.3 = (bf16[1,2048,1280]{2,1,0:T(8,128)(2,1)S(1)}, bf16[1,2048,1280]{2,1,0:T(8,128)(2,1)}, u32[]{:S(2)}) copy-start(bf16[1,2048,1280]{2,1,0:T(8,128)(2,1)} %sources_ref.5) | copy-start | bytes 15728644
  6.6 0.9 %copy-start.10 = (f32[1,4,8,640]{3,2,1,0:T(8,128)S(1)}, f32[1,4,8,640]{3,2,1,0:T(8,128)}, u32[]{:S(2)}) copy-start(f32[1,4,8,640]{3,2,1,0:T(8,128)} %history_ref.1) | copy-start | bytes 245764
  7.5 0.7 copy-start.11
  8.2 0.7 copy-start.13
  8.9 0.7 copy-start.15
  9.5 12.1 %copy-start.1 = (bf16[1,2048,2048]{2,1,0:T(8,128)(2,1)S(1)}, bf16[1,2048,2048]{2,1,0:T(8,128)(2,1)}, u32[]{:S(2)}) copy-start(bf16[1,2048,2048]{2,1,0:T(8,128)(2,1)} %coupling_ref.5) | copy-start | bytes 25165828
  9.5 12.2 %copy-start.4 = (bf16[1,2048,1280]{2,1,0:T(8,128)(2,1)S(1)}, bf16[1,2048,1280]{2,1,0:T(8,128)(2,1)}, u32[]{:S(2)}) copy-start(bf16[1,2048,1280]{2,1,0:T(8,128)(2,1)} %sources_ref.5) | copy-start | bytes 15728644
  9.5 12.2 %copy-start.16 = (s32[256,1]{0,1:T(1,128)S(1)}, s32[256,1]{0,1:T(1,128)}, u32[]{:S(2)}) copy-start(s32[256,1]{0,1:T(1,128)} %param.17) | copy-start | bytes 3076
  15.6 20.5 %collective-permute-start = (f32[8,640]{1,0:T(8,128)S(1)}, f32[8,640]{1,0:T(8,128)S(1)}, u32[]{:S(2)}, u32[]{:S(2)}) collective-permute-start(f32[8,640]{1,0:T(8,128)S(1)} %get-tuple-element.17), channel_id=1, source_target_pairs={{0,1},{1,0},{2,3},{3,2},{4,5},{5,4},{6,7},{7,6},{8,9},{9,8},{10,11... | collective-permute-start | bytes 61448 | tf_op jit(solution)/shard_map/ppermute | solution.py:366
  17.7 18.4 %collective-permute-start.1 = (f32[8,640]{1,0:T(8,128)S(1)}, f32[8,640]{1,0:T(8,128)S(1)}, u32[]{:S(2)}, u32[]{:S(2)}) collective-permute-start(f32[8,640]{1,0:T(8,128)S(1)} %get-tuple-element.18), channel_id=1, source_target_pairs={{0,2},{2,0},{4,6},{6,4},{8,10},{10,8},{12,14},{14,12},{16,18},{18,... | collective-permute-start | bytes 61448 | tf_op jit(solution)/shard_map/ppermute | solution.py:366
  18.7 17.5 %collective-permute-start.2 = (f32[8,640]{1,0:T(8,128)S(1)}, f32[8,640]{1,0:T(8,128)S(1)}, u32[]{:S(2)}, u32[]{:S(2)}) collective-permute-start(f32[8,640]{1,0:T(8,128)S(1)} %get-tuple-element.19), channel_id=1, source_target_pairs={{2,4},{4,2},{6,8},{8,6},{10,12},{12,10},{14,16},{16,14},{18,20},{2... | collective-permute-start | bytes 61448 | tf_op jit(solution)/shard_map/ppermute | solution.py:366
  21.7 1.3 %copy-start.6 = (bf16[1280,512]{1,0:T(8,128)(2,1)S(1)}, bf16[1280,512]{1,0:T(8,128)(2,1)}, u32[]{:S(2)}) copy-start(bf16[1280,512]{1,0:T(8,128)(2,1)} %constant.32.clone.table_ref) | copy-start | bytes 3932164
  23.0 1.1 %copy-start.7 = (bf16[256,1280]{1,0:T(8,128)(2,1)S(1)}, bf16[256,1280]{1,0:T(8,128)(2,1)}, u32[]{:S(2)}) copy-start(bf16[256,1280]{1,0:T(8,128)(2,1)} %old_ref.1) | copy-start | bytes 1966084
  24.1 0.9 %copy-start.9 = (f32[256,2,128]{2,1,0:T(2,128)S(1)}, f32[256,2,128]{2,1,0:T(2,128)}, u32[]{:S(2)}) copy-start(f32[256,2,128]{2,1,0:T(2,128)} %param.19) | copy-start | bytes 786436
  25.1 11.1 %copy-start.8 = (bf16[640,512]{1,0:T(8,128)(2,1)S(1)}, bf16[640,512]{1,0:T(8,128)(2,1)}, u32[]{:S(2)}) copy-start(bf16[640,512]{1,0:T(8,128)(2,1)} %constant.33.clone.table_ref) | copy-start | bytes 1966084
  25.1 23.5 %copy-start.12 = (f32[1,2048]{1,0:T(1,128)S(1)}, f32[1,2048]{1,0:T(1,128)}, u32[]{:S(2)}) copy-start(f32[1,2048]{1,0:T(1,128)} %self_ref.7) | copy-start | bytes 24580
  25.1 23.5 %copy-start.14 = (s32[1,4,8]{2,1,0:T(4,128)S(1)}, s32[1,4,8]{2,1,0:T(4,128)}, u32[]{:S(2)}) copy-start(s32[1,4,8]{2,1,0:T(4,128)} %param.15) | copy-start | bytes 388
  39.2 38.5 %all-to-all-start = ((f32[16,128,128]{2,1,0:T(8,128)}), f32[16,128,128]{2,1,0:T(8,128)S(1)}, u32[]{:S(2)}, u32[]{:S(2)}) async-start(f32[16,128,128]{2,1,0:T(8,128)} %bitcast.11), calls=%async_computation | async-start | bytes 2097152 | tf_op jit(solution)/shard_map/all_to_all | solution.py:452
  44.5 32.5 %collective-permute-start.3 = (f32[8,640]{1,0:T(8,128)S(1)}, f32[8,640]{1,0:T(8,128)S(1)}, u32[]{:S(2)}, u32[]{:S(2)}) collective-permute-start(f32[8,640]{1,0:T(8,128)S(1)} %get-tuple-element.26), channel_id=1, source_target_pairs={{0,1},{1,0},{2,3},{3,2},{4,5},{5,4},{6,7},{7,6},{8,9},{9,8},{10,11... | collective-permute-start | bytes 61448 | tf_op jit(solution)/shard_map/ppermute | solution.py:366
  44.8 32.3 %collective-permute-start.4 = (f32[8,640]{1,0:T(8,128)S(1)}, f32[8,640]{1,0:T(8,128)S(1)}, u32[]{:S(2)}, u32[]{:S(2)}) collective-permute-start(f32[8,640]{1,0:T(8,128)S(1)} %get-tuple-element.27), channel_id=1, source_target_pairs={{0,2},{2,0},{4,6},{6,4},{8,10},{10,8},{12,14},{14,12},{16,18},{18,... | collective-permute-start | bytes 61448 | tf_op jit(solution)/shard_map/ppermute | solution.py:366
  45.2 31.8 %collective-permute-start.5 = (f32[8,640]{1,0:T(8,128)S(1)}, f32[8,640]{1,0:T(8,128)S(1)}, u32[]{:S(2)}, u32[]{:S(2)}) collective-permute-start(f32[8,640]{1,0:T(8,128)S(1)} %get-tuple-element.28), channel_id=1, source_target_pairs={{2,4},{4,2},{6,8},{8,6},{10,12},{12,10},{14,16},{16,14},{18,20},{2... | collective-permute-start | bytes 61448 | tf_op jit(solution)/shard_map/ppermute | solution.py:366
  48.6 3.4 %copy-start.2 = (bf16[1,2048,2048]{2,1,0:T(8,128)(2,1)S(1)}, bf16[1,2048,2048]{2,1,0:T(8,128)(2,1)}, u32[]{:S(2)}) copy-start(bf16[1,2048,2048]{2,1,0:T(8,128)(2,1)} %coupling_ref.5) | copy-start | bytes 25165828
  52.0 2.5 %copy-start.5 = (bf16[1,2048,1280]{2,1,0:T(8,128)(2,1)S(1)}, bf16[1,2048,1280]{2,1,0:T(8,128)(2,1)}, u32[]{:S(2)}) copy-start(bf16[1,2048,1280]{2,1,0:T(8,128)(2,1)} %sources_ref.5) | copy-start | bytes 15728644

commit v2 on v1

v2 whole, which is shorter than its diff:
```python
import functools
import math

import jax
import jax.numpy as jnp
import numpy as np
from jax import lax
from jax.experimental import pallas as pl
from jax.experimental.pallas import tpu as pltpu
from jax.sharding import PartitionSpec as P

NODES = 2048
NEIGH = 4
LPP = 8
DELAY = 40
SPANS = 2
SCEN = 16
TERM_DEV = 256
BINS = 8
DFT_LEN = 2048

LINES = NEIGH * LPP
COLS = DELAY * SCEN
LANES = 128
PHASOR = 2 * BINS * SCEN
ROWS = 512
VMEM_LIMIT = 32 * 1024 * 1024

F32 = jnp.float32
BF16 = jnp.bfloat16


def fit_tables():
    step = np.arange(SPANS * DELAY)
    harmonic = np.arange(1, BINS + 1)
    angles = (step[:, None] * harmonic[None, :] % DFT_LEN) * (2.0 * math.pi / DFT_LEN)
    twiddle = np.stack([np.cos(angles), -np.sin(angles)], axis=1) / math.sqrt(DFT_LEN)
    table = np.einsum("uch,st->uscht", twiddle, np.eye(SCEN))
    table = table.reshape(SPANS, COLS, PHASOR).astype(np.float32)
    high = table.astype(jnp.bfloat16)
    low = (table - high.astype(np.float32)).astype(jnp.bfloat16)
    return np.concatenate([high, low, high], axis=1)


def dot(left, right):
    return jnp.dot(left, right, preferred_element_type=F32)


def split(value):
    high = value.astype(BF16)
    return high, (value - high.astype(F32)).astype(BF16)


def iota(shape, axis):
    return lax.broadcasted_iota(jnp.int32, shape, axis)


def slot_vectors(nodes_ref, admit_ref):
    lane = iota((1, LANES), 1)
    row_id = iota((LINES, 1), 0)
    along = jnp.full((1, LANES), -1, jnp.int32)
    down = jnp.full((LINES, 1), -1, jnp.int32)
    admit = jnp.zeros((LINES, 1), F32)
    for slot in range(LINES):
        node = nodes_ref[0, slot // LPP, slot % LPP]
        along = jnp.where((lane % LINES == slot) & (lane < 3 * LINES), node, along)
        down = jnp.where(row_id == slot, node, down)
        admit = jnp.where(row_id == slot, admit_ref[0, slot // LPP, slot % LPP], admit)
    return along, down, admit


def same_node(along, down):
    return (down == along) & (down >= 0)


def first_along(along, down):
    shape = (LINES, LANES)
    before = same_node(along, down) & (iota(shape, 0) < iota(shape, 1) % LINES)
    return (jnp.sum(jnp.where(before, 1, 0), axis=0, keepdims=True) == 0) & (along >= 0)


def first_down(along, down):
    shape = (LINES, LANES)
    before = same_node(along, down) & (iota(shape, 1) < iota(shape, 0))
    return (jnp.sum(jnp.where(before, 1, 0), axis=1, keepdims=True) == 0) & (down >= 0)


def injected(lines, along, down):
    pick = jnp.where(same_node(along, down), 1.0, 0.0).astype(BF16)[:, : 3 * LINES]
    high = lines.astype(BF16)
    mid, low = split(lines - high.astype(F32))
    total = dot(pick, jnp.concatenate([high, mid, low], axis=0)).astype(BF16)
    return total, jnp.where(first_down(along, down), total, jnp.zeros_like(total))


def three_times(rows):
    width = rows.shape[1]
    return jnp.concatenate([rows, rows, rows, jnp.zeros((LANES - 3 * LINES, width), rows.dtype)], axis=0)


def column_of(row):
    size = row.shape[1]
    eye = iota((size, size), 0) == iota((size, size), 1)
    return jnp.sum(jnp.where(eye, row, 0.0), axis=1, keepdims=True)


def small_left(gathered, self_col, along, first, offset):
    rows = gathered.shape[0]
    lane = iota((1, LANES), 1)
    high, low = split(self_col)
    here = (iota((rows, LANES), 0) + offset == along) & first & (lane >= LINES)
    weight = jnp.where(lane < 2 * LINES, high.astype(F32), low.astype(F32))
    return (gathered + jnp.where(here, weight, 0.0)).astype(BF16)


def send_out(volts, lines, admit, down, place_ref, sub_ref, near_ref, far_ref):
    outgoing = jnp.where(down >= 0, 2.0 * admit * volts - lines, 0.0)
    odd_region = place_ref[0] == 1
    odd_sub = place_ref[1] == 1
    lower_sub, upper_sub = outgoing[:LPP], outgoing[LPP : 2 * LPP]
    lower, upper = outgoing[2 * LPP : 3 * LPP], outgoing[3 * LPP :]
    sub_ref[...] = jnp.where(odd_sub, lower_sub, upper_sub)
    near_ref[...] = jnp.where(odd_region, lower, upper)
    far_ref[...] = jnp.where(odd_region, upper, lower)


def arrived(place_ref, from_sub_ref, from_near_ref, from_far_ref):
    odd_region = place_ref[0] == 1
    odd_sub = place_ref[1] == 1
    from_sub, near, far = from_sub_ref[...], from_near_ref[...], from_far_ref[...]
    none = jnp.zeros_like(from_sub)
    return jnp.concatenate(
        [
            jnp.where(odd_sub, from_sub, none),
            jnp.where(odd_sub, none, from_sub),
            jnp.where(odd_region, near, far),
            jnp.where(odd_region, far, near),
        ],
        axis=0,
    )


def lines_kernel(
    place_ref, nodes_hbm, admit_hbm, self_hbm, history_hbm, coupling_hbm, sources_hbm,
    sub_ref, near_ref, far_ref, src_ref, term_ref, rows_ref, gathered_ref, inj_ref,
    slot_ref, value_ref, self_ref,
    nodes_ref, admit_ref, history_ref, blocks, early_sem, src_sem, late_sem, block_sem,
):
    chunks = 2
    depth = NODES // chunks
    first_cols, later_cols = pl.ds(0, COLS), pl.ds(COLS, COLS)

    def early(index, source, target):
        return pltpu.make_async_copy(source, target, early_sem.at[index])

    def src_copy(part):
        rows = pl.ds(part * depth, depth)
        return pltpu.make_async_copy(
            sources_hbm.at[0, rows, first_cols], src_ref.at[rows, first_cols], src_sem.at[part]
        )

    def block_copy(slot):
        node = jnp.maximum(nodes_ref[0, slot // LPP, slot % LPP], 0)
        start = pl.multiple_of((node // 16) * 16, 16)
        return pltpu.make_async_copy(
            coupling_hbm.at[0, pl.ds(start, 16)], blocks.at[pl.ds(slot * 16, 16)], block_sem.at[slot]
        )

    nodes_copy = early(0, nodes_hbm, nodes_ref)
    admit_copy = early(1, admit_hbm, admit_ref)
    self_copy = early(2, self_hbm, self_ref)
    history_copy = early(3, history_hbm, history_ref)
    src_later = pltpu.make_async_copy(
        sources_hbm.at[0, :, later_cols], src_ref.at[:, later_cols], late_sem.at[0]
    )
    term_copy = pltpu.make_async_copy(
        coupling_hbm.at[0, pl.ds(0, TERM_DEV)], term_ref, late_sem.at[1]
    )
    nodes_copy.start()
    admit_copy.start()
    self_copy.start()
    history_copy.start()
    src_copy(0).start()
    nodes_copy.wait()
    for slot in range(LINES):
        block_copy(slot).start()
    for part in range(1, chunks):
        src_copy(part).start()
    admit_copy.wait()
    self_copy.wait()
    history_copy.wait()

    along, down, admit = slot_vectors(nodes_ref, admit_ref)
    lines = history_ref[0].reshape(LINES, COLS)
    total, injection = injected(lines, along, down)
    inj_ref[...] = injection
    at_node = jnp.maximum(down, 0)
    choose = jnp.where(
        iota((LINES, LINES * 16), 1) == iota((LINES, LINES * 16), 0) * 16 + at_node % 16, 1.0, 0.0
    ).astype(BF16)
    own_row = iota((LINES, NODES), 1) == at_node
    own = jnp.where(own_row, 1.0, 0.0).astype(BF16)
    self_col = jnp.sum(jnp.where(own_row, self_ref[...], 0.0), axis=1, keepdims=True)
    wanted = jnp.where(iota((1, LANES), 1) < LINES, along, -1)
    hot = jnp.where(iota((NODES, LANES), 0) == wanted, 1.0, 0.0).astype(BF16)
    src_ref[:, SPANS * COLS :] = hot
    slot_ref[:LINES, :] = jnp.broadcast_to(down, (LINES, LANES))
    slot_ref[LINES:, :] = jnp.broadcast_to(along, (8, LANES))
    value_ref[:LINES, :] = jnp.broadcast_to(admit, (LINES, LANES))
    value_ref[LINES:, :] = jnp.broadcast_to(self_col, (LINES, LANES))

    for slot in range(LINES):
        block_copy(slot).wait()
    term_copy.start()
    src_later.start()
    rows = dot(choose, blocks[...]).astype(BF16)
    rows_ref[...] = rows
    gathered = dot(rows, hot).astype(BF16)
    gathered_ref[...] = gathered
    volts = dot(gathered[:, :LINES], injection)
    left = jnp.concatenate([rows, own], axis=0)
    for part in range(chunks):
        src_copy(part).wait()
    picked = jnp.zeros((2 * LINES, COLS), F32)
    for part in range(chunks):
        span = slice(part * depth, (part + 1) * depth)
        picked = picked + dot(left[:, span], src_ref[span, :COLS])
    volts = volts + picked[:LINES] + self_col * (picked[LINES:] + total.astype(F32))
    send_out(volts, lines, admit, down, place_ref, sub_ref, near_ref, far_ref)
    src_later.wait()
    term_copy.wait()


def terminals_kernel(
    capacity, slots,
    slot_ref, inj_ref, src_ref, term_ref, self_ref, region_hbm, prior_hbm, old_hbm, table_hbm,
    packed_ref, left_ref, second_table,
    region_ref, prior_ref, old_ref, first_table, sems,
):
    copies = [
        pltpu.make_async_copy(source, target, sems.at[index])
        for index, (source, target) in enumerate(
            [
                (region_hbm, region_ref),
                (old_hbm, old_ref),
                (prior_hbm, prior_ref),
                (table_hbm.at[0], first_table),
                (table_hbm.at[1], second_table),
            ]
        )
    ]
    for copy in copies:
        copy.start()
    down = slot_ref[:LINES, :1]
    along = slot_ref[LINES : LINES + 1, :]
    first = first_along(along, down)
    term_self = column_of(self_ref[:, :TERM_DEV])

    sources = slice(0, SPANS * COLS)
    small = small_left(dot(term_ref[...], src_ref[:, SPANS * COLS :]), term_self, along, first, 0)
    volts = dot(term_ref[...], src_ref[:, sources])
    volts = volts + term_self * src_ref[:TERM_DEV, sources].astype(F32)
    from_lines = dot(small, three_times(inj_ref[...]))

    copies[0].wait()
    region_row = region_ref[...]
    region_col = column_of(region_row.astype(F32)).astype(jnp.int32)
    earlier = iota((TERM_DEV, TERM_DEV), 0) < iota((TERM_DEV, TERM_DEV), 1)
    rank = jnp.sum(
        jnp.where((region_col == region_row) & earlier, 1, 0), axis=0, keepdims=True
    )
    dest = region_row * capacity + rank
    pack = jnp.where(iota((slots, TERM_DEV), 0) == dest, 1.0, 0.0).astype(BF16)
    left_ref[...] = dot(pack, small).astype(BF16)

    for copy in copies[1:]:
        copy.wait()
    differences = volts - old_ref[...].astype(F32)
    running = jnp.concatenate(
        [prior_ref[pl.ds(part, TERM_DEV, stride=2), :] for part in range(2)], axis=1
    )
    highs, lows = [], []
    for span_index, table_ref in enumerate([first_table, second_table]):
        values = differences[:, span_index * COLS : (span_index + 1) * COLS]
        if span_index == 0:
            values = values + from_lines
        high, low = split(values)
        running = running + dot(jnp.concatenate([high, high, low], axis=1), table_ref[...])
        high, low = split(running)
        highs.append(high)
        lows.append(low)
    fitted = jnp.concatenate(
        [jnp.concatenate(highs, axis=1), jnp.concatenate(lows, axis=1)], axis=0
    )
    filled = dot(jnp.concatenate([pack, pack], axis=1), fitted)
    for part in range(4):
        packed_ref[pl.ds(part, slots, stride=4), :] = filled[:, part * LANES : (part + 1) * LANES]


def second_kernel(
    slots,
    place_ref, slot_ref, from_sub_ref, from_near_ref, from_far_ref, left_ref, table_ref, packed_in_ref,
    packed_ref,
):
    down = slot_ref[:LINES, :1]
    along = slot_ref[LINES : LINES + 1, :]
    lines = arrived(place_ref, from_sub_ref, from_near_ref, from_far_ref)
    _, injection = injected(lines, along, down)
    spectrum = dot(jnp.concatenate([injection, injection], axis=1), table_ref[: 2 * COLS, :])
    high, low = split(spectrum)
    left = left_ref[...]
    change = dot(
        jnp.concatenate([left, left], axis=1),
        jnp.concatenate([three_times(high), three_times(low)], axis=0),
    )
    for row in range(2):
        rows = pl.ds(row, slots, stride=4)
        packed_ref[rows, :] = packed_in_ref[rows, :]
    for part in range(2):
        rows = pl.ds(2 + part, slots, stride=4)
        packed_ref[rows, :] = packed_in_ref[rows, :] + change[:, part * LANES : (part + 1) * LANES]


def last_lines_kernel(
    place_ref, slot_ref, value_ref, from_sub_ref, from_near_ref, from_far_ref,
    rows_ref, gathered_ref, src_ref, started_ref,
    sub_ref, near_ref, far_ref, inj_ref,
):
    del started_ref
    down = slot_ref[:LINES, :1]
    along = slot_ref[LINES : LINES + 1, :]
    admit, self_col = value_ref[:LINES, :1], value_ref[LINES:, :1]
    lines = arrived(place_ref, from_sub_ref, from_near_ref, from_far_ref)
    total, injection = injected(lines, along, down)
    inj_ref[...] = injection
    own = jnp.where(iota((LINES, NODES), 1) == jnp.maximum(down, 0), 1.0, 0.0).astype(BF16)
    left = jnp.concatenate([rows_ref[...], own], axis=0)
    picked = dot(left, src_ref[:, COLS : SPANS * COLS])
    volts = picked[:LINES] + dot(gathered_ref[:, :LINES], injection)
    volts = volts + self_col * (picked[LINES:] + total.astype(F32))
    send_out(volts, lines, admit, down, place_ref, sub_ref, near_ref, far_ref)


def nodes_kernel(
    slot_ref, inj0_ref, inj1_ref, src_ref, self_ref, coupling_hbm,
    volts_hbm,
    matrix_buf, volts_buf, small_buf, in_sem, out_sem,
):
    down = slot_ref[:LINES, :1]
    along = slot_ref[LINES : LINES + 1, :]
    first = first_along(along, down)
    blocks = NODES // ROWS

    def load(block, place):
        rows = pl.ds(pl.multiple_of(block * ROWS, ROWS), ROWS)
        return pltpu.make_async_copy(coupling_hbm.at[0, rows], matrix_buf.at[place], in_sem.at[place])

    def store(block, place):
        rows = pl.ds(pl.multiple_of(block * ROWS, ROWS), ROWS)
        return pltpu.make_async_copy(volts_buf.at[place], volts_hbm.at[0, rows], out_sem.at[place])

    load(0, 0).start()
    small_buf[...] = three_times(jnp.concatenate([inj0_ref[...], inj1_ref[...]], axis=1))

    @pl.loop(0, blocks)
    def _(block):
        place = lax.rem(block, 2)

        @pl.when(block + 1 < blocks)
        def _():
            load(block + 1, 1 - place).start()

        load(block, place).wait()

        @pl.when(block >= 2)
        def _():
            store(block - 2, place).wait()

        start = pl.multiple_of(block * ROWS, ROWS)
        matrix = matrix_buf[place]
        self_col = jnp.concatenate(
            [
                column_of(self_ref[:, pl.ds(pl.multiple_of(start + part, 256), 256)])
                for part in range(0, ROWS, 256)
            ],
            axis=0,
        )
        products = dot(matrix, src_ref[...])
        small = small_left(products[:, SPANS * COLS :], self_col, along, first, start)
        total = products[:, : SPANS * COLS] + dot(small, small_buf[...])
        total = total + self_col * src_ref[pl.ds(start, ROWS), : SPANS * COLS].astype(F32)
        volts_buf[place] = total.astype(BF16)
        store(block, place).start()

    for block in range(blocks - 2, blocks):
        store(block, block % 2).wait()


VM = pl.BlockSpec(memory_space=pltpu.VMEM)
SM = pl.BlockSpec(memory_space=pltpu.SMEM)
HB = pl.BlockSpec(memory_space=pltpu.HBM)


def struct(shape, dtype):
    return jax.ShapeDtypeStruct(shape, dtype)


def in_hbm(*arrays):
    return [pltpu.with_memory_space_constraint(array, pltpu.HBM) for array in arrays]


def in_vmem(*arrays):
    return [pltpu.with_memory_space_constraint(array, pltpu.VMEM) for array in arrays]


def params():
    return pltpu.CompilerParams(vmem_limit_bytes=VMEM_LIMIT)


def exchange(sub, near, far):
    subs = lax.axis_size("sub")
    regions = lax.axis_size("region")

    def swap(block, axis, size, first):
        pairs = []
        for low in range(first, size - 1, 2):
            pairs += [(low, low + 1), (low + 1, low)]
        return lax.ppermute(block, axis, pairs)

    return (
        swap(near, "region", regions, 0),
        swap(sub, "sub", subs, 0),
        swap(far, "region", regions, 1),
    )


def body(
    sources,
    coupling,
    self_term,
    history,
    line_nodes,
    line_admit,
    term_region,
    old_samples,
    prior_phasor,
):
    region_count = lax.axis_size("region")
    capacity = max(2, 2 * TERM_DEV // region_count)
    slots = region_count * capacity
    odd_region = lax.axis_index("region") % 2
    odd_sub = lax.axis_index("sub") % 2
    place = jnp.stack([odd_region, odd_sub]).astype(jnp.int32)
    block = struct((LPP, COLS), F32)
    injection = struct((LINES, COLS), BF16)
    tables = fit_tables()
    DMA = pltpu.SemaphoreType.DMA

    (sub, near, far, src, term, rows, gathered, inj0, slot, value, self_row) = pl.pallas_call(
        lines_kernel,
        out_shape=[
            block, block, block,
            struct((NODES, SPANS * COLS + LANES), BF16),
            struct((TERM_DEV, NODES), BF16),
            struct((LINES, NODES), BF16),
            struct((LINES, LANES), BF16),
            injection,
            struct((LINES + 8, LANES), jnp.int32),
            struct((2 * LINES, LANES), F32),
            struct((1, NODES), F32),
        ],
        in_specs=[SM] + [HB] * 6,
        out_specs=[VM] * 11,
        scratch_shapes=[
            pltpu.SMEM((1, NEIGH, LPP), jnp.int32),
            pltpu.SMEM((1, NEIGH, LPP), F32),
            pltpu.VMEM((1, NEIGH, LPP, COLS), F32),
            pltpu.VMEM((LINES * 16, NODES), BF16),
            DMA((4,)), DMA((2,)), DMA((2,)), DMA((LINES,)),
        ],
        compiler_params=params(),
        name="lines",
    )(place, *in_hbm(line_nodes, line_admit, self_term, history, coupling, sources))

    from_near, from_sub, from_far = exchange(sub, near, far)

    packed, left, table = pl.pallas_call(
        functools.partial(terminals_kernel, capacity, slots),
        out_shape=[
            struct((slots * 4, LANES), F32),
            struct((slots, LANES), BF16),
            struct((3 * COLS, PHASOR), BF16),
        ],
        in_specs=[VM] * 5 + [HB] * 4,
        out_specs=[VM] * 3,
        scratch_shapes=[
            pltpu.VMEM((1, TERM_DEV), jnp.int32),
            pltpu.VMEM((TERM_DEV * 2, LANES), F32),
            pltpu.VMEM((TERM_DEV, SPANS * COLS), BF16),
            pltpu.VMEM((3 * COLS, PHASOR), BF16),
            DMA((5,)),
        ],
        compiler_params=params(),
        name="terminals",
    )(
        slot, inj0, src, term, self_row,
        *in_hbm(
            term_region.reshape(1, TERM_DEV),
            prior_phasor.reshape(TERM_DEV * 2, LANES),
            old_samples,
            jnp.asarray(tables),
        ),
    )

    packed = pl.pallas_call(
        functools.partial(second_kernel, slots),
        out_shape=struct((slots * 4, LANES), F32),
        in_specs=[SM] + [VM] * 7,
        out_specs=VM,
        compiler_params=params(),
        name="second",
    )(place, slot, from_sub, from_near, from_far, left, table, packed)

    result = lax.all_to_all(
        packed.reshape(region_count, capacity * 4, LANES),
        "region",
        split_axis=0,
        concat_axis=0,
        tiled=True,
    )
    phasors = result.reshape(slots, SPANS, 2, LANES)

    sub, near, far, inj1 = pl.pallas_call(
        last_lines_kernel,
        out_shape=[block, block, block, injection],
        in_specs=[SM] + [VM] * 8 + [pl.BlockSpec(memory_space=pl.ANY)],
        out_specs=[VM] * 4,
        compiler_params=params(),
        name="last_lines",
    )(place, slot, value, from_sub, from_near, from_far, rows, gathered, src, packed)

    from_near, from_sub, from_far = exchange(sub, near, far)
    none = jnp.zeros_like(from_sub)
    next_history = jnp.stack(
        [
            jnp.where(odd_sub == 1, from_sub, none),
            jnp.where(odd_sub == 1, none, from_sub),
            jnp.where(odd_region == 1, from_near, from_far),
            jnp.where(odd_region == 1, from_far, from_near),
        ],
        axis=0,
    )[None]

    node_voltages = pl.pallas_call(
        nodes_kernel,
        out_shape=struct((1, NODES, SPANS * COLS), BF16),
        in_specs=[VM] * 5 + [HB],
        out_specs=HB,
        scratch_shapes=[
            pltpu.VMEM((2, ROWS, NODES), BF16),
            pltpu.VMEM((2, ROWS, SPANS * COLS), BF16),
            pltpu.VMEM((LANES, SPANS * COLS), BF16),
            DMA((2,)), DMA((2,)),
        ],
        compiler_params=params(),
        cost_estimate=pl.CostEstimate(
            flops=2 * NODES * NODES * SPANS * COLS, bytes_accessed=20_000_000, transcendentals=0
        ),
        name="nodes",
    )(slot, inj0, inj1, src, self_row, *in_hbm(coupling))
    return (next_history, node_voltages, phasors)


def solution(mesh):
    return jax.shard_map(
        body,
        mesh=mesh,
        in_specs=(
            P(("region", "sub"), None, None),
            P(("region", "sub"), None, None),
            P(("region", "sub"), None),
            P(("region", "sub"), None, None, None),
            P(("region", "sub"), None, None),
            P(("region", "sub"), None, None),
            P(("region", "sub"), None),
            P(("region", "sub"), None),
            P(("region", "sub"), None, None),
        ),
        out_specs=(
            P(("region", "sub"), None, None, None),
            P(("region", "sub"), None, None),
            P(("region", "sub"), None, None, None),
        ),
        check_vma=False,
    )
```

time: 79.3 us -> 56.7 us (0.72)
  the two profiles are of different devices: /device:TPU:1 before, /device:TPU:13 now
where the time goes in v2:
time: 56.7 us; the launch traced here: 56.2 us
  Pallas kernels  32.4 us (57%)
  starting transfers between devices  14.6 us (26%)
  local copies, waits for them, and re-layouts  4.84 us (9%)
  waiting for transfers between devices  2.84 us (5%)
  between operations  0.76 us (1%)
  other arithmetic  0.73 us (1%)
    pallas_call x1, Pallas kernels, body(): pl.pallas_call(nodes_kernel, out_shape=struct((1, NODES, SPANS * COLS), B...  18.2 us
    ppermute x6, starting transfers between devices, swap(): return lax.ppermute(block, axis, pairs)  8.83 us
    pallas_call x1, Pallas kernels, body(): pl.pallas_call(lines_kernel, out_shape=[block, block, block, struct((NODE...  6.32 us
    all_to_all x1, starting transfers between devices, body(): lax.all_to_all(packed.reshape(region_count, capacity * 4, LANES), 'region...  5.79 us
    unnamed x7, local copies, waits for them, and re-layouts  4.84 us
    pallas_call x1, Pallas kernels, body(): pl.pallas_call(functools.partial(terminals_kernel, capacity, slots), out_...  4.45 us
    ppermute x6, waiting for transfers between devices, swap(): return lax.ppermute(block, axis, pairs)  2.84 us
    pallas_call x1, Pallas kernels, body(): pl.pallas_call(functools.partial(second_kernel, slots), out_shape=struct(...  2.27 us
  transfers between devices with their start and end apart: 7, of which 1 were waited for; matrix products, arithmetic and copies ran while one was open for 1% of the time, Pallas kernels for 42%

profile of v2, /device:TPU:13, one launch (start us, length us, event | category | flops | bytes accessed | tf_op | source)
XLA Modules:
  0.0 56.2 jit_solution(3612768918575956551)
XLA Ops:
  0.6 0.1 pad_add_fusion.place_ref
  0.7 6.3 %lines.1 = (f32[8,640]{1,0:T(8,128)S(1)}, f32[8,640]{1,0:T(8,128)S(1)}, f32[8,640]{1,0:T(8,128)S(1)}, bf16[2048,1408]{1,0:T(8,128)(2,1)S(1)}, bf16[256,2048]{1,0...) custom-call(s32[2]{0:T(128)S(1)} %pad_add_fusion.place_ref, ...), custom_call_target="tpu_custom_call" | custom-call | tf_op jit(solution)/shard_map/lines/pallas_call | solution.py:459
  7.1 0.0 copy-start
  7.1 1.0 %collective-permute-start = (f32[8,640]{1,0:T(8,128)S(1)}, f32[8,640]{1,0:T(8,128)S(1)}, u32[]{:S(2)}, u32[]{:S(2)}) collective-permute-start(f32[8,640]{1,0:T(8,128)S(1)} %get-tuple-element.23), channel_id=1, source_target_pairs={{0,1},{1,0},{2,3},{3,2},{4,5},{5,4},{6,7},{7,6},{8,9},{9,8},{10,11... | collective-permute-start | bytes 61448 | tf_op jit(solution)/shard_map/ppermute | solution.py:428
  8.1 1.4 %collective-permute-start.1 = (f32[8,640]{1,0:T(8,128)S(1)}, f32[8,640]{1,0:T(8,128)S(1)}, u32[]{:S(2)}, u32[]{:S(2)}) collective-permute-start(f32[8,640]{1,0:T(8,128)S(1)} %get-tuple-element.24), channel_id=1, source_target_pairs={{0,2},{2,0},{4,6},{6,4},{8,10},{10,8},{12,14},{14,12},{16,18},{18,... | collective-permute-start | bytes 61448 | tf_op jit(solution)/shard_map/ppermute | solution.py:428
  9.5 2.6 %collective-permute-start.2 = (f32[8,640]{1,0:T(8,128)S(1)}, f32[8,640]{1,0:T(8,128)S(1)}, u32[]{:S(2)}, u32[]{:S(2)}) collective-permute-start(f32[8,640]{1,0:T(8,128)S(1)} %get-tuple-element.25), channel_id=1, source_target_pairs={{2,4},{4,2},{6,8},{8,6},{10,12},{12,10},{14,16},{16,14},{18,20},{2... | collective-permute-start | bytes 61448 | tf_op jit(solution)/shard_map/ppermute | solution.py:428
  12.1 4.5 %terminals.1 = (f32[2048,128]{1,0:T(8,128)S(1)}, bf16[512,128]{1,0:T(8,128)(2,1)S(1)}, bf16[1920,256]{1,0:T(8,128)(2,1)S(1)}) custom-call(s32[40,128]{1,0:T(8,128)S(1)} %get-tuple-element.21.slot_ref, bf16[32,640]{1,0:T(8,128)(2,1)S(1)} %get-tuple-element.29.inj_ref.inj0_ref, bf16[2048,1408]{1,0:T(8,128)(2,1)S(1)} %get-tuple-element.28.src_ref, ...), custom_call_target="tpu_custom_call" | custom-call | tf_op jit(solution)/shard_map/terminals/pallas_call | solution.py:487
  16.6 0.0 collective-permute-done.from_sub_ref
  16.6 0.0 collective-permute-done.1.from_near_ref
  16.6 0.0 collective-permute-done.2.from_far_ref
  16.6 2.3 %second.1.started_ref = f32[2048,128]{1,0:T(8,128)} custom-call(s32[2]{0:T(128)S(1)} %pad_add_fusion.place_ref, s32[40,128]{1,0:T(8,128)S(1)} %get-tuple-element.21.slot_ref, f32[8,640]{1,0:T(8,128)S(1)} %collective-permute-done.from_sub_ref, f32[8,640]{1,0:T(8,128)S(1)} %collective-permute-done.1.from_near_ref, ...), custom_call_target="tpu_custom_call" | custom-call | tf_op jit(solution)/shard_map/second/pallas_call | solution.py:515
  18.9 0.0 copy-done
  18.9 5.8 %all-to-all-start = ((f32[16,128,128]{2,1,0:T(8,128)}), f32[16,128,128]{2,1,0:T(8,128)S(1)}, u32[]{:S(2)}, u32[]{:S(2)}) async-start(f32[16,128,128]{2,1,0:T(8,128)} %bitcast.9), calls=%async_computation | async-start | bytes 2097152 | tf_op jit(solution)/shard_map/all_to_all | solution.py:524
  24.7 0.0 copy-start.1
  24.7 2.6 %copy-done.1 = bf16[2048,1408]{1,0:T(8,128)(2,1)S(1)} copy-done((bf16[2048,1408]{1,0:T(8,128)(2,1)S(1)}, bf16[2048,1408]{1,0:T(8,128)(2,1)}, u32[]{:S(2)}) %copy-start.1) | copy-done | bytes 5767192
  27.3 0.0 copy-start.2
  27.3 1.1 %last_lines.1 = (f32[8,640]{1,0:T(8,128)S(1)}, f32[8,640]{1,0:T(8,128)S(1)}, f32[8,640]{1,0:T(8,128)S(1)}, bf16[32,640]{1,0:T(8,128)(2,1)S(1)}) custom-call(s32[2]{0:T(128)S(1)} %pad_add_fusion.place_ref, s32[40,128]{1,0:T(8,128)S(1)} %get-tuple-element.21.slot_ref, f32[64,128]{1,0:T(8,128)S(1)} %get-tuple-element.22.value_ref, ...), custom_call_target="tpu_custom_call" | custom-call | tf_op jit(solution)/shard_map/last_lines/pallas_call | solution.py:533
  28.5 0.3 collective-permute-start.3
  28.7 1.2 %copy-done.2 = bf16[2048,1408]{1,0:T(8,128)(2,1)S(1)} copy-done((bf16[2048,1408]{1,0:T(8,128)(2,1)S(1)}, bf16[2048,1408]{1,0:T(8,128)(2,1)}, u32[]{:S(2)}) %copy-start.2) | copy-done | bytes 5767192
  29.9 18.2 %nodes.1 = bf16[1,2048,1280]{2,1,0:T(8,128)(2,1)} custom-call(s32[40,128]{1,0:T(8,128)S(1)} %get-tuple-element.21.slot_ref, bf16[32,640]{1,0:T(8,128)(2,1)S(1)} %get-tuple-element.29.inj_ref.inj0_ref, bf16[32,640]{1,0:T(8,128)(2,1)S(1)} %get-tuple-element.38.inj1_ref, bf16[2048,1408]{1,0:T(8,128)(2,1)S(1)} %copy-done.2, ...), custom_call_target="tpu_custom_call" | custom-call | flops 10737418240 | bytes 20000000 | tf_op jit(solution)/shard_map/nodes/pallas_call | solution.py:554
  48.2 0.4 collective-permute-start.4
  48.6 3.1 %collective-permute-start.5 = (f32[8,640]{1,0:T(8,128)S(1)}, f32[8,640]{1,0:T(8,128)S(1)}, u32[]{:S(2)}, u32[]{:S(2)}) collective-permute-start(f32[8,640]{1,0:T(8,128)S(1)} %get-tuple-element.37), channel_id=1, source_target_pairs={{2,4},{4,2},{6,8},{8,6},{10,12},{12,10},{14,16},{16,14},{18,20},{2... | collective-permute-start | bytes 61448 | tf_op jit(solution)/shard_map/ppermute | solution.py:428
  51.7 0.0 collective-permute-done.3
  51.8 0.0 collective-permute-done.4
  51.8 2.8 %collective-permute-done.5 = f32[8,640]{1,0:T(8,128)S(1)} collective-permute-done((f32[8,640]{1,0:T(8,128)S(1)}, f32[8,640]{1,0:T(8,128)S(1)}, u32[]{:S(2)}, u32[]{:S(2)}) %collective-permute-start.5) | collective-permute-done | bytes 20512 | tf_op jit(solution)/shard_map/ppermute | solution.py:428
  54.6 0.6 %maximum_bitcast_fusion = f32[1,4,8,640]{3,2,1,0:T(8,128)} fusion(f32[1,8,640]{2,1,0:T(8,128)S(1)} %get-tuple-element.40, f32[1,8,640]{2,1,0:T(8,128)S(1)} %get-tuple-element.39, f32[1,8,640]{2,1,0:T(8,128)S(1)} %get-tuple-element.42, f32[1,8,640]{2,1,0:T(8,128)S(1)} %get-tuple-element.41), kind=kLoop, calls=%fused_computation | loop fusion | flops 61440 | bytes 163840 | tf_op jit(solution)/shard_map/broadcast_in_dim | solution.py:544
  55.3 0.0 all-to-all-done
  55.3 1.0 %copy.14 = f32[512,2,2,128]{3,2,1,0:T(2,128)} copy(f32[512,2,2,128]{3,2,1,0:T(2,128)S(1)} %bitcast.16) | data formatting | bytes 2097152
  (2 shorter events, 0.0 us)
Async XLA Ops:
  7.1 11.8 %copy-start = (bf16[2048,1408]{1,0:T(8,128)(2,1)}, bf16[2048,1408]{1,0:T(8,128)(2,1)S(1)}, u32[]{:S(2)}) copy-start(bf16[2048,1408]{1,0:T(8,128)(2,1)S(1)} %get-tuple-element.28.src_ref) | copy-start | bytes 17301508
  7.1 9.5 %collective-permute-start = (f32[8,640]{1,0:T(8,128)S(1)}, f32[8,640]{1,0:T(8,128)S(1)}, u32[]{:S(2)}, u32[]{:S(2)}) collective-permute-start(f32[8,640]{1,0:T(8,128)S(1)} %get-tuple-element.23), channel_id=1, source_target_pairs={{0,1},{1,0},{2,3},{3,2},{4,5},{5,4},{6,7},{7,6},{8,9},{9,8},{10,11... | collective-permute-start | bytes 61448 | tf_op jit(solution)/shard_map/ppermute | solution.py:428
  8.1 8.5 %collective-permute-start.1 = (f32[8,640]{1,0:T(8,128)S(1)}, f32[8,640]{1,0:T(8,128)S(1)}, u32[]{:S(2)}, u32[]{:S(2)}) collective-permute-start(f32[8,640]{1,0:T(8,128)S(1)} %get-tuple-element.24), channel_id=1, source_target_pairs={{0,2},{2,0},{4,6},{6,4},{8,10},{10,8},{12,14},{14,12},{16,18},{18,... | collective-permute-start | bytes 61448 | tf_op jit(solution)/shard_map/ppermute | solution.py:428
  9.5 7.1 %collective-permute-start.2 = (f32[8,640]{1,0:T(8,128)S(1)}, f32[8,640]{1,0:T(8,128)S(1)}, u32[]{:S(2)}, u32[]{:S(2)}) collective-permute-start(f32[8,640]{1,0:T(8,128)S(1)} %get-tuple-element.25), channel_id=1, source_target_pairs={{2,4},{4,2},{6,8},{8,6},{10,12},{12,10},{14,16},{16,14},{18,20},{2... | collective-permute-start | bytes 61448 | tf_op jit(solution)/shard_map/ppermute | solution.py:428
  18.9 36.4 %all-to-all-start = ((f32[16,128,128]{2,1,0:T(8,128)}), f32[16,128,128]{2,1,0:T(8,128)S(1)}, u32[]{:S(2)}, u32[]{:S(2)}) async-start(f32[16,128,128]{2,1,0:T(8,128)} %bitcast.9), calls=%async_computation | async-start | bytes 2097152 | tf_op jit(solution)/shard_map/all_to_all | solution.py:524
  24.7 2.6 %copy-start.1 = (bf16[2048,1408]{1,0:T(8,128)(2,1)S(1)}, bf16[2048,1408]{1,0:T(8,128)(2,1)}, u32[]{:S(2)}) copy-start(bf16[2048,1408]{1,0:T(8,128)(2,1)} %copy-done) | copy-start | bytes 17301508
  27.3 2.6 %copy-start.2 = (bf16[2048,1408]{1,0:T(8,128)(2,1)S(1)}, bf16[2048,1408]{1,0:T(8,128)(2,1)}, u32[]{:S(2)}) copy-start(bf16[2048,1408]{1,0:T(8,128)(2,1)} %copy-done) | copy-start | bytes 17301508
  28.5 23.3 %collective-permute-start.3 = (f32[8,640]{1,0:T(8,128)S(1)}, f32[8,640]{1,0:T(8,128)S(1)}, u32[]{:S(2)}, u32[]{:S(2)}) collective-permute-start(f32[8,640]{1,0:T(8,128)S(1)} %get-tuple-element.35), channel_id=1, source_target_pairs={{0,1},{1,0},{2,3},{3,2},{4,5},{5,4},{6,7},{7,6},{8,9},{9,8},{10,11... | collective-permute-start | bytes 61448 | tf_op jit(solution)/shard_map/ppermute | solution.py:428
  48.2 3.6 %collective-permute-start.4 = (f32[8,640]{1,0:T(8,128)S(1)}, f32[8,640]{1,0:T(8,128)S(1)}, u32[]{:S(2)}, u32[]{:S(2)}) collective-permute-start(f32[8,640]{1,0:T(8,128)S(1)} %get-tuple-element.36), channel_id=1, source_target_pairs={{0,2},{2,0},{4,6},{6,4},{8,10},{10,8},{12,14},{14,12},{16,18},{18,... | collective-permute-start | bytes 61448 | tf_op jit(solution)/shard_map/ppermute | solution.py:428
  48.6 6.0 %collective-permute-start.5 = (f32[8,640]{1,0:T(8,128)S(1)}, f32[8,640]{1,0:T(8,128)S(1)}, u32[]{:S(2)}, u32[]{:S(2)}) collective-permute-start(f32[8,640]{1,0:T(8,128)S(1)} %get-tuple-element.37), channel_id=1, source_target_pairs={{2,4},{4,2},{6,8},{8,6},{10,12},{12,10},{14,16},{16,14},{18,20},{2... | collective-permute-start | bytes 61448 | tf_op jit(solution)/shard_map/ppermute | solution.py:428

commit v3 on v2

--- a/solution.py
+++ b/solution.py
@@ -30,16 +30,33 @@
 BF16 = jnp.bfloat16
 
 
-def fit_tables():
-    step = np.arange(SPANS * DELAY)
+def fit_table():
+    step = np.arange(DELAY)
     harmonic = np.arange(1, BINS + 1)
     angles = (step[:, None] * harmonic[None, :] % DFT_LEN) * (2.0 * math.pi / DFT_LEN)
     twiddle = np.stack([np.cos(angles), -np.sin(angles)], axis=1) / math.sqrt(DFT_LEN)
     table = np.einsum("uch,st->uscht", twiddle, np.eye(SCEN))
-    table = table.reshape(SPANS, COLS, PHASOR).astype(np.float32)
+    table = table.reshape(COLS, PHASOR).astype(np.float32)
     high = table.astype(jnp.bfloat16)
     low = (table - high.astype(np.float32)).astype(jnp.bfloat16)
-    return np.concatenate([high, low, high], axis=1)
+    return np.concatenate([high, low], axis=1)
+
+
+def fit(values, table_ref):
+    high, low = split(values)
+    both = dot(high, table_ref[...])
+    return both[:, :PHASOR] + both[:, PHASOR:] + dot(low, table_ref[:, :PHASOR])
+
+
+def span_turn():
+    angles = 2.0 * math.pi / DFT_LEN * DELAY * np.repeat(np.arange(1, BINS + 1), SCEN)
+    return np.stack([np.cos(angles), np.sin(angles)] * 4).astype(np.float32)
+
+
+def turned(values, turn_ref):
+    cosine, sine = turn_ref[0:1, :], turn_ref[1:2, :]
+    real, imag = values[:, :LANES], values[:, LANES:]
+    return jnp.concatenate([real * cosine + imag * sine, imag * cosine - real * sine], axis=1)
 
 
 def dot(left, right):
@@ -142,13 +159,14 @@
 
 def lines_kernel(
     place_ref, nodes_hbm, admit_hbm, self_hbm, history_hbm, coupling_hbm, sources_hbm,
+    region_hbm, prior_hbm, old_hbm, table_hbm, turn_hbm,
     sub_ref, near_ref, far_ref, src_ref, term_ref, rows_ref, gathered_ref, inj_ref,
-    slot_ref, value_ref, self_ref,
+    slot_ref, value_ref, self_ref, region_ref, prior_ref, old_ref, table_ref, turn_ref,
     nodes_ref, admit_ref, history_ref, blocks, early_sem, src_sem, late_sem, block_sem,
 ):
     chunks = 2
     depth = NODES // chunks
-    first_cols, later_cols = pl.ds(0, COLS), pl.ds(COLS, COLS)
+    first_cols = pl.ds(0, COLS)
 
     def early(index, source, target):
         return pltpu.make_async_copy(source, target, early_sem.at[index])
@@ -170,22 +188,28 @@
     admit_copy = early(1, admit_hbm, admit_ref)
     self_copy = early(2, self_hbm, self_ref)
     history_copy = early(3, history_hbm, history_ref)
-    src_later = pltpu.make_async_copy(
-        sources_hbm.at[0, :, later_cols], src_ref.at[:, later_cols], late_sem.at[0]
-    )
-    term_copy = pltpu.make_async_copy(
-        coupling_hbm.at[0, pl.ds(0, TERM_DEV)], term_ref, late_sem.at[1]
-    )
+    late_copies = [
+        pltpu.make_async_copy(source, target, late_sem.at[index])
+        for index, (source, target) in enumerate(
+            [
+                (coupling_hbm.at[0, pl.ds(0, TERM_DEV)], term_ref),
+                (region_hbm, region_ref),
+                (prior_hbm, prior_ref),
+                (old_hbm, old_ref),
+                (table_hbm, table_ref),
+                (turn_hbm, turn_ref),
+            ]
+        )
+    ]
     nodes_copy.start()
     admit_copy.start()
     self_copy.start()
     history_copy.start()
-    src_copy(0).start()
+    for part in range(chunks):
+        src_copy(part).start()
     nodes_copy.wait()
     for slot in range(LINES):
         block_copy(slot).start()
-    for part in range(1, chunks):
-        src_copy(part).start()
     admit_copy.wait()
     self_copy.wait()
     history_copy.wait()
@@ -203,7 +227,7 @@
     self_col = jnp.sum(jnp.where(own_row, self_ref[...], 0.0), axis=1, keepdims=True)
     wanted = jnp.where(iota((1, LANES), 1) < LINES, along, -1)
     hot = jnp.where(iota((NODES, LANES), 0) == wanted, 1.0, 0.0).astype(BF16)
-    src_ref[:, SPANS * COLS :] = hot
+    src_ref[:, COLS:] = hot
     slot_ref[:LINES, :] = jnp.broadcast_to(down, (LINES, LANES))
     slot_ref[LINES:, :] = jnp.broadcast_to(along, (8, LANES))
     value_ref[:LINES, :] = jnp.broadcast_to(admit, (LINES, LANES))
@@ -211,8 +235,8 @@
 
     for slot in range(LINES):
         block_copy(slot).wait()
-    term_copy.start()
-    src_later.start()
+    for copy in late_copies:
+        copy.start()
     rows = dot(choose, blocks[...]).astype(BF16)
     rows_ref[...] = rows
     gathered = dot(rows, hot).astype(BF16)
@@ -227,42 +251,29 @@
         picked = picked + dot(left[:, span], src_ref[span, :COLS])
     volts = volts + picked[:LINES] + self_col * (picked[LINES:] + total.astype(F32))
     send_out(volts, lines, admit, down, place_ref, sub_ref, near_ref, far_ref)
-    src_later.wait()
-    term_copy.wait()
+    for copy in late_copies:
+        copy.wait()
 
 
 def terminals_kernel(
     capacity, slots,
-    slot_ref, inj_ref, src_ref, term_ref, self_ref, region_hbm, prior_hbm, old_hbm, table_hbm,
-    packed_ref, left_ref, second_table,
-    region_ref, prior_ref, old_ref, first_table, sems,
+    slot_ref, inj_ref, src_ref, term_ref, self_ref, region_ref, prior_ref, old_ref, table_ref, turn_ref,
+    sources_hbm,
+    packed_ref, left_ref,
+    later_ref, later_sem,
 ):
-    copies = [
-        pltpu.make_async_copy(source, target, sems.at[index])
-        for index, (source, target) in enumerate(
-            [
-                (region_hbm, region_ref),
-                (old_hbm, old_ref),
-                (prior_hbm, prior_ref),
-                (table_hbm.at[0], first_table),
-                (table_hbm.at[1], second_table),
-            ]
-        )
-    ]
-    for copy in copies:
-        copy.start()
+    later_copy = pltpu.make_async_copy(sources_hbm.at[0, :, pl.ds(COLS, COLS)], later_ref, later_sem)
+    later_copy.start()
     down = slot_ref[:LINES, :1]
     along = slot_ref[LINES : LINES + 1, :]
     first = first_along(along, down)
     term_self = column_of(self_ref[:, :TERM_DEV])
 
-    sources = slice(0, SPANS * COLS)
-    small = small_left(dot(term_ref[...], src_ref[:, SPANS * COLS :]), term_self, along, first, 0)
-    volts = dot(term_ref[...], src_ref[:, sources])
-    volts = volts + term_self * src_ref[:TERM_DEV, sources].astype(F32)
-    from_lines = dot(small, three_times(inj_ref[...]))
-
-    copies[0].wait()
+    products = dot(term_ref[...], src_ref[...])
+    small = small_left(products[:, COLS:], term_self, along, first, 0)
+    volts = products[:, :COLS] + term_self * src_ref[:TERM_DEV, :COLS].astype(F32)
+    volts = volts + dot(small, three_times(inj_ref[...]))
+
     region_row = region_ref[...]
     region_col = column_of(region_row.astype(F32)).astype(jnp.int32)
     earlier = iota((TERM_DEV, TERM_DEV), 0) < iota((TERM_DEV, TERM_DEV), 1)
@@ -273,41 +284,36 @@
     pack = jnp.where(iota((slots, TERM_DEV), 0) == dest, 1.0, 0.0).astype(BF16)
     left_ref[...] = dot(pack, small).astype(BF16)
 
-    for copy in copies[1:]:
-        copy.wait()
-    differences = volts - old_ref[...].astype(F32)
+    doubled = jnp.concatenate([pack, pack], axis=1)
+
+    def put(span_index, running):
+        filled = dot(doubled, jnp.concatenate(split(running), axis=0))
+        for part in range(2):
+            packed_ref[pl.ds(2 * span_index + part, slots, stride=4), :] = filled[
+                :, part * LANES : (part + 1) * LANES
+            ]
+
     running = jnp.concatenate(
         [prior_ref[pl.ds(part, TERM_DEV, stride=2), :] for part in range(2)], axis=1
     )
-    highs, lows = [], []
-    for span_index, table_ref in enumerate([first_table, second_table]):
-        values = differences[:, span_index * COLS : (span_index + 1) * COLS]
-        if span_index == 0:
-            values = values + from_lines
-        high, low = split(values)
-        running = running + dot(jnp.concatenate([high, high, low], axis=1), table_ref[...])
-        high, low = split(running)
-        highs.append(high)
-        lows.append(low)
-    fitted = jnp.concatenate(
-        [jnp.concatenate(highs, axis=1), jnp.concatenate(lows, axis=1)], axis=0
-    )
-    filled = dot(jnp.concatenate([pack, pack], axis=1), fitted)
-    for part in range(4):
-        packed_ref[pl.ds(part, slots, stride=4), :] = filled[:, part * LANES : (part + 1) * LANES]
+    running = running + fit(volts - old_ref[:, :COLS].astype(F32), table_ref)
+    put(0, running)
+    later_copy.wait()
+    volts = dot(term_ref[...], later_ref[...]) + term_self * later_ref[:TERM_DEV, :].astype(F32)
+    put(1, running + turned(fit(volts - old_ref[:, COLS:].astype(F32), table_ref), turn_ref))
 
 
 def second_kernel(
     slots,
-    place_ref, slot_ref, from_sub_ref, from_near_ref, from_far_ref, left_ref, table_ref, packed_in_ref,
+    place_ref, slot_ref, from_sub_ref, from_near_ref, from_far_ref, left_ref, table_ref, turn_ref, packed_in_ref,
     packed_ref,
 ):
     down = slot_ref[:LINES, :1]
     along = slot_ref[LINES : LINES + 1, :]
     lines = arrived(place_ref, from_sub_ref, from_near_ref, from_far_ref)
     _, injection = injected(lines, along, down)
-    spectrum = dot(jnp.concatenate([injection, injection], axis=1), table_ref[: 2 * COLS, :])
-    high, low = split(spectrum)
+    both = dot(injection, table_ref[...])
+    high, low = split(turned(both[:, :PHASOR] + both[:, PHASOR:], turn_ref))
     left = left_ref[...]
     change = dot(
         jnp.concatenate([left, left], axis=1),
@@ -323,10 +329,23 @@
 
 def last_lines_kernel(
     place_ref, slot_ref, value_ref, from_sub_ref, from_near_ref, from_far_ref,
-    rows_ref, gathered_ref, src_ref, started_ref,
+    rows_ref, gathered_ref, sources_hbm, started_ref,
     sub_ref, near_ref, far_ref, inj_ref,
+    src_ref, sems,
 ):
     del started_ref
+    chunks = 2
+    depth = NODES // chunks
+    copies = [
+        pltpu.make_async_copy(
+            sources_hbm.at[0, pl.ds(part * depth, depth), pl.ds(COLS, COLS)],
+            src_ref.at[pl.ds(part * depth, depth)],
+            sems.at[part],
+        )
+        for part in range(chunks)
+    ]
+    for copy in copies:
+        copy.start()
     down = slot_ref[:LINES, :1]
     along = slot_ref[LINES : LINES + 1, :]
     admit, self_col = value_ref[:LINES, :1], value_ref[LINES:, :1]
@@ -335,20 +354,21 @@
     inj_ref[...] = injection
     own = jnp.where(iota((LINES, NODES), 1) == jnp.maximum(down, 0), 1.0, 0.0).astype(BF16)
     left = jnp.concatenate([rows_ref[...], own], axis=0)
-    picked = dot(left, src_ref[:, COLS : SPANS * COLS])
-    volts = picked[:LINES] + dot(gathered_ref[:, :LINES], injection)
-    volts = volts + self_col * (picked[LINES:] + total.astype(F32))
+    volts = dot(gathered_ref[:, :LINES], injection)
+    picked = jnp.zeros((2 * LINES, COLS), F32)
+    for part in range(chunks):
+        copies[part].wait()
+        span = slice(part * depth, (part + 1) * depth)
+        picked = picked + dot(left[:, span], src_ref[span, :])
+    volts = volts + picked[:LINES] + self_col * (picked[LINES:] + total.astype(F32))
     send_out(volts, lines, admit, down, place_ref, sub_ref, near_ref, far_ref)
 
 
 def nodes_kernel(
-    slot_ref, inj0_ref, inj1_ref, src_ref, self_ref, coupling_hbm,
+    inj0_ref, inj1_ref, self_ref, nodes_hbm, sources_hbm, coupling_hbm,
     volts_hbm,
-    matrix_buf, volts_buf, small_buf, in_sem, out_sem,
+    nodes_ref, drive_ref, matrix_buf, volts_buf, early_sem, in_sem, out_sem,
 ):
-    down = slot_ref[:LINES, :1]
-    along = slot_ref[LINES : LINES + 1, :]
-    first = first_along(along, down)
     blocks = NODES // ROWS
 
     def load(block, place):
@@ -359,8 +379,20 @@
         rows = pl.ds(pl.multiple_of(block * ROWS, ROWS), ROWS)
         return pltpu.make_async_copy(volts_buf.at[place], volts_hbm.at[0, rows], out_sem.at[place])
 
+    nodes_copy = pltpu.make_async_copy(nodes_hbm, nodes_ref, early_sem.at[0])
+    drive_copy = pltpu.make_async_copy(sources_hbm.at[0], drive_ref, early_sem.at[1])
+    nodes_copy.start()
+    drive_copy.start()
     load(0, 0).start()
-    small_buf[...] = three_times(jnp.concatenate([inj0_ref[...], inj1_ref[...]], axis=1))
+    nodes_copy.wait()
+    drive_copy.wait()
+
+    both = jnp.concatenate([inj0_ref[...], inj1_ref[...]], axis=1).astype(F32)
+    for slot in range(LINES):
+        node = jnp.maximum(nodes_ref[0, slot // LPP, slot % LPP], 0)
+        rows = pl.ds(pl.multiple_of((node // 16) * 16, 16), 16)
+        extra = jnp.where(iota((16, 1), 0) == node % 16, both[slot : slot + 1, :], 0.0)
+        drive_ref[rows, :] = (drive_ref[rows, :].astype(F32) + extra).astype(BF16)
 
     @pl.loop(0, blocks)
     def _(block):
@@ -377,19 +409,16 @@
             store(block - 2, place).wait()
 
         start = pl.multiple_of(block * ROWS, ROWS)
-        matrix = matrix_buf[place]
-        self_col = jnp.concatenate(
+        block_self = jnp.concatenate(
             [
                 column_of(self_ref[:, pl.ds(pl.multiple_of(start + part, 256), 256)])
                 for part in range(0, ROWS, 256)
             ],
             axis=0,
         )
-        products = dot(matrix, src_ref[...])
-        small = small_left(products[:, SPANS * COLS :], self_col, along, first, start)
-        total = products[:, : SPANS * COLS] + dot(small, small_buf[...])
-        total = total + self_col * src_ref[pl.ds(start, ROWS), : SPANS * COLS].astype(F32)
-        volts_buf[place] = total.astype(BF16)
+        result = dot(matrix_buf[place], drive_ref[...])
+        result = result + block_self * drive_ref[pl.ds(start, ROWS), :].astype(F32)
+        volts_buf[place] = result.astype(BF16)
         store(block, place).start()
 
     for block in range(blocks - 2, blocks):
@@ -453,14 +482,16 @@
     place = jnp.stack([odd_region, odd_sub]).astype(jnp.int32)
     block = struct((LPP, COLS), F32)
     injection = struct((LINES, COLS), BF16)
-    tables = fit_tables()
     DMA = pltpu.SemaphoreType.DMA
 
-    (sub, near, far, src, term, rows, gathered, inj0, slot, value, self_row) = pl.pallas_call(
+    (
+        sub, near, far, src, term, rows, gathered, inj0, slot, value, self_row,
+        region, prior, old, table, turn,
+    ) = pl.pallas_call(
         lines_kernel,
         out_shape=[
             block, block, block,
-            struct((NODES, SPANS * COLS + LANES), BF16),
+            struct((NODES, COLS + LANES), BF16),
             struct((TERM_DEV, NODES), BF16),
             struct((LINES, NODES), BF16),
             struct((LINES, LANES), BF16),
@@ -468,58 +499,52 @@
             struct((LINES + 8, LANES), jnp.int32),
             struct((2 * LINES, LANES), F32),
             struct((1, NODES), F32),
+            struct((1, TERM_DEV), jnp.int32),
+            struct((TERM_DEV * 2, LANES), F32),
+            struct((TERM_DEV, SPANS * COLS), BF16),
+            struct((COLS, 2 * PHASOR), BF16),
+            struct((8, LANES), F32),
         ],
-        in_specs=[SM] + [HB] * 6,
-        out_specs=[VM] * 11,
+        in_specs=[SM] + [HB] * 11,
+        out_specs=[VM] * 16,
         scratch_shapes=[
             pltpu.SMEM((1, NEIGH, LPP), jnp.int32),
             pltpu.SMEM((1, NEIGH, LPP), F32),
             pltpu.VMEM((1, NEIGH, LPP, COLS), F32),
             pltpu.VMEM((LINES * 16, NODES), BF16),
-            DMA((4,)), DMA((2,)), DMA((2,)), DMA((LINES,)),
+            DMA((4,)), DMA((2,)), DMA((6,)), DMA((LINES,)),
         ],
         compiler_params=params(),
         name="lines",
-    )(place, *in_hbm(line_nodes, line_admit, self_term, history, coupling, sources))
+    )(
+        place,
+        *in_hbm(
+            line_nodes, line_admit, self_term, history, coupling, sources,
+            term_region.reshape(1, TERM_DEV), prior_phasor.reshape(TERM_DEV * 2, LANES), old_samples,
+            jnp.asarray(fit_table()), jnp.asarray(span_turn()),
+        ),
+    )
 
     from_near, from_sub, from_far = exchange(sub, near, far)
 
-    packed, left, table = pl.pallas_call(
+    packed, left = pl.pallas_call(
         functools.partial(terminals_kernel, capacity, slots),
-        out_shape=[
-            struct((slots * 4, LANES), F32),
-            struct((slots, LANES), BF16),
-            struct((3 * COLS, PHASOR), BF16),
-        ],
-        in_specs=[VM] * 5 + [HB] * 4,
-        out_specs=[VM] * 3,
-        scratch_shapes=[
-            pltpu.VMEM((1, TERM_DEV), jnp.int32),
-            pltpu.VMEM((TERM_DEV * 2, LANES), F32),
-            pltpu.VMEM((TERM_DEV, SPANS * COLS), BF16),
-            pltpu.VMEM((3 * COLS, PHASOR), BF16),
-            DMA((5,)),
-        ],
+        out_shape=[struct((slots * 4, LANES), F32), struct((slots, LANES), BF16)],
+        in_specs=[VM] * 10 + [HB],
+        out_specs=[VM] * 2,
+        scratch_shapes=[pltpu.VMEM((NODES, COLS), BF16), DMA],
         compiler_params=params(),
         name="terminals",
-    )(
-        slot, inj0, src, term, self_row,
-        *in_hbm(
-            term_region.reshape(1, TERM_DEV),
-            prior_phasor.reshape(TERM_DEV * 2, LANES),
-            old_samples,
-            jnp.asarray(tables),
-        ),
-    )
+    )(slot, inj0, src, term, self_row, region, prior, old, table, turn, *in_hbm(sources))
 
     packed = pl.pallas_call(
         functools.partial(second_kernel, slots),
         out_shape=struct((slots * 4, LANES), F32),
-        in_specs=[SM] + [VM] * 7,
+        in_specs=[SM] + [VM] * 8,
         out_specs=VM,
         compiler_params=params(),
         name="second",
-    )(place, slot, from_sub, from_near, from_far, left, table, packed)
+    )(place, slot, from_sub, from_near, from_far, left, table, turn, packed)
 
     result = lax.all_to_all(
         packed.reshape(region_count, capacity * 4, LANES),
@@ -533,11 +558,15 @@
     sub, near, far, inj1 = pl.pallas_call(
         last_lines_kernel,
         out_shape=[block, block, block, injection],
-        in_specs=[SM] + [VM] * 8 + [pl.BlockSpec(memory_space=pl.ANY)],
+        in_specs=[SM] + [VM] * 7 + [HB, pl.BlockSpec(memory_space=pl.ANY)],
         out_specs=[VM] * 4,
+        scratch_shapes=[pltpu.VMEM((NODES, COLS), BF16), DMA((2,))],
         compiler_params=params(),
         name="last_lines",
-    )(place, slot, value, from_sub, from_near, from_far, rows, gathered, src, packed)
+    )(
+        place, slot, value, from_sub, from_near, from_far, rows, gathered,
+        *in_hbm(sources), packed,
+    )
 
     from_near, from_sub, from_far = exchange(sub, near, far)
     none = jnp.zeros_like(from_sub)
@@ -554,20 +583,21 @@
     node_voltages = pl.pallas_call(
         nodes_kernel,
         out_shape=struct((1, NODES, SPANS * COLS), BF16),
-        in_specs=[VM] * 5 + [HB],
+        in_specs=[VM] * 3 + [HB] * 3,
         out_specs=HB,
         scratch_shapes=[
+            pltpu.SMEM((1, NEIGH, LPP), jnp.int32),
+            pltpu.VMEM((NODES, SPANS * COLS), BF16),
             pltpu.VMEM((2, ROWS, NODES), BF16),
             pltpu.VMEM((2, ROWS, SPANS * COLS), BF16),
-            pltpu.VMEM((LANES, SPANS * COLS), BF16),
-            DMA((2,)), DMA((2,)),
+            DMA((2,)), DMA((2,)), DMA((2,)),
         ],
         compiler_params=params(),
         cost_estimate=pl.CostEstimate(
             flops=2 * NODES * NODES * SPANS * COLS, bytes_accessed=20_000_000, transcendentals=0
         ),
         name="nodes",
-    )(slot, inj0, inj1, src, self_row, *in_hbm(coupling))
+    )(inj0, inj1, self_row, *in_hbm(line_nodes, sources, coupling))
     return (next_history, node_voltages, phasors)
 
 

time: 56.7 us -> 50.9 us (0.90)
  local copies, waits for them, and re-layouts: 4.84 us -> 0.97 us
  Pallas kernels: 32.4 us -> 31.4 us
    unnamed x7 -> x1, local copies, waits for them, and re-layouts: 4.84 us -> 0.97 us
    pallas_call x1, Pallas kernels: 18.2 us -> 16 us  [body(): pl.pallas_call(nodes_kernel, out_shape=struct((1, NODES, SPANS * COLS), B...]
    pallas_call x1, Pallas kernels: 1.14 us -> 2.89 us  [body(): pl.pallas_call(last_lines_kernel, out_shape=[block, block, block, injecti...]
  transfers between devices with their start and end apart: 7 -> 7, of which waited for: 1 -> 1; matrix products, arithmetic and copies ran while one was open for 1% -> 1% of each run, Pallas kernels for 42% -> 46%
where the time goes in v3:
time: 50.9 us; the launch traced here: 50.6 us
  Pallas kernels  31.4 us (62%)
  starting transfers between devices  14.4 us (28%)
  waiting for transfers between devices  2.39 us (5%)
  local copies, waits for them, and re-layouts  0.97 us (2%)
  between operations  0.75 us (1%)
  other arithmetic  0.73 us (1%)
    pallas_call x1, Pallas kernels, body(): pl.pallas_call(nodes_kernel, out_shape=struct((1, NODES, SPANS * COLS), B...  16 us
    ppermute x6, starting transfers between devices, swap(): return lax.ppermute(block, axis, pairs)  8.94 us
    pallas_call x1, Pallas kernels, body(): pl.pallas_call(lines_kernel, out_shape=[block, block, block, struct((NODE...  5.78 us
    all_to_all x1, starting transfers between devices, body(): lax.all_to_all(packed.reshape(region_count, capacity * 4, LANES), 'region...  5.42 us
    pallas_call x1, Pallas kernels, body(): pl.pallas_call(functools.partial(terminals_kernel, capacity, slots), out_...  4.46 us
    pallas_call x1, Pallas kernels, body(): pl.pallas_call(last_lines_kernel, out_shape=[block, block, block, injecti...  2.89 us
    ppermute x6, waiting for transfers between devices, swap(): return lax.ppermute(block, axis, pairs)  2.38 us
    pallas_call x1, Pallas kernels, body(): pl.pallas_call(functools.partial(second_kernel, slots), out_shape=struct(...  2.28 us
  transfers between devices with their start and end apart: 7, of which 1 were waited for; matrix products, arithmetic and copies ran while one was open for 1% of the time, Pallas kernels for 46%

profile of v3, /device:TPU:13, one launch (start us, length us, event | category | flops | bytes accessed | tf_op | source)
XLA Modules:
  0.0 50.6 jit_solution(654382704952332839)
XLA Ops:
  0.6 0.1 pad_add_fusion.place_ref
  0.7 5.8 %lines.1 = (f32[8,640]{1,0:T(8,128)S(1)}, f32[8,640]{1,0:T(8,128)S(1)}, f32[8,640]{1,0:T(8,128)S(1)}, bf16[2048,768]{1,0:T(8,128)(2,1)S(1)}, bf16[256,2048]{1,0:...) custom-call(s32[2]{0:T(128)S(1)} %pad_add_fusion.place_ref, ...), custom_call_target="tpu_custom_call" | custom-call | tf_op jit(solution)/shard_map/lines/pallas_call | solution.py:490
  6.5 1.1 %collective-permute-start = (f32[8,640]{1,0:T(8,128)S(1)}, f32[8,640]{1,0:T(8,128)S(1)}, u32[]{:S(2)}, u32[]{:S(2)}) collective-permute-start(f32[8,640]{1,0:T(8,128)S(1)} %get-tuple-element.27), channel_id=1, source_target_pairs={{0,1},{1,0},{2,3},{3,2},{4,5},{5,4},{6,7},{7,6},{8,9},{9,8},{10,11... | collective-permute-start | bytes 61448 | tf_op jit(solution)/shard_map/ppermute | solution.py:457
  7.6 0.7 %collective-permute-start.1 = (f32[8,640]{1,0:T(8,128)S(1)}, f32[8,640]{1,0:T(8,128)S(1)}, u32[]{:S(2)}, u32[]{:S(2)}) collective-permute-start(f32[8,640]{1,0:T(8,128)S(1)} %get-tuple-element.28), channel_id=1, source_target_pairs={{0,2},{2,0},{4,6},{6,4},{8,10},{10,8},{12,14},{14,12},{16,18},{18,... | collective-permute-start | bytes 61448 | tf_op jit(solution)/shard_map/ppermute | solution.py:457
  8.4 3.4 %collective-permute-start.2 = (f32[8,640]{1,0:T(8,128)S(1)}, f32[8,640]{1,0:T(8,128)S(1)}, u32[]{:S(2)}, u32[]{:S(2)}) collective-permute-start(f32[8,640]{1,0:T(8,128)S(1)} %get-tuple-element.29), channel_id=1, source_target_pairs={{2,4},{4,2},{6,8},{8,6},{10,12},{12,10},{14,16},{16,14},{18,20},{2... | collective-permute-start | bytes 61448 | tf_op jit(solution)/shard_map/ppermute | solution.py:457
  11.7 4.5 %terminals.1 = (f32[2048,128]{1,0:T(8,128)S(1)}, bf16[512,128]{1,0:T(8,128)(2,1)S(1)}) custom-call(s32[40,128]{1,0:T(8,128)S(1)} %get-tuple-element.25.slot_ref, bf16[32,640]{1,0:T(8,128)(2,1)S(1)} %get-tuple-element.32.inj_ref.inj0_ref, bf16[2048,768]{1,0:T(8,128)(2,1)S(1)} %get-tuple-element.33.src_ref, bf16[256,2048]{1,0:T(8,128)(2,1)S(1)} %get-tuple-element.34.term_ref, ...), custom_call_target="tpu_custom_call" | custom-call | tf_op jit(solution)/shard_map/terminals/pallas_call | solution.py:530
  16.2 0.0 collective-permute-done.from_sub_ref
  16.2 0.0 collective-permute-done.1.from_near_ref
  16.2 0.0 collective-permute-done.2.from_far_ref
  16.2 2.3 %second.1.started_ref = f32[2048,128]{1,0:T(8,128)} custom-call(s32[2]{0:T(128)S(1)} %pad_add_fusion.place_ref, s32[40,128]{1,0:T(8,128)S(1)} %get-tuple-element.25.slot_ref, f32[8,640]{1,0:T(8,128)S(1)} %collective-permute-done.from_sub_ref, f32[8,640]{1,0:T(8,128)S(1)} %collective-permute-done.1.from_near_ref, ...), custom_call_target="tpu_custom_call" | custom-call | tf_op jit(solution)/shard_map/second/pallas_call | solution.py:540
  18.5 5.4 %all-to-all-start = ((f32[16,128,128]{2,1,0:T(8,128)}), f32[16,128,128]{2,1,0:T(8,128)S(1)}, u32[]{:S(2)}, u32[]{:S(2)}) async-start(f32[16,128,128]{2,1,0:T(8,128)} %bitcast.9), calls=%async_computation | async-start | bytes 2097152 | tf_op jit(solution)/shard_map/all_to_all | solution.py:549
  23.9 2.9 %last_lines.1 = (f32[8,640]{1,0:T(8,128)S(1)}, f32[8,640]{1,0:T(8,128)S(1)}, f32[8,640]{1,0:T(8,128)S(1)}, bf16[32,640]{1,0:T(8,128)(2,1)S(1)}) custom-call(s32[2]{0:T(128)S(1)} %pad_add_fusion.place_ref, s32[40,128]{1,0:T(8,128)S(1)} %get-tuple-element.25.slot_ref, f32[64,128]{1,0:T(8,128)S(1)} %get-tuple-element.26.value_ref, ...), custom_call_target="tpu_custom_call" | custom-call | tf_op jit(solution)/shard_map/last_lines/pallas_call | solution.py:558
  26.8 0.1 collective-permute-start.3
  26.9 0.6 %collective-permute-start.4 = (f32[8,640]{1,0:T(8,128)S(1)}, f32[8,640]{1,0:T(8,128)S(1)}, u32[]{:S(2)}, u32[]{:S(2)}) collective-permute-start(f32[8,640]{1,0:T(8,128)S(1)} %get-tuple-element.44), channel_id=1, source_target_pairs={{0,2},{2,0},{4,6},{6,4},{8,10},{10,8},{12,14},{14,12},{16,18},{18,... | collective-permute-start | bytes 61448 | tf_op jit(solution)/shard_map/ppermute | solution.py:457
  27.6 3.0 %collective-permute-start.5 = (f32[8,640]{1,0:T(8,128)S(1)}, f32[8,640]{1,0:T(8,128)S(1)}, u32[]{:S(2)}, u32[]{:S(2)}) collective-permute-start(f32[8,640]{1,0:T(8,128)S(1)} %get-tuple-element.45), channel_id=1, source_target_pairs={{2,4},{4,2},{6,8},{8,6},{10,12},{12,10},{14,16},{16,14},{18,20},{2... | collective-permute-start | bytes 61448 | tf_op jit(solution)/shard_map/ppermute | solution.py:457
  30.6 16.0 %nodes.1 = bf16[1,2048,1280]{2,1,0:T(8,128)(2,1)} custom-call(bf16[32,640]{1,0:T(8,128)(2,1)S(1)} %get-tuple-element.32.inj_ref.inj0_ref, bf16[32,640]{1,0:T(8,128)(2,1)S(1)} %get-tuple-element.46.inj1_ref, f32[1,2048]{1,0:T(1,128)S(1)} %get-tuple-element.35.self_ref, s32[1,4,8]{2,1,0:T(4,128)} %nodes_hbm.3, bf16[1,2048,1280]{2,1,0:T(8,128)(2,1)} %sources_hbm.7, ...), custom_call_target="tpu_custom_call" | custom-call | flops 10737418240 | bytes 20000000 | tf_op jit(solution)/shard_map/nodes/pallas_call | solution.py:583
  46.6 0.0 collective-permute-done.3
  46.6 0.0 collective-permute-done.4
  46.7 2.4 %collective-permute-done.5 = f32[8,640]{1,0:T(8,128)S(1)} collective-permute-done((f32[8,640]{1,0:T(8,128)S(1)}, f32[8,640]{1,0:T(8,128)S(1)}, u32[]{:S(2)}, u32[]{:S(2)}) %collective-permute-start.5) | collective-permute-done | bytes 20512 | tf_op jit(solution)/shard_map/ppermute | solution.py:457
  49.0 0.6 %maximum_bitcast_fusion = f32[1,4,8,640]{3,2,1,0:T(8,128)} fusion(f32[1,8,640]{2,1,0:T(8,128)S(1)} %get-tuple-element.48, f32[1,8,640]{2,1,0:T(8,128)S(1)} %get-tuple-element.47, f32[1,8,640]{2,1,0:T(8,128)S(1)} %get-tuple-element.50, f32[1,8,640]{2,1,0:T(8,128)S(1)} %get-tuple-element.49), kind=kLoop, calls=%fused_computation | loop fusion | flops 61440 | bytes 163840 | tf_op jit(solution)/shard_map/broadcast_in_dim | solution.py:573
  49.7 0.0 all-to-all-done
  49.7 1.0 %copy.15 = f32[512,2,2,128]{3,2,1,0:T(2,128)} copy(f32[512,2,2,128]{3,2,1,0:T(2,128)S(1)} %bitcast.16) | data formatting | bytes 2097152
  (2 shorter events, 0.0 us)
Async XLA Ops:
  6.5 9.7 %collective-permute-start = (f32[8,640]{1,0:T(8,128)S(1)}, f32[8,640]{1,0:T(8,128)S(1)}, u32[]{:S(2)}, u32[]{:S(2)}) collective-permute-start(f32[8,640]{1,0:T(8,128)S(1)} %get-tuple-element.27), channel_id=1, source_target_pairs={{0,1},{1,0},{2,3},{3,2},{4,5},{5,4},{6,7},{7,6},{8,9},{9,8},{10,11... | collective-permute-start | bytes 61448 | tf_op jit(solution)/shard_map/ppermute | solution.py:457
  7.6 8.6 %collective-permute-start.1 = (f32[8,640]{1,0:T(8,128)S(1)}, f32[8,640]{1,0:T(8,128)S(1)}, u32[]{:S(2)}, u32[]{:S(2)}) collective-permute-start(f32[8,640]{1,0:T(8,128)S(1)} %get-tuple-element.28), channel_id=1, source_target_pairs={{0,2},{2,0},{4,6},{6,4},{8,10},{10,8},{12,14},{14,12},{16,18},{18,... | collective-permute-start | bytes 61448 | tf_op jit(solution)/shard_map/ppermute | solution.py:457
  8.4 7.9 %collective-permute-start.2 = (f32[8,640]{1,0:T(8,128)S(1)}, f32[8,640]{1,0:T(8,128)S(1)}, u32[]{:S(2)}, u32[]{:S(2)}) collective-permute-start(f32[8,640]{1,0:T(8,128)S(1)} %get-tuple-element.29), channel_id=1, source_target_pairs={{2,4},{4,2},{6,8},{8,6},{10,12},{12,10},{14,16},{16,14},{18,20},{2... | collective-permute-start | bytes 61448 | tf_op jit(solution)/shard_map/ppermute | solution.py:457
  18.5 31.2 %all-to-all-start = ((f32[16,128,128]{2,1,0:T(8,128)}), f32[16,128,128]{2,1,0:T(8,128)S(1)}, u32[]{:S(2)}, u32[]{:S(2)}) async-start(f32[16,128,128]{2,1,0:T(8,128)} %bitcast.9), calls=%async_computation | async-start | bytes 2097152 | tf_op jit(solution)/shard_map/all_to_all | solution.py:549
  26.8 19.8 %collective-permute-start.3 = (f32[8,640]{1,0:T(8,128)S(1)}, f32[8,640]{1,0:T(8,128)S(1)}, u32[]{:S(2)}, u32[]{:S(2)}) collective-permute-start(f32[8,640]{1,0:T(8,128)S(1)} %get-tuple-element.43), channel_id=1, source_target_pairs={{0,1},{1,0},{2,3},{3,2},{4,5},{5,4},{6,7},{7,6},{8,9},{9,8},{10,11... | collective-permute-start | bytes 61448 | tf_op jit(solution)/shard_map/ppermute | solution.py:457
  26.9 19.7 %collective-permute-start.4 = (f32[8,640]{1,0:T(8,128)S(1)}, f32[8,640]{1,0:T(8,128)S(1)}, u32[]{:S(2)}, u32[]{:S(2)}) collective-permute-start(f32[8,640]{1,0:T(8,128)S(1)} %get-tuple-element.44), channel_id=1, source_target_pairs={{0,2},{2,0},{4,6},{6,4},{8,10},{10,8},{12,14},{14,12},{16,18},{18,... | collective-permute-start | bytes 61448 | tf_op jit(solution)/shard_map/ppermute | solution.py:457
  27.6 21.4 %collective-permute-start.5 = (f32[8,640]{1,0:T(8,128)S(1)}, f32[8,640]{1,0:T(8,128)S(1)}, u32[]{:S(2)}, u32[]{:S(2)}) collective-permute-start(f32[8,640]{1,0:T(8,128)S(1)} %get-tuple-element.45), channel_id=1, source_target_pairs={{2,4},{4,2},{6,8},{8,6},{10,12},{12,10},{14,16},{16,14},{18,20},{2... | collective-permute-start | bytes 61448 | tf_op jit(solution)/shard_map/ppermute | solution.py:457

commit v4 on v3

--- a/solution.py
+++ b/solution.py
@@ -141,7 +141,7 @@
     far_ref[...] = jnp.where(odd_region, upper, lower)
 
 
-def arrived(place_ref, from_sub_ref, from_near_ref, from_far_ref):
+def arrived(place_ref, from_far_ref, from_sub_ref, from_near_ref):
     odd_region = place_ref[0] == 1
     odd_sub = place_ref[1] == 1
     from_sub, near, far = from_sub_ref[...], from_near_ref[...], from_far_ref[...]
@@ -159,9 +159,8 @@
 
 def lines_kernel(
     place_ref, nodes_hbm, admit_hbm, self_hbm, history_hbm, coupling_hbm, sources_hbm,
-    region_hbm, prior_hbm, old_hbm, table_hbm, turn_hbm,
     sub_ref, near_ref, far_ref, src_ref, term_ref, rows_ref, gathered_ref, inj_ref,
-    slot_ref, value_ref, self_ref, region_ref, prior_ref, old_ref, table_ref, turn_ref,
+    slot_ref, value_ref, self_ref,
     nodes_ref, admit_ref, history_ref, blocks, early_sem, src_sem, late_sem, block_sem,
 ):
     chunks = 2
@@ -188,19 +187,7 @@
     admit_copy = early(1, admit_hbm, admit_ref)
     self_copy = early(2, self_hbm, self_ref)
     history_copy = early(3, history_hbm, history_ref)
-    late_copies = [
-        pltpu.make_async_copy(source, target, late_sem.at[index])
-        for index, (source, target) in enumerate(
-            [
-                (coupling_hbm.at[0, pl.ds(0, TERM_DEV)], term_ref),
-                (region_hbm, region_ref),
-                (prior_hbm, prior_ref),
-                (old_hbm, old_ref),
-                (table_hbm, table_ref),
-                (turn_hbm, turn_ref),
-            ]
-        )
-    ]
+    term_copy = pltpu.make_async_copy(coupling_hbm.at[0, pl.ds(0, TERM_DEV)], term_ref, late_sem)
     nodes_copy.start()
     admit_copy.start()
     self_copy.start()
@@ -235,8 +222,7 @@
 
     for slot in range(LINES):
         block_copy(slot).wait()
-    for copy in late_copies:
-        copy.start()
+    term_copy.start()
     rows = dot(choose, blocks[...]).astype(BF16)
     rows_ref[...] = rows
     gathered = dot(rows, hot).astype(BF16)
@@ -251,19 +237,15 @@
         picked = picked + dot(left[:, span], src_ref[span, :COLS])
     volts = volts + picked[:LINES] + self_col * (picked[LINES:] + total.astype(F32))
     send_out(volts, lines, admit, down, place_ref, sub_ref, near_ref, far_ref)
-    for copy in late_copies:
-        copy.wait()
+    term_copy.wait()
 
 
 def terminals_kernel(
     capacity, slots,
     slot_ref, inj_ref, src_ref, term_ref, self_ref, region_ref, prior_ref, old_ref, table_ref, turn_ref,
-    sources_hbm,
+    sources_ref,
     packed_ref, left_ref,
-    later_ref, later_sem,
 ):
-    later_copy = pltpu.make_async_copy(sources_hbm.at[0, :, pl.ds(COLS, COLS)], later_ref, later_sem)
-    later_copy.start()
     down = slot_ref[:LINES, :1]
     along = slot_ref[LINES : LINES + 1, :]
     first = first_along(along, down)
@@ -284,33 +266,36 @@
     pack = jnp.where(iota((slots, TERM_DEV), 0) == dest, 1.0, 0.0).astype(BF16)
     left_ref[...] = dot(pack, small).astype(BF16)
 
-    doubled = jnp.concatenate([pack, pack], axis=1)
-
-    def put(span_index, running):
-        filled = dot(doubled, jnp.concatenate(split(running), axis=0))
-        for part in range(2):
-            packed_ref[pl.ds(2 * span_index + part, slots, stride=4), :] = filled[
-                :, part * LANES : (part + 1) * LANES
-            ]
-
+    later = dot(term_ref[...], sources_ref[0, :, COLS:])
+    later = later + term_self * sources_ref[0, :TERM_DEV, COLS:].astype(F32)
     running = jnp.concatenate(
         [prior_ref[pl.ds(part, TERM_DEV, stride=2), :] for part in range(2)], axis=1
     )
-    running = running + fit(volts - old_ref[:, :COLS].astype(F32), table_ref)
-    put(0, running)
-    later_copy.wait()
-    volts = dot(term_ref[...], later_ref[...]) + term_self * later_ref[:TERM_DEV, :].astype(F32)
-    put(1, running + turned(fit(volts - old_ref[:, COLS:].astype(F32), table_ref), turn_ref))
+    first = fit(volts - old_ref[:, :COLS].astype(F32), table_ref)
+    second = turned(fit(later - old_ref[:, COLS:].astype(F32), table_ref), turn_ref)
+    high, low = split(running + first)
+    later_high, later_low = split(running + first + second)
+    fitted = jnp.concatenate(
+        [
+            jnp.concatenate([high, later_high], axis=1),
+            jnp.concatenate([low, later_low], axis=1),
+        ],
+        axis=0,
+    )
+    filled = dot(jnp.concatenate([pack, pack], axis=1), fitted)
+    for part in range(4):
+        packed_ref[pl.ds(part, slots, stride=4), :] = filled[:, part * LANES : (part + 1) * LANES]
 
 
 def second_kernel(
     slots,
-    place_ref, slot_ref, from_sub_ref, from_near_ref, from_far_ref, left_ref, table_ref, turn_ref, packed_in_ref,
-    packed_ref,
+    place_ref, slot_ref, from_far_ref, from_sub_ref, from_near_ref, left_ref, table_ref, turn_ref, packed_in_ref,
+    packed_hbm,
+    packed_ref, sems,
 ):
     down = slot_ref[:LINES, :1]
     along = slot_ref[LINES : LINES + 1, :]
-    lines = arrived(place_ref, from_sub_ref, from_near_ref, from_far_ref)
+    lines = arrived(place_ref, from_far_ref, from_sub_ref, from_near_ref)
     _, injection = injected(lines, along, down)
     both = dot(injection, table_ref[...])
     high, low = split(turned(both[:, :PHASOR] + both[:, PHASOR:], turn_ref))
@@ -319,110 +304,114 @@
         jnp.concatenate([left, left], axis=1),
         jnp.concatenate([three_times(high), three_times(low)], axis=0),
     )
-    for row in range(2):
-        rows = pl.ds(row, slots, stride=4)
-        packed_ref[rows, :] = packed_in_ref[rows, :]
-    for part in range(2):
-        rows = pl.ds(2 + part, slots, stride=4)
-        packed_ref[rows, :] = packed_in_ref[rows, :] + change[:, part * LANES : (part + 1) * LANES]
+    chunks = 4
+    depth = slots // chunks
+
+    def send(chunk):
+        rows = pl.ds(chunk * depth * 4, depth * 4)
+        return pltpu.make_async_copy(packed_ref.at[rows], packed_hbm.at[rows], sems.at[chunk])
+
+    for chunk in range(chunks):
+        for part in range(4):
+            rows = pl.ds(chunk * depth * 4 + part, depth, stride=4)
+            values = packed_in_ref[rows, :]
+            if part >= 2:
+                values = values + change[
+                    chunk * depth : (chunk + 1) * depth, (part - 2) * LANES : (part - 1) * LANES
+                ]
+            packed_ref[rows, :] = values
+        send(chunk).start()
+    for chunk in range(chunks):
+        send(chunk).wait()
 
 
 def last_lines_kernel(
-    place_ref, slot_ref, value_ref, from_sub_ref, from_near_ref, from_far_ref,
-    rows_ref, gathered_ref, sources_hbm, started_ref,
-    sub_ref, near_ref, far_ref, inj_ref,
-    src_ref, sems,
+    place_ref, slot_ref, value_ref, from_far_ref, from_sub_ref, from_near_ref,
+    rows_ref, gathered_ref, inj0_ref, nodes_hbm, sources_hbm, coupling_hbm, started_ref,
+    sub_ref, near_ref, far_ref, drive_ref, head_ref,
+    nodes_ref, sems,
 ):
     del started_ref
-    chunks = 2
-    depth = NODES // chunks
+    nodes_copy = pltpu.make_async_copy(nodes_hbm, nodes_ref, sems.at[0])
+    head_copy = pltpu.make_async_copy(coupling_hbm.at[0, pl.ds(0, ROWS)], head_ref, sems.at[1])
     copies = [
         pltpu.make_async_copy(
-            sources_hbm.at[0, pl.ds(part * depth, depth), pl.ds(COLS, COLS)],
-            src_ref.at[pl.ds(part * depth, depth)],
-            sems.at[part],
+            sources_hbm.at[0, :, pl.ds(span * COLS, COLS)],
+            drive_ref.at[:, pl.ds(span * COLS, COLS)],
+            sems.at[2 + span],
         )
-        for part in range(chunks)
+        for span in range(SPANS)
     ]
-    for copy in copies:
-        copy.start()
+    nodes_copy.start()
+    copies[1].start()
+    copies[0].start()
+    head_copy.start()
     down = slot_ref[:LINES, :1]
     along = slot_ref[LINES : LINES + 1, :]
     admit, self_col = value_ref[:LINES, :1], value_ref[LINES:, :1]
-    lines = arrived(place_ref, from_sub_ref, from_near_ref, from_far_ref)
+    lines = arrived(place_ref, from_far_ref, from_sub_ref, from_near_ref)
     total, injection = injected(lines, along, down)
-    inj_ref[...] = injection
     own = jnp.where(iota((LINES, NODES), 1) == jnp.maximum(down, 0), 1.0, 0.0).astype(BF16)
     left = jnp.concatenate([rows_ref[...], own], axis=0)
     volts = dot(gathered_ref[:, :LINES], injection)
-    picked = jnp.zeros((2 * LINES, COLS), F32)
-    for part in range(chunks):
-        copies[part].wait()
-        span = slice(part * depth, (part + 1) * depth)
-        picked = picked + dot(left[:, span], src_ref[span, :])
+    nodes_copy.wait()
+    copies[1].wait()
+    picked = dot(left, drive_ref[:, COLS:])
     volts = volts + picked[:LINES] + self_col * (picked[LINES:] + total.astype(F32))
     send_out(volts, lines, admit, down, place_ref, sub_ref, near_ref, far_ref)
 
-
-def nodes_kernel(
-    inj0_ref, inj1_ref, self_ref, nodes_hbm, sources_hbm, coupling_hbm,
-    volts_hbm,
-    nodes_ref, drive_ref, matrix_buf, volts_buf, early_sem, in_sem, out_sem,
-):
-    blocks = NODES // ROWS
-
-    def load(block, place):
-        rows = pl.ds(pl.multiple_of(block * ROWS, ROWS), ROWS)
-        return pltpu.make_async_copy(coupling_hbm.at[0, rows], matrix_buf.at[place], in_sem.at[place])
-
-    def store(block, place):
-        rows = pl.ds(pl.multiple_of(block * ROWS, ROWS), ROWS)
-        return pltpu.make_async_copy(volts_buf.at[place], volts_hbm.at[0, rows], out_sem.at[place])
-
-    nodes_copy = pltpu.make_async_copy(nodes_hbm, nodes_ref, early_sem.at[0])
-    drive_copy = pltpu.make_async_copy(sources_hbm.at[0], drive_ref, early_sem.at[1])
-    nodes_copy.start()
-    drive_copy.start()
-    load(0, 0).start()
-    nodes_copy.wait()
-    drive_copy.wait()
-
-    both = jnp.concatenate([inj0_ref[...], inj1_ref[...]], axis=1).astype(F32)
+    copies[0].wait()
+    both = jnp.concatenate([inj0_ref[...], injection], axis=1).astype(F32)
     for slot in range(LINES):
         node = jnp.maximum(nodes_ref[0, slot // LPP, slot % LPP], 0)
         rows = pl.ds(pl.multiple_of((node // 16) * 16, 16), 16)
         extra = jnp.where(iota((16, 1), 0) == node % 16, both[slot : slot + 1, :], 0.0)
         drive_ref[rows, :] = (drive_ref[rows, :].astype(F32) + extra).astype(BF16)
-
-    @pl.loop(0, blocks)
-    def _(block):
-        place = lax.rem(block, 2)
-
-        @pl.when(block + 1 < blocks)
-        def _():
-            load(block + 1, 1 - place).start()
-
-        load(block, place).wait()
-
-        @pl.when(block >= 2)
-        def _():
-            store(block - 2, place).wait()
-
-        start = pl.multiple_of(block * ROWS, ROWS)
+    head_copy.wait()
+
+
+def nodes_kernel(
+    drive_ref, head_ref, self_ref, coupling_hbm,
+    volts_hbm,
+    matrix_buf, volts_buf, in_sem, out_sem,
+):
+    blocks = NODES // ROWS
+
+    def load(block):
+        place = block % 2
+        return pltpu.make_async_copy(
+            coupling_hbm.at[0, pl.ds(block * ROWS, ROWS)], matrix_buf.at[place], in_sem.at[place]
+        )
+
+    def store(block):
+        place = block % 2
+        return pltpu.make_async_copy(
+            volts_buf.at[place], volts_hbm.at[0, pl.ds(block * ROWS, ROWS)], out_sem.at[place]
+        )
+
+    load(1).start()
+    for block in range(blocks):
+        if 0 < block:
+            load(block).wait()
+        if 0 < block < blocks - 1:
+            load(block + 1).start()
+        if block >= 2:
+            store(block - 2).wait()
+        span = slice(block * ROWS, (block + 1) * ROWS)
         block_self = jnp.concatenate(
             [
-                column_of(self_ref[:, pl.ds(pl.multiple_of(start + part, 256), 256)])
-                for part in range(0, ROWS, 256)
+                column_of(self_ref[:, start : start + 256])
+                for start in range(block * ROWS, (block + 1) * ROWS, 256)
             ],
             axis=0,
         )
-        result = dot(matrix_buf[place], drive_ref[...])
-        result = result + block_self * drive_ref[pl.ds(start, ROWS), :].astype(F32)
-        volts_buf[place] = result.astype(BF16)
-        store(block, place).start()
-
+        matrix = head_ref[...] if block == 0 else matrix_buf[block % 2]
+        result = dot(matrix, drive_ref[...])
+        result = result + block_self * drive_ref[span, :].astype(F32)
+        volts_buf[block % 2] = result.astype(BF16)
+        store(block).start()
     for block in range(blocks - 2, blocks):
-        store(block, block % 2).wait()
+        store(block).wait()
 
 
 VM = pl.BlockSpec(memory_space=pltpu.VMEM)
@@ -484,10 +473,7 @@
     injection = struct((LINES, COLS), BF16)
     DMA = pltpu.SemaphoreType.DMA
 
-    (
-        sub, near, far, src, term, rows, gathered, inj0, slot, value, self_row,
-        region, prior, old, table, turn,
-    ) = pl.pallas_call(
+    (sub, near, far, src, term, rows, gathered, inj0, slot, value, self_row) = pl.pallas_call(
         lines_kernel,
         out_shape=[
             block, block, block,
@@ -499,52 +485,44 @@
             struct((LINES + 8, LANES), jnp.int32),
             struct((2 * LINES, LANES), F32),
             struct((1, NODES), F32),
-            struct((1, TERM_DEV), jnp.int32),
-            struct((TERM_DEV * 2, LANES), F32),
-            struct((TERM_DEV, SPANS * COLS), BF16),
-            struct((COLS, 2 * PHASOR), BF16),
-            struct((8, LANES), F32),
         ],
-        in_specs=[SM] + [HB] * 11,
-        out_specs=[VM] * 16,
+        in_specs=[SM] + [HB] * 6,
+        out_specs=[VM] * 11,
         scratch_shapes=[
             pltpu.SMEM((1, NEIGH, LPP), jnp.int32),
             pltpu.SMEM((1, NEIGH, LPP), F32),
             pltpu.VMEM((1, NEIGH, LPP, COLS), F32),
             pltpu.VMEM((LINES * 16, NODES), BF16),
-            DMA((4,)), DMA((2,)), DMA((6,)), DMA((LINES,)),
+            DMA((4,)), DMA((2,)), DMA, DMA((LINES,)),
         ],
         compiler_params=params(),
         name="lines",
-    )(
-        place,
-        *in_hbm(
-            line_nodes, line_admit, self_term, history, coupling, sources,
-            term_region.reshape(1, TERM_DEV), prior_phasor.reshape(TERM_DEV * 2, LANES), old_samples,
-            jnp.asarray(fit_table()), jnp.asarray(span_turn()),
-        ),
-    )
+    )(place, *in_hbm(line_nodes, line_admit, self_term, history, coupling, sources))
+    region = term_region.reshape(1, TERM_DEV)
+    prior = prior_phasor.reshape(TERM_DEV * 2, LANES)
+    table = jnp.asarray(fit_table())
+    turn = jnp.asarray(span_turn())
 
     from_near, from_sub, from_far = exchange(sub, near, far)
 
     packed, left = pl.pallas_call(
         functools.partial(terminals_kernel, capacity, slots),
         out_shape=[struct((slots * 4, LANES), F32), struct((slots, LANES), BF16)],
-        in_specs=[VM] * 10 + [HB],
+        in_specs=[VM] * 11,
         out_specs=[VM] * 2,
-        scratch_shapes=[pltpu.VMEM((NODES, COLS), BF16), DMA],
         compiler_params=params(),
         name="terminals",
-    )(slot, inj0, src, term, self_row, region, prior, old, table, turn, *in_hbm(sources))
+    )(slot, inj0, src, term, self_row, region, prior, old_samples, table, turn, sources)
 
     packed = pl.pallas_call(
         functools.partial(second_kernel, slots),
         out_shape=struct((slots * 4, LANES), F32),
         in_specs=[SM] + [VM] * 8,
-        out_specs=VM,
+        out_specs=HB,
+        scratch_shapes=[pltpu.VMEM((slots * 4, LANES), F32), DMA((4,))],
         compiler_params=params(),
         name="second",
-    )(place, slot, from_sub, from_near, from_far, left, table, turn, packed)
+    )(place, slot, from_far, from_sub, from_near, left, table, turn, packed)
 
     result = lax.all_to_all(
         packed.reshape(region_count, capacity * 4, LANES),
@@ -555,17 +533,19 @@
     )
     phasors = result.reshape(slots, SPANS, 2, LANES)
 
-    sub, near, far, inj1 = pl.pallas_call(
+    sub, near, far, drive, head = pl.pallas_call(
         last_lines_kernel,
-        out_shape=[block, block, block, injection],
-        in_specs=[SM] + [VM] * 7 + [HB, pl.BlockSpec(memory_space=pl.ANY)],
-        out_specs=[VM] * 4,
-        scratch_shapes=[pltpu.VMEM((NODES, COLS), BF16), DMA((2,))],
+        out_shape=[
+            block, block, block, struct((NODES, SPANS * COLS), BF16), struct((ROWS, NODES), BF16)
+        ],
+        in_specs=[SM] + [VM] * 8 + [HB] * 3 + [pl.BlockSpec(memory_space=pl.ANY)],
+        out_specs=[VM] * 5,
+        scratch_shapes=[pltpu.SMEM((1, NEIGH, LPP), jnp.int32), DMA((4,))],
         compiler_params=params(),
         name="last_lines",
     )(
-        place, slot, value, from_sub, from_near, from_far, rows, gathered,
-        *in_hbm(sources), packed,
+        place, slot, value, from_far, from_sub, from_near, rows, gathered, inj0,
+        *in_hbm(line_nodes, sources, coupling), packed,
     )
 
     from_near, from_sub, from_far = exchange(sub, near, far)
@@ -583,21 +563,19 @@
     node_voltages = pl.pallas_call(
         nodes_kernel,
         out_shape=struct((1, NODES, SPANS * COLS), BF16),
-        in_specs=[VM] * 3 + [HB] * 3,
+        in_specs=[VM] * 3 + [HB],
         out_specs=HB,
         scratch_shapes=[
-            pltpu.SMEM((1, NEIGH, LPP), jnp.int32),
-            pltpu.VMEM((NODES, SPANS * COLS), BF16),
             pltpu.VMEM((2, ROWS, NODES), BF16),
             pltpu.VMEM((2, ROWS, SPANS * COLS), BF16),
-            DMA((2,)), DMA((2,)), DMA((2,)),
+            DMA((2,)), DMA((2,)),
         ],
         compiler_params=params(),
         cost_estimate=pl.CostEstimate(
             flops=2 * NODES * NODES * SPANS * COLS, bytes_accessed=20_000_000, transcendentals=0
         ),
         name="nodes",
-    )(inj0, inj1, self_row, *in_hbm(line_nodes, sources, coupling))
+    )(drive, head, self_row, *in_hbm(coupling))
     return (next_history, node_voltages, phasors)
 
 

time: 50.9 us -> 49.5 us (0.972)
  Pallas kernels: 31.4 us -> 29.7 us
    pallas_call x1, Pallas kernels: 16 us -> 14.8 us  [body(): pl.pallas_call(nodes_kernel, out_shape=struct((1, NODES, SPANS * COLS), B...]
    pallas_call x1, Pallas kernels: 2.89 us -> 3.76 us  [body(): pl.pallas_call(last_lines_kernel, out_shape=[block, block, block, struct(...]
    pallas_call x1, Pallas kernels: 4.46 us -> 3.67 us  [body(): pl.pallas_call(functools.partial(terminals_kernel, capacity, slots), out_...]
  transfers between devices with their start and end apart: 7 -> 7, of which waited for: 1 -> 1; matrix products, arithmetic and copies ran while one was open for 1% -> 1% of each run, Pallas kernels for 46% -> 45%
where the time goes in v4:
time: 49.5 us; the launch traced here: 49.2 us
  Pallas kernels  29.7 us (60%)
  starting transfers between devices  14.4 us (29%)
  waiting for transfers between devices  2.59 us (5%)
  local copies, waits for them, and re-layouts  1 us (2%)
  between operations  0.81 us (2%)
  other arithmetic  0.73 us (1%)
    pallas_call x1, Pallas kernels, body(): pl.pallas_call(nodes_kernel, out_shape=struct((1, NODES, SPANS * COLS), B...  14.8 us
    ppermute x6, starting transfers between devices, swap(): return lax.ppermute(block, axis, pairs)  9.02 us
    all_to_all x1, starting transfers between devices, body(): lax.all_to_all(packed.reshape(region_count, capacity * 4, LANES), 'region...  5.39 us
    pallas_call x1, Pallas kernels, body(): pl.pallas_call(lines_kernel, out_shape=[block, block, block, struct((NODE...  5.28 us
    pallas_call x1, Pallas kernels, body(): pl.pallas_call(last_lines_kernel, out_shape=[block, block, block, struct(...  3.76 us
    pallas_call x1, Pallas kernels, body(): pl.pallas_call(functools.partial(terminals_kernel, capacity, slots), out_...  3.67 us
    ppermute x6, waiting for transfers between devices, swap(): return lax.ppermute(block, axis, pairs)  2.58 us
    pallas_call x1, Pallas kernels, body(): pl.pallas_call(functools.partial(second_kernel, slots), out_shape=struct(...  2.2 us
  transfers between devices with their start and end apart: 7, of which 1 were waited for; matrix products, arithmetic and copies ran while one was open for 1% of the time, Pallas kernels for 45%

profile of v4, /device:TPU:13, one launch (start us, length us, event | category | flops | bytes accessed | tf_op | source)
XLA Modules:
  0.0 49.2 jit_solution(6949274840832086041)
XLA Ops:
  0.6 0.1 pad_add_fusion.place_ref
  0.7 0.0 copy-start
  0.7 0.0 copy-start.1
  0.7 0.0 copy-start.4
  0.7 0.0 copy-start.5
  0.8 5.3 %lines.1 = (f32[8,640]{1,0:T(8,128)S(1)}, f32[8,640]{1,0:T(8,128)S(1)}, f32[8,640]{1,0:T(8,128)S(1)}, bf16[2048,768]{1,0:T(8,128)(2,1)S(1)}, bf16[256,2048]{1,0:...) custom-call(s32[2]{0:T(128)S(1)} %pad_add_fusion.place_ref, ...), custom_call_target="tpu_custom_call" | custom-call | tf_op jit(solution)/shard_map/lines/pallas_call | solution.py:476
  6.0 3.7 %collective-permute-start = (f32[8,640]{1,0:T(8,128)S(1)}, f32[8,640]{1,0:T(8,128)S(1)}, u32[]{:S(2)}, u32[]{:S(2)}) collective-permute-start(f32[8,640]{1,0:T(8,128)S(1)} %get-tuple-element.23), channel_id=1, source_target_pairs={{2,4},{4,2},{6,8},{8,6},{10,12},{12,10},{14,16},{16,14},{18,20},{2... | collective-permute-start | bytes 61448 | tf_op jit(solution)/shard_map/ppermute | solution.py:446
  9.8 1.4 %collective-permute-start.1 = (f32[8,640]{1,0:T(8,128)S(1)}, f32[8,640]{1,0:T(8,128)S(1)}, u32[]{:S(2)}, u32[]{:S(2)}) collective-permute-start(f32[8,640]{1,0:T(8,128)S(1)} %get-tuple-element.24), channel_id=1, source_target_pairs={{0,1},{1,0},{2,3},{3,2},{4,5},{5,4},{6,7},{7,6},{8,9},{9,8},{10,11... | collective-permute-start | bytes 61448 | tf_op jit(solution)/shard_map/ppermute | solution.py:446
  11.2 0.0 collective-permute-start.2
  11.2 0.0 copy-done
  11.2 0.0 copy-done.1
  11.2 0.0 copy-done.2
  11.2 0.0 copy-done.3
  11.2 0.0 copy-done.4
  11.2 0.0 copy-done.5
  11.2 3.7 %terminals.1 = (f32[2048,128]{1,0:T(8,128)S(1)}, bf16[512,128]{1,0:T(8,128)(2,1)S(1)}) custom-call(s32[40,128]{1,0:T(8,128)S(1)} %get-tuple-element.21.slot_ref, bf16[32,640]{1,0:T(8,128)(2,1)S(1)} %get-tuple-element.28.inj_ref.inj0_ref, bf16[2048,768]{1,0:T(8,128)(2,1)S(1)} %get-tuple-element.29.src_ref, bf16[256,2048]{1,0:T(8,128)(2,1)S(1)} %get-tuple-element.30.term_ref, ...), custom_call_target="tpu_custom_call" | custom-call | tf_op jit(solution)/shard_map/terminals/pallas_call | solution.py:508
  14.9 0.0 collective-permute-done.from_far_ref
  14.9 0.0 collective-permute-done.1.from_sub_ref
  14.9 0.0 collective-permute-done.2.from_near_ref
  14.9 2.2 %second.1.started_ref = f32[2048,128]{1,0:T(8,128)} custom-call(s32[2]{0:T(128)S(1)} %pad_add_fusion.place_ref, s32[40,128]{1,0:T(8,128)S(1)} %get-tuple-element.21.slot_ref, f32[8,640]{1,0:T(8,128)S(1)} %collective-permute-done.from_far_ref, f32[8,640]{1,0:T(8,128)S(1)} %collective-permute-done.1.from_sub_ref, ...), custom_call_target="tpu_custom_call" | custom-call | tf_op jit(solution)/shard_map/second/pallas_call | solution.py:517
  17.1 5.4 %all-to-all-start = ((f32[16,128,128]{2,1,0:T(8,128)}), f32[16,128,128]{2,1,0:T(8,128)S(1)}, u32[]{:S(2)}, u32[]{:S(2)}) async-start(f32[16,128,128]{2,1,0:T(8,128)} %bitcast.9), calls=%async_computation | async-start | bytes 2097152 | tf_op jit(solution)/shard_map/all_to_all | solution.py:527
  22.5 3.8 %last_lines.1 = (f32[8,640]{1,0:T(8,128)S(1)}, f32[8,640]{1,0:T(8,128)S(1)}, f32[8,640]{1,0:T(8,128)S(1)}, bf16[2048,1280]{1,0:T(8,128)(2,1)S(1)}, bf16[512,2048]{1,0:T(8,128)(2,1)S(1)}) custom-call(s32[2]{0:T(128)S(1)} %pad_add_fusion.place_ref, s32[40,128]{1,0:T(8,128)S(1)} %get-tuple-element.21.slot_ref, f32[64,128]{1,0:T(8,128)S(1)} %get-tuple-element.22.value_ref, ...), custom_call_target="tpu_custom_call" | custom-call | tf_op jit(solution)/shard_map/last_lines/pallas_call | solution.py:536
  26.3 0.4 collective-permute-start.4
  26.7 3.3 %collective-permute-start.5 = (f32[8,640]{1,0:T(8,128)S(1)}, f32[8,640]{1,0:T(8,128)S(1)}, u32[]{:S(2)}, u32[]{:S(2)}) collective-permute-start(f32[8,640]{1,0:T(8,128)S(1)} %get-tuple-element.36), channel_id=1, source_target_pairs={{2,4},{4,2},{6,8},{8,6},{10,12},{12,10},{14,16},{16,14},{18,20},{2... | collective-permute-start | bytes 61448 | tf_op jit(solution)/shard_map/ppermute | solution.py:446
  30.0 0.2 collective-permute-start.3
  30.2 14.8 %nodes.1 = bf16[1,2048,1280]{2,1,0:T(8,128)(2,1)} custom-call(bf16[2048,1280]{1,0:T(8,128)(2,1)S(1)} %get-tuple-element.37.drive_ref, bf16[512,2048]{1,0:T(8,128)(2,1)S(1)} %get-tuple-element.38.head_ref, f32[1,2048]{1,0:T(1,128)S(1)} %get-tuple-element.31.self_ref, bf16[1,2048,2048]{2,1,0:T(8,128)(2,1)} %coupling_hbm.5), custom_call_target="tpu_custom_call" | custom-call | flops 10737418240 | bytes 20000000 | tf_op jit(solution)/shard_map/nodes/pallas_call | solution.py:563
  45.0 0.0 collective-permute-done.3
  45.0 0.0 collective-permute-done.4
  45.0 2.6 %collective-permute-done.5 = f32[8,640]{1,0:T(8,128)S(1)} collective-permute-done((f32[8,640]{1,0:T(8,128)S(1)}, f32[8,640]{1,0:T(8,128)S(1)}, u32[]{:S(2)}, u32[]{:S(2)}) %collective-permute-start.5) | collective-permute-done | bytes 20512 | tf_op jit(solution)/shard_map/ppermute | solution.py:446
  47.6 0.6 %maximum_bitcast_fusion = f32[1,4,8,640]{3,2,1,0:T(8,128)} fusion(f32[1,8,640]{2,1,0:T(8,128)S(1)} %get-tuple-element.40, f32[1,8,640]{2,1,0:T(8,128)S(1)} %get-tuple-element.39, f32[1,8,640]{2,1,0:T(8,128)S(1)} %get-tuple-element.42, f32[1,8,640]{2,1,0:T(8,128)S(1)} %get-tuple-element.41), kind=kLoop, calls=%fused_computation | loop fusion | flops 61440 | bytes 163840 | tf_op jit(solution)/shard_map/broadcast_in_dim | solution.py:553
  48.2 0.0 all-to-all-done
  48.2 1.0 %copy.15 = f32[512,2,2,128]{3,2,1,0:T(2,128)} copy(f32[512,2,2,128]{3,2,1,0:T(2,128)S(1)} %bitcast.18) | data formatting | bytes 2097152
  (4 shorter events, 0.0 us)
Async XLA Ops:
  0.7 10.4 %copy-start = (bf16[1,2048,1280]{2,1,0:T(8,128)(2,1)S(1)}, bf16[1,2048,1280]{2,1,0:T(8,128)(2,1)}, u32[]{:S(2)}) copy-start(bf16[1,2048,1280]{2,1,0:T(8,128)(2,1)} %sources_hbm.3) | copy-start | bytes 15728644
  0.7 10.4 %copy-start.1 = (bf16[640,512]{1,0:T(8,128)(2,1)S(1)}, bf16[640,512]{1,0:T(8,128)(2,1)}, u32[]{:S(2)}) copy-start(bf16[640,512]{1,0:T(8,128)(2,1)} %constant.32.clone.table_ref) | copy-start | bytes 1966084
  0.7 10.4 %copy-start.2 = (bf16[256,1280]{1,0:T(8,128)(2,1)S(1)}, bf16[256,1280]{1,0:T(8,128)(2,1)}, u32[]{:S(2)}) copy-start(bf16[256,1280]{1,0:T(8,128)(2,1)} %old_ref.1) | copy-start | bytes 1966084
  0.7 10.4 %copy-start.3 = (f32[256,2,128]{2,1,0:T(2,128)S(1)}, f32[256,2,128]{2,1,0:T(2,128)}, u32[]{:S(2)}) copy-start(f32[256,2,128]{2,1,0:T(2,128)} %param.19) | copy-start | bytes 786436
  0.7 10.4 %copy-start.4 = (f32[8,128]{1,0:T(8,128)S(1)}, f32[8,128]{1,0:T(8,128)}, u32[]{:S(2)}) copy-start(f32[8,128]{1,0:T(8,128)} %constant.33.clone.turn_ref) | copy-start | bytes 12292
  0.7 10.4 %copy-start.5 = (s32[256,1]{0,1:T(1,128)S(1)}, s32[256,1]{0,1:T(1,128)}, u32[]{:S(2)}) copy-start(s32[256,1]{0,1:T(1,128)} %param.17) | copy-start | bytes 3076
  6.0 8.8 %collective-permute-start = (f32[8,640]{1,0:T(8,128)S(1)}, f32[8,640]{1,0:T(8,128)S(1)}, u32[]{:S(2)}, u32[]{:S(2)}) collective-permute-start(f32[8,640]{1,0:T(8,128)S(1)} %get-tuple-element.23), channel_id=1, source_target_pairs={{2,4},{4,2},{6,8},{8,6},{10,12},{12,10},{14,16},{16,14},{18,20},{2... | collective-permute-start | bytes 61448 | tf_op jit(solution)/shard_map/ppermute | solution.py:446
  9.8 5.1 %collective-permute-start.1 = (f32[8,640]{1,0:T(8,128)S(1)}, f32[8,640]{1,0:T(8,128)S(1)}, u32[]{:S(2)}, u32[]{:S(2)}) collective-permute-start(f32[8,640]{1,0:T(8,128)S(1)} %get-tuple-element.24), channel_id=1, source_target_pairs={{0,1},{1,0},{2,3},{3,2},{4,5},{5,4},{6,7},{7,6},{8,9},{9,8},{10,11... | collective-permute-start | bytes 61448 | tf_op jit(solution)/shard_map/ppermute | solution.py:446
  11.2 3.8 %collective-permute-start.2 = (f32[8,640]{1,0:T(8,128)S(1)}, f32[8,640]{1,0:T(8,128)S(1)}, u32[]{:S(2)}, u32[]{:S(2)}) collective-permute-start(f32[8,640]{1,0:T(8,128)S(1)} %get-tuple-element.25), channel_id=1, source_target_pairs={{0,2},{2,0},{4,6},{6,4},{8,10},{10,8},{12,14},{14,12},{16,18},{18,... | collective-permute-start | bytes 61448 | tf_op jit(solution)/shard_map/ppermute | solution.py:446
  17.1 31.1 %all-to-all-start = ((f32[16,128,128]{2,1,0:T(8,128)}), f32[16,128,128]{2,1,0:T(8,128)S(1)}, u32[]{:S(2)}, u32[]{:S(2)}) async-start(f32[16,128,128]{2,1,0:T(8,128)} %bitcast.9), calls=%async_computation | async-start | bytes 2097152 | tf_op jit(solution)/shard_map/all_to_all | solution.py:527
  26.3 18.7 %collective-permute-start.4 = (f32[8,640]{1,0:T(8,128)S(1)}, f32[8,640]{1,0:T(8,128)S(1)}, u32[]{:S(2)}, u32[]{:S(2)}) collective-permute-start(f32[8,640]{1,0:T(8,128)S(1)} %get-tuple-element.35), channel_id=1, source_target_pairs={{0,2},{2,0},{4,6},{6,4},{8,10},{10,8},{12,14},{14,12},{16,18},{18,... | collective-permute-start | bytes 61448 | tf_op jit(solution)/shard_map/ppermute | solution.py:446
  26.7 20.9 %collective-permute-start.5 = (f32[8,640]{1,0:T(8,128)S(1)}, f32[8,640]{1,0:T(8,128)S(1)}, u32[]{:S(2)}, u32[]{:S(2)}) collective-permute-start(f32[8,640]{1,0:T(8,128)S(1)} %get-tuple-element.36), channel_id=1, source_target_pairs={{2,4},{4,2},{6,8},{8,6},{10,12},{12,10},{14,16},{16,14},{18,20},{2... | collective-permute-start | bytes 61448 | tf_op jit(solution)/shard_map/ppermute | solution.py:446
  30.0 15.0 %collective-permute-start.3 = (f32[8,640]{1,0:T(8,128)S(1)}, f32[8,640]{1,0:T(8,128)S(1)}, u32[]{:S(2)}, u32[]{:S(2)}) collective-permute-start(f32[8,640]{1,0:T(8,128)S(1)} %get-tuple-element.34), channel_id=1, source_target_pairs={{0,1},{1,0},{2,3},{3,2},{4,5},{5,4},{6,7},{7,6},{8,9},{9,8},{10,11... | collective-permute-start | bytes 61448 | tf_op jit(solution)/shard_map/ppermute | solution.py:446

commit v5 on v4

--- a/solution.py
+++ b/solution.py
@@ -159,9 +159,9 @@
 
 def lines_kernel(
     place_ref, nodes_hbm, admit_hbm, self_hbm, history_hbm, coupling_hbm, sources_hbm,
-    sub_ref, near_ref, far_ref, src_ref, term_ref, rows_ref, gathered_ref, inj_ref,
+    sub_ref, near_ref, far_ref, hot_ref, term_ref, rows_ref, gathered_ref, inj_ref,
     slot_ref, value_ref, self_ref,
-    nodes_ref, admit_ref, history_ref, blocks, early_sem, src_sem, late_sem, block_sem,
+    src_ref, nodes_ref, admit_ref, history_ref, blocks, early_sem, src_sem, late_sem, block_sem,
 ):
     chunks = 2
     depth = NODES // chunks
@@ -173,7 +173,7 @@
     def src_copy(part):
         rows = pl.ds(part * depth, depth)
         return pltpu.make_async_copy(
-            sources_hbm.at[0, rows, first_cols], src_ref.at[rows, first_cols], src_sem.at[part]
+            sources_hbm.at[0, rows, first_cols], src_ref.at[rows], src_sem.at[part]
         )
 
     def block_copy(slot):
@@ -214,7 +214,7 @@
     self_col = jnp.sum(jnp.where(own_row, self_ref[...], 0.0), axis=1, keepdims=True)
     wanted = jnp.where(iota((1, LANES), 1) < LINES, along, -1)
     hot = jnp.where(iota((NODES, LANES), 0) == wanted, 1.0, 0.0).astype(BF16)
-    src_ref[:, COLS:] = hot
+    hot_ref[...] = hot
     slot_ref[:LINES, :] = jnp.broadcast_to(down, (LINES, LANES))
     slot_ref[LINES:, :] = jnp.broadcast_to(along, (8, LANES))
     value_ref[:LINES, :] = jnp.broadcast_to(admit, (LINES, LANES))
@@ -234,7 +234,7 @@
     picked = jnp.zeros((2 * LINES, COLS), F32)
     for part in range(chunks):
         span = slice(part * depth, (part + 1) * depth)
-        picked = picked + dot(left[:, span], src_ref[span, :COLS])
+        picked = picked + dot(left[:, span], src_ref[span, :])
     volts = volts + picked[:LINES] + self_col * (picked[LINES:] + total.astype(F32))
     send_out(volts, lines, admit, down, place_ref, sub_ref, near_ref, far_ref)
     term_copy.wait()
@@ -242,7 +242,7 @@
 
 def terminals_kernel(
     capacity, slots,
-    slot_ref, inj_ref, src_ref, term_ref, self_ref, region_ref, prior_ref, old_ref, table_ref, turn_ref,
+    slot_ref, inj_ref, hot_ref, term_ref, self_ref, region_ref, prior_ref, old_ref, table_ref, turn_ref,
     sources_ref,
     packed_ref, left_ref,
 ):
@@ -251,10 +251,10 @@
     first = first_along(along, down)
     term_self = column_of(self_ref[:, :TERM_DEV])
 
-    products = dot(term_ref[...], src_ref[...])
-    small = small_left(products[:, COLS:], term_self, along, first, 0)
-    volts = products[:, :COLS] + term_self * src_ref[:TERM_DEV, :COLS].astype(F32)
-    volts = volts + dot(small, three_times(inj_ref[...]))
+    products = dot(term_ref[...], sources_ref[0])
+    products = products + term_self * sources_ref[0, :TERM_DEV, :].astype(F32)
+    small = small_left(dot(term_ref[...], hot_ref[...]), term_self, along, first, 0)
+    volts = products[:, :COLS] + dot(small, three_times(inj_ref[...]))
 
     region_row = region_ref[...]
     region_col = column_of(region_row.astype(F32)).astype(jnp.int32)
@@ -266,8 +266,7 @@
     pack = jnp.where(iota((slots, TERM_DEV), 0) == dest, 1.0, 0.0).astype(BF16)
     left_ref[...] = dot(pack, small).astype(BF16)
 
-    later = dot(term_ref[...], sources_ref[0, :, COLS:])
-    later = later + term_self * sources_ref[0, :TERM_DEV, COLS:].astype(F32)
+    later = products[:, COLS:]
     running = jnp.concatenate(
         [prior_ref[pl.ds(part, TERM_DEV, stride=2), :] for part in range(2)], axis=1
     )
@@ -473,11 +472,11 @@
     injection = struct((LINES, COLS), BF16)
     DMA = pltpu.SemaphoreType.DMA
 
-    (sub, near, far, src, term, rows, gathered, inj0, slot, value, self_row) = pl.pallas_call(
+    (sub, near, far, hot, term, rows, gathered, inj0, slot, value, self_row) = pl.pallas_call(
         lines_kernel,
         out_shape=[
             block, block, block,
-            struct((NODES, COLS + LANES), BF16),
+            struct((NODES, LANES), BF16),
             struct((TERM_DEV, NODES), BF16),
             struct((LINES, NODES), BF16),
             struct((LINES, LANES), BF16),
@@ -489,6 +488,7 @@
         in_specs=[SM] + [HB] * 6,
         out_specs=[VM] * 11,
         scratch_shapes=[
+            pltpu.VMEM((NODES, COLS), BF16),
             pltpu.SMEM((1, NEIGH, LPP), jnp.int32),
             pltpu.SMEM((1, NEIGH, LPP), F32),
             pltpu.VMEM((1, NEIGH, LPP, COLS), F32),
@@ -512,7 +512,7 @@
         out_specs=[VM] * 2,
         compiler_params=params(),
         name="terminals",
-    )(slot, inj0, src, term, self_row, region, prior, old_samples, table, turn, sources)
+    )(slot, inj0, hot, term, self_row, region, prior, old_samples, table, turn, sources)
 
     packed = pl.pallas_call(
         functools.partial(second_kernel, slots),

time: 49.5 us -> 49 us (0.990)
  Pallas kernels: 29.7 us -> 29.1 us
    pallas_call x1, Pallas kernels: 3.67 us -> 3.16 us  [body(): pl.pallas_call(functools.partial(terminals_kernel, capacity, slots), out_...]
where the time goes in v5:
time: 49 us; the launch traced here: 48.6 us
  Pallas kernels  29.1 us (59%)
  starting transfers between devices  14.6 us (30%)
  waiting for transfers between devices  2.41 us (5%)
  local copies, waits for them, and re-layouts  1 us (2%)
  between operations  0.81 us (2%)
  other arithmetic  0.73 us (1%)
    pallas_call x1, Pallas kernels, body(): pl.pallas_call(nodes_kernel, out_shape=struct((1, NODES, SPANS * COLS), B...  14.8 us
    ppermute x6, starting transfers between devices, swap(): return lax.ppermute(block, axis, pairs)  9.14 us
    all_to_all x1, starting transfers between devices, body(): lax.all_to_all(packed.reshape(region_count, capacity * 4, LANES), 'region...  5.42 us
    pallas_call x1, Pallas kernels, body(): pl.pallas_call(lines_kernel, out_shape=[block, block, block, struct((NODE...  5.23 us
    pallas_call x1, Pallas kernels, body(): pl.pallas_call(last_lines_kernel, out_shape=[block, block, block, struct(...  3.76 us
    pallas_call x1, Pallas kernels, body(): pl.pallas_call(functools.partial(terminals_kernel, capacity, slots), out_...  3.16 us
    ppermute x6, waiting for transfers between devices, swap(): return lax.ppermute(block, axis, pairs)  2.4 us
    pallas_call x1, Pallas kernels, body(): pl.pallas_call(functools.partial(second_kernel, slots), out_shape=struct(...  2.2 us
  transfers between devices with their start and end apart: 7, of which 1 were waited for; matrix products, arithmetic and copies ran while one was open for 1% of the time, Pallas kernels for 45%

profile of v5, /device:TPU:13, one launch (start us, length us, event | category | flops | bytes accessed | tf_op | source)
XLA Modules:
  0.0 48.6 jit_solution(2678596990687980767)
XLA Ops:
  0.6 0.1 pad_add_fusion.place_ref
  0.7 0.0 copy-start
  0.7 0.0 copy-start.1
  0.7 0.0 copy-start.4
  0.7 0.0 copy-start.5
  0.8 5.2 %lines.1 = (f32[8,640]{1,0:T(8,128)S(1)}, f32[8,640]{1,0:T(8,128)S(1)}, f32[8,640]{1,0:T(8,128)S(1)}, bf16[2048,128]{1,0:T(8,128)(2,1)S(1)}, bf16[256,2048]{1,0:...) custom-call(s32[2]{0:T(128)S(1)} %pad_add_fusion.place_ref, ...), custom_call_target="tpu_custom_call" | custom-call | tf_op jit(solution)/shard_map/lines/pallas_call | solution.py:475
  6.0 3.7 %collective-permute-start = (f32[8,640]{1,0:T(8,128)S(1)}, f32[8,640]{1,0:T(8,128)S(1)}, u32[]{:S(2)}, u32[]{:S(2)}) collective-permute-start(f32[8,640]{1,0:T(8,128)S(1)} %get-tuple-element.23), channel_id=1, source_target_pairs={{2,4},{4,2},{6,8},{8,6},{10,12},{12,10},{14,16},{16,14},{18,20},{2... | collective-permute-start | bytes 61448 | tf_op jit(solution)/shard_map/ppermute | solution.py:445
  9.7 1.3 %collective-permute-start.1 = (f32[8,640]{1,0:T(8,128)S(1)}, f32[8,640]{1,0:T(8,128)S(1)}, u32[]{:S(2)}, u32[]{:S(2)}) collective-permute-start(f32[8,640]{1,0:T(8,128)S(1)} %get-tuple-element.24), channel_id=1, source_target_pairs={{0,1},{1,0},{2,3},{3,2},{4,5},{5,4},{6,7},{7,6},{8,9},{9,8},{10,11... | collective-permute-start | bytes 61448 | tf_op jit(solution)/shard_map/ppermute | solution.py:445
  11.0 0.0 collective-permute-start.2
  11.1 0.0 copy-done
  11.1 0.0 copy-done.1
  11.1 0.0 copy-done.2
  11.1 0.0 copy-done.3
  11.1 0.0 copy-done.4
  11.1 0.0 copy-done.5
  11.1 3.2 %terminals.1 = (f32[2048,128]{1,0:T(8,128)S(1)}, bf16[512,128]{1,0:T(8,128)(2,1)S(1)}) custom-call(s32[40,128]{1,0:T(8,128)S(1)} %get-tuple-element.21.slot_ref, bf16[32,640]{1,0:T(8,128)(2,1)S(1)} %get-tuple-element.28.inj_ref.inj0_ref, bf16[2048,128]{1,0:T(8,128)(2,1)S(1)} %get-tuple-element.29.hot_ref, bf16[256,2048]{1,0:T(8,128)(2,1)S(1)} %get-tuple-element.30.term_ref, ...), custom_call_target="tpu_custom_call" | custom-call | tf_op jit(solution)/shard_map/terminals/pallas_call | solution.py:508
  14.3 0.0 collective-permute-done.from_far_ref
  14.3 0.0 collective-permute-done.1.from_sub_ref
  14.3 0.0 collective-permute-done.2.from_near_ref
  14.3 2.2 %second.1.started_ref = f32[2048,128]{1,0:T(8,128)} custom-call(s32[2]{0:T(128)S(1)} %pad_add_fusion.place_ref, s32[40,128]{1,0:T(8,128)S(1)} %get-tuple-element.21.slot_ref, f32[8,640]{1,0:T(8,128)S(1)} %collective-permute-done.from_far_ref, f32[8,640]{1,0:T(8,128)S(1)} %collective-permute-done.1.from_sub_ref, ...), custom_call_target="tpu_custom_call" | custom-call | tf_op jit(solution)/shard_map/second/pallas_call | solution.py:517
  16.5 5.4 %all-to-all-start = ((f32[16,128,128]{2,1,0:T(8,128)}), f32[16,128,128]{2,1,0:T(8,128)S(1)}, u32[]{:S(2)}, u32[]{:S(2)}) async-start(f32[16,128,128]{2,1,0:T(8,128)} %bitcast.9), calls=%async_computation | async-start | bytes 2097152 | tf_op jit(solution)/shard_map/all_to_all | solution.py:527
  21.9 3.8 %last_lines.1 = (f32[8,640]{1,0:T(8,128)S(1)}, f32[8,640]{1,0:T(8,128)S(1)}, f32[8,640]{1,0:T(8,128)S(1)}, bf16[2048,1280]{1,0:T(8,128)(2,1)S(1)}, bf16[512,2048]{1,0:T(8,128)(2,1)S(1)}) custom-call(s32[2]{0:T(128)S(1)} %pad_add_fusion.place_ref, s32[40,128]{1,0:T(8,128)S(1)} %get-tuple-element.21.slot_ref, f32[64,128]{1,0:T(8,128)S(1)} %get-tuple-element.22.value_ref, ...), custom_call_target="tpu_custom_call" | custom-call | tf_op jit(solution)/shard_map/last_lines/pallas_call | solution.py:536
  25.7 0.4 collective-permute-start.4
  26.1 3.3 %collective-permute-start.5 = (f32[8,640]{1,0:T(8,128)S(1)}, f32[8,640]{1,0:T(8,128)S(1)}, u32[]{:S(2)}, u32[]{:S(2)}) collective-permute-start(f32[8,640]{1,0:T(8,128)S(1)} %get-tuple-element.36), channel_id=1, source_target_pairs={{2,4},{4,2},{6,8},{8,6},{10,12},{12,10},{14,16},{16,14},{18,20},{2... | collective-permute-start | bytes 61448 | tf_op jit(solution)/shard_map/ppermute | solution.py:445
  29.4 0.4 collective-permute-start.3
  29.8 14.8 %nodes.1 = bf16[1,2048,1280]{2,1,0:T(8,128)(2,1)} custom-call(bf16[2048,1280]{1,0:T(8,128)(2,1)S(1)} %get-tuple-element.37.drive_ref, bf16[512,2048]{1,0:T(8,128)(2,1)S(1)} %get-tuple-element.38.head_ref, f32[1,2048]{1,0:T(1,128)S(1)} %get-tuple-element.31.self_ref, bf16[1,2048,2048]{2,1,0:T(8,128)(2,1)} %coupling_hbm.5), custom_call_target="tpu_custom_call" | custom-call | flops 10737418240 | bytes 20000000 | tf_op jit(solution)/shard_map/nodes/pallas_call | solution.py:563
  44.6 0.0 collective-permute-done.3
  44.6 0.0 collective-permute-done.4
  44.6 2.4 %collective-permute-done.5 = f32[8,640]{1,0:T(8,128)S(1)} collective-permute-done((f32[8,640]{1,0:T(8,128)S(1)}, f32[8,640]{1,0:T(8,128)S(1)}, u32[]{:S(2)}, u32[]{:S(2)}) %collective-permute-start.5) | collective-permute-done | bytes 20512 | tf_op jit(solution)/shard_map/ppermute | solution.py:445
  47.0 0.6 %maximum_bitcast_fusion = f32[1,4,8,640]{3,2,1,0:T(8,128)} fusion(f32[1,8,640]{2,1,0:T(8,128)S(1)} %get-tuple-element.40, f32[1,8,640]{2,1,0:T(8,128)S(1)} %get-tuple-element.39, f32[1,8,640]{2,1,0:T(8,128)S(1)} %get-tuple-element.42, f32[1,8,640]{2,1,0:T(8,128)S(1)} %get-tuple-element.41), kind=kLoop, calls=%fused_computation | loop fusion | flops 61440 | bytes 163840 | tf_op jit(solution)/shard_map/broadcast_in_dim | solution.py:553
  47.6 0.0 all-to-all-done
  47.6 1.0 %copy.15 = f32[512,2,2,128]{3,2,1,0:T(2,128)} copy(f32[512,2,2,128]{3,2,1,0:T(2,128)S(1)} %bitcast.18) | data formatting | bytes 2097152
  (4 shorter events, 0.0 us)
Async XLA Ops:
  0.7 10.3 %copy-start = (bf16[1,2048,1280]{2,1,0:T(8,128)(2,1)S(1)}, bf16[1,2048,1280]{2,1,0:T(8,128)(2,1)}, u32[]{:S(2)}) copy-start(bf16[1,2048,1280]{2,1,0:T(8,128)(2,1)} %sources_hbm.3) | copy-start | bytes 15728644
  0.7 10.3 %copy-start.1 = (bf16[640,512]{1,0:T(8,128)(2,1)S(1)}, bf16[640,512]{1,0:T(8,128)(2,1)}, u32[]{:S(2)}) copy-start(bf16[640,512]{1,0:T(8,128)(2,1)} %constant.32.clone.table_ref) | copy-start | bytes 1966084
  0.7 10.3 %copy-start.2 = (bf16[256,1280]{1,0:T(8,128)(2,1)S(1)}, bf16[256,1280]{1,0:T(8,128)(2,1)}, u32[]{:S(2)}) copy-start(bf16[256,1280]{1,0:T(8,128)(2,1)} %old_ref.1) | copy-start | bytes 1966084
  0.7 10.3 %copy-start.3 = (f32[256,2,128]{2,1,0:T(2,128)S(1)}, f32[256,2,128]{2,1,0:T(2,128)}, u32[]{:S(2)}) copy-start(f32[256,2,128]{2,1,0:T(2,128)} %param.19) | copy-start | bytes 786436
  0.7 10.3 %copy-start.4 = (f32[8,128]{1,0:T(8,128)S(1)}, f32[8,128]{1,0:T(8,128)}, u32[]{:S(2)}) copy-start(f32[8,128]{1,0:T(8,128)} %constant.33.clone.turn_ref) | copy-start | bytes 12292
  0.7 10.3 %copy-start.5 = (s32[256,1]{0,1:T(1,128)S(1)}, s32[256,1]{0,1:T(1,128)}, u32[]{:S(2)}) copy-start(s32[256,1]{0,1:T(1,128)} %param.17) | copy-start | bytes 3076
  6.0 8.3 %collective-permute-start = (f32[8,640]{1,0:T(8,128)S(1)}, f32[8,640]{1,0:T(8,128)S(1)}, u32[]{:S(2)}, u32[]{:S(2)}) collective-permute-start(f32[8,640]{1,0:T(8,128)S(1)} %get-tuple-element.23), channel_id=1, source_target_pairs={{2,4},{4,2},{6,8},{8,6},{10,12},{12,10},{14,16},{16,14},{18,20},{2... | collective-permute-start | bytes 61448 | tf_op jit(solution)/shard_map/ppermute | solution.py:445
  9.7 4.6 %collective-permute-start.1 = (f32[8,640]{1,0:T(8,128)S(1)}, f32[8,640]{1,0:T(8,128)S(1)}, u32[]{:S(2)}, u32[]{:S(2)}) collective-permute-start(f32[8,640]{1,0:T(8,128)S(1)} %get-tuple-element.24), channel_id=1, source_target_pairs={{0,1},{1,0},{2,3},{3,2},{4,5},{5,4},{6,7},{7,6},{8,9},{9,8},{10,11... | collective-permute-start | bytes 61448 | tf_op jit(solution)/shard_map/ppermute | solution.py:445
  11.0 3.2 %collective-permute-start.2 = (f32[8,640]{1,0:T(8,128)S(1)}, f32[8,640]{1,0:T(8,128)S(1)}, u32[]{:S(2)}, u32[]{:S(2)}) collective-permute-start(f32[8,640]{1,0:T(8,128)S(1)} %get-tuple-element.25), channel_id=1, source_target_pairs={{0,2},{2,0},{4,6},{6,4},{8,10},{10,8},{12,14},{14,12},{16,18},{18,... | collective-permute-start | bytes 61448 | tf_op jit(solution)/shard_map/ppermute | solution.py:445
  16.5 31.1 %all-to-all-start = ((f32[16,128,128]{2,1,0:T(8,128)}), f32[16,128,128]{2,1,0:T(8,128)S(1)}, u32[]{:S(2)}, u32[]{:S(2)}) async-start(f32[16,128,128]{2,1,0:T(8,128)} %bitcast.9), calls=%async_computation | async-start | bytes 2097152 | tf_op jit(solution)/shard_map/all_to_all | solution.py:527
  25.7 18.9 %collective-permute-start.4 = (f32[8,640]{1,0:T(8,128)S(1)}, f32[8,640]{1,0:T(8,128)S(1)}, u32[]{:S(2)}, u32[]{:S(2)}) collective-permute-start(f32[8,640]{1,0:T(8,128)S(1)} %get-tuple-element.35), channel_id=1, source_target_pairs={{0,2},{2,0},{4,6},{6,4},{8,10},{10,8},{12,14},{14,12},{16,18},{18,... | collective-permute-start | bytes 61448 | tf_op jit(solution)/shard_map/ppermute | solution.py:445
  26.1 20.9 %collective-permute-start.5 = (f32[8,640]{1,0:T(8,128)S(1)}, f32[8,640]{1,0:T(8,128)S(1)}, u32[]{:S(2)}, u32[]{:S(2)}) collective-permute-start(f32[8,640]{1,0:T(8,128)S(1)} %get-tuple-element.36), channel_id=1, source_target_pairs={{2,4},{4,2},{6,8},{8,6},{10,12},{12,10},{14,16},{16,14},{18,20},{2... | collective-permute-start | bytes 61448 | tf_op jit(solution)/shard_map/ppermute | solution.py:445
  29.4 15.2 %collective-permute-start.3 = (f32[8,640]{1,0:T(8,128)S(1)}, f32[8,640]{1,0:T(8,128)S(1)}, u32[]{:S(2)}, u32[]{:S(2)}) collective-permute-start(f32[8,640]{1,0:T(8,128)S(1)} %get-tuple-element.34), channel_id=1, source_target_pairs={{0,1},{1,0},{2,3},{3,2},{4,5},{5,4},{6,7},{7,6},{8,9},{9,8},{10,11... | collective-permute-start | bytes 61448 | tf_op jit(solution)/shard_map/ppermute | solution.py:445

commit v6 on v5

--- a/solution.py
+++ b/solution.py
@@ -298,11 +298,7 @@
     _, injection = injected(lines, along, down)
     both = dot(injection, table_ref[...])
     high, low = split(turned(both[:, :PHASOR] + both[:, PHASOR:], turn_ref))
-    left = left_ref[...]
-    change = dot(
-        jnp.concatenate([left, left], axis=1),
-        jnp.concatenate([three_times(high), three_times(low)], axis=0),
-    )
+    right = jnp.concatenate([three_times(high), three_times(low)], axis=0)
     chunks = 4
     depth = slots // chunks
 
@@ -311,13 +307,13 @@
         return pltpu.make_async_copy(packed_ref.at[rows], packed_hbm.at[rows], sems.at[chunk])
 
     for chunk in range(chunks):
+        left = left_ref[chunk * depth : (chunk + 1) * depth, :]
+        change = dot(jnp.concatenate([left, left], axis=1), right)
         for part in range(4):
             rows = pl.ds(chunk * depth * 4 + part, depth, stride=4)
             values = packed_in_ref[rows, :]
             if part >= 2:
-                values = values + change[
-                    chunk * depth : (chunk + 1) * depth, (part - 2) * LANES : (part - 1) * LANES
-                ]
+                values = values + change[:, (part - 2) * LANES : (part - 1) * LANES]
             packed_ref[rows, :] = values
         send(chunk).start()
     for chunk in range(chunks):

time: 49 us -> 48.9 us (level)
  no operation moved by 1% of the time
where the time goes in v6:
time: 48.9 us; the launch traced here: 48.6 us
  Pallas kernels  29.1 us (60%)
  starting transfers between devices  14.5 us (30%)
  waiting for transfers between devices  2.46 us (5%)
  local copies, waits for them, and re-layouts  1 us (2%)
  between operations  0.81 us (2%)
  other arithmetic  0.73 us (1%)
    pallas_call x1, Pallas kernels, body(): pl.pallas_call(nodes_kernel, out_shape=struct((1, NODES, SPANS * COLS), B...  14.8 us
    ppermute x6, starting transfers between devices, swap(): return lax.ppermute(block, axis, pairs)  9.22 us
    all_to_all x1, starting transfers between devices, body(): lax.all_to_all(packed.reshape(region_count, capacity * 4, LANES), 'region...  5.23 us
    pallas_call x1, Pallas kernels, body(): pl.pallas_call(lines_kernel, out_shape=[block, block, block, struct((NODE...  5.23 us
    pallas_call x1, Pallas kernels, body(): pl.pallas_call(last_lines_kernel, out_shape=[block, block, block, struct(...  3.76 us
    pallas_call x1, Pallas kernels, body(): pl.pallas_call(functools.partial(terminals_kernel, capacity, slots), out_...  3.16 us
    ppermute x6, waiting for transfers between devices, swap(): return lax.ppermute(block, axis, pairs)  2.46 us
    pallas_call x1, Pallas kernels, body(): pl.pallas_call(functools.partial(second_kernel, slots), out_shape=struct(...  2.2 us
  transfers between devices with their start and end apart: 7, of which 1 were waited for; matrix products, arithmetic and copies ran while one was open for 1% of the time, Pallas kernels for 45%

profile of v6, /device:TPU:13, one launch (start us, length us, event | category | flops | bytes accessed | tf_op | source)
XLA Modules:
  0.0 48.6 jit_solution(9945455749757446232)
XLA Ops:
  0.6 0.1 pad_add_fusion.place_ref
  0.7 0.0 copy-start
  0.7 0.0 copy-start.1
  0.7 0.0 copy-start.4
  0.7 0.0 copy-start.5
  0.8 5.2 %lines.1 = (f32[8,640]{1,0:T(8,128)S(1)}, f32[8,640]{1,0:T(8,128)S(1)}, f32[8,640]{1,0:T(8,128)S(1)}, bf16[2048,128]{1,0:T(8,128)(2,1)S(1)}, bf16[256,2048]{1,0:...) custom-call(s32[2]{0:T(128)S(1)} %pad_add_fusion.place_ref, ...), custom_call_target="tpu_custom_call" | custom-call | tf_op jit(solution)/shard_map/lines/pallas_call | solution.py:471
  6.0 3.8 %collective-permute-start = (f32[8,640]{1,0:T(8,128)S(1)}, f32[8,640]{1,0:T(8,128)S(1)}, u32[]{:S(2)}, u32[]{:S(2)}) collective-permute-start(f32[8,640]{1,0:T(8,128)S(1)} %get-tuple-element.23), channel_id=1, source_target_pairs={{2,4},{4,2},{6,8},{8,6},{10,12},{12,10},{14,16},{16,14},{18,20},{2... | collective-permute-start | bytes 61448 | tf_op jit(solution)/shard_map/ppermute | solution.py:441
  9.8 1.4 %collective-permute-start.1 = (f32[8,640]{1,0:T(8,128)S(1)}, f32[8,640]{1,0:T(8,128)S(1)}, u32[]{:S(2)}, u32[]{:S(2)}) collective-permute-start(f32[8,640]{1,0:T(8,128)S(1)} %get-tuple-element.24), channel_id=1, source_target_pairs={{0,1},{1,0},{2,3},{3,2},{4,5},{5,4},{6,7},{7,6},{8,9},{9,8},{10,11... | collective-permute-start | bytes 61448 | tf_op jit(solution)/shard_map/ppermute | solution.py:441
  11.2 0.0 collective-permute-start.2
  11.2 0.0 copy-done
  11.2 0.0 copy-done.1
  11.2 0.0 copy-done.2
  11.2 0.0 copy-done.3
  11.2 0.0 copy-done.4
  11.2 0.0 copy-done.5
  11.2 3.2 %terminals.1 = (f32[2048,128]{1,0:T(8,128)S(1)}, bf16[512,128]{1,0:T(8,128)(2,1)S(1)}) custom-call(s32[40,128]{1,0:T(8,128)S(1)} %get-tuple-element.21.slot_ref, bf16[32,640]{1,0:T(8,128)(2,1)S(1)} %get-tuple-element.28.inj_ref.inj0_ref, bf16[2048,128]{1,0:T(8,128)(2,1)S(1)} %get-tuple-element.29.hot_ref, bf16[256,2048]{1,0:T(8,128)(2,1)S(1)} %get-tuple-element.30.term_ref, ...), custom_call_target="tpu_custom_call" | custom-call | tf_op jit(solution)/shard_map/terminals/pallas_call | solution.py:504
  14.4 0.0 collective-permute-done.from_far_ref
  14.4 0.0 collective-permute-done.1.from_sub_ref
  14.4 0.0 collective-permute-done.2.from_near_ref
  14.4 2.2 %second.1.started_ref = f32[2048,128]{1,0:T(8,128)} custom-call(s32[2]{0:T(128)S(1)} %pad_add_fusion.place_ref, s32[40,128]{1,0:T(8,128)S(1)} %get-tuple-element.21.slot_ref, f32[8,640]{1,0:T(8,128)S(1)} %collective-permute-done.from_far_ref, f32[8,640]{1,0:T(8,128)S(1)} %collective-permute-done.1.from_sub_ref, ...), custom_call_target="tpu_custom_call" | custom-call | tf_op jit(solution)/shard_map/second/pallas_call | solution.py:513
  16.6 5.2 %all-to-all-start = ((f32[16,128,128]{2,1,0:T(8,128)}), f32[16,128,128]{2,1,0:T(8,128)S(1)}, u32[]{:S(2)}, u32[]{:S(2)}) async-start(f32[16,128,128]{2,1,0:T(8,128)} %bitcast.9), calls=%async_computation | async-start | bytes 2097152 | tf_op jit(solution)/shard_map/all_to_all | solution.py:523
  21.9 3.8 %last_lines.1 = (f32[8,640]{1,0:T(8,128)S(1)}, f32[8,640]{1,0:T(8,128)S(1)}, f32[8,640]{1,0:T(8,128)S(1)}, bf16[2048,1280]{1,0:T(8,128)(2,1)S(1)}, bf16[512,2048]{1,0:T(8,128)(2,1)S(1)}) custom-call(s32[2]{0:T(128)S(1)} %pad_add_fusion.place_ref, s32[40,128]{1,0:T(8,128)S(1)} %get-tuple-element.21.slot_ref, f32[64,128]{1,0:T(8,128)S(1)} %get-tuple-element.22.value_ref, ...), custom_call_target="tpu_custom_call" | custom-call | tf_op jit(solution)/shard_map/last_lines/pallas_call | solution.py:532
  25.6 0.4 collective-permute-start.4
  26.1 3.3 %collective-permute-start.5 = (f32[8,640]{1,0:T(8,128)S(1)}, f32[8,640]{1,0:T(8,128)S(1)}, u32[]{:S(2)}, u32[]{:S(2)}) collective-permute-start(f32[8,640]{1,0:T(8,128)S(1)} %get-tuple-element.36), channel_id=1, source_target_pairs={{2,4},{4,2},{6,8},{8,6},{10,12},{12,10},{14,16},{16,14},{18,20},{2... | collective-permute-start | bytes 61448 | tf_op jit(solution)/shard_map/ppermute | solution.py:441
  29.4 0.3 collective-permute-start.3
  29.7 14.8 %nodes.1 = bf16[1,2048,1280]{2,1,0:T(8,128)(2,1)} custom-call(bf16[2048,1280]{1,0:T(8,128)(2,1)S(1)} %get-tuple-element.37.drive_ref, bf16[512,2048]{1,0:T(8,128)(2,1)S(1)} %get-tuple-element.38.head_ref, f32[1,2048]{1,0:T(1,128)S(1)} %get-tuple-element.31.self_ref, bf16[1,2048,2048]{2,1,0:T(8,128)(2,1)} %coupling_hbm.5), custom_call_target="tpu_custom_call" | custom-call | flops 10737418240 | bytes 20000000 | tf_op jit(solution)/shard_map/nodes/pallas_call | solution.py:559
  44.5 0.0 collective-permute-done.3
  44.5 0.0 collective-permute-done.4
  44.5 2.4 %collective-permute-done.5 = f32[8,640]{1,0:T(8,128)S(1)} collective-permute-done((f32[8,640]{1,0:T(8,128)S(1)}, f32[8,640]{1,0:T(8,128)S(1)}, u32[]{:S(2)}, u32[]{:S(2)}) %collective-permute-start.5) | collective-permute-done | bytes 20512 | tf_op jit(solution)/shard_map/ppermute | solution.py:441
  47.0 0.6 %maximum_bitcast_fusion = f32[1,4,8,640]{3,2,1,0:T(8,128)} fusion(f32[1,8,640]{2,1,0:T(8,128)S(1)} %get-tuple-element.40, f32[1,8,640]{2,1,0:T(8,128)S(1)} %get-tuple-element.39, f32[1,8,640]{2,1,0:T(8,128)S(1)} %get-tuple-element.42, f32[1,8,640]{2,1,0:T(8,128)S(1)} %get-tuple-element.41), kind=kLoop, calls=%fused_computation | loop fusion | flops 61440 | bytes 163840 | tf_op jit(solution)/shard_map/broadcast_in_dim | solution.py:549
  47.6 0.0 all-to-all-done
  47.6 1.0 %copy.15 = f32[512,2,2,128]{3,2,1,0:T(2,128)} copy(f32[512,2,2,128]{3,2,1,0:T(2,128)S(1)} %bitcast.18) | data formatting | bytes 2097152
  (4 shorter events, 0.0 us)
Async XLA Ops:
  0.7 10.5 %copy-start = (bf16[1,2048,1280]{2,1,0:T(8,128)(2,1)S(1)}, bf16[1,2048,1280]{2,1,0:T(8,128)(2,1)}, u32[]{:S(2)}) copy-start(bf16[1,2048,1280]{2,1,0:T(8,128)(2,1)} %sources_hbm.3) | copy-start | bytes 15728644
  0.7 10.5 %copy-start.1 = (bf16[640,512]{1,0:T(8,128)(2,1)S(1)}, bf16[640,512]{1,0:T(8,128)(2,1)}, u32[]{:S(2)}) copy-start(bf16[640,512]{1,0:T(8,128)(2,1)} %constant.32.clone.table_ref) | copy-start | bytes 1966084
  0.7 10.5 %copy-start.2 = (bf16[256,1280]{1,0:T(8,128)(2,1)S(1)}, bf16[256,1280]{1,0:T(8,128)(2,1)}, u32[]{:S(2)}) copy-start(bf16[256,1280]{1,0:T(8,128)(2,1)} %old_ref.1) | copy-start | bytes 1966084
  0.7 10.5 %copy-start.3 = (f32[256,2,128]{2,1,0:T(2,128)S(1)}, f32[256,2,128]{2,1,0:T(2,128)}, u32[]{:S(2)}) copy-start(f32[256,2,128]{2,1,0:T(2,128)} %param.19) | copy-start | bytes 786436
  0.7 10.5 %copy-start.4 = (f32[8,128]{1,0:T(8,128)S(1)}, f32[8,128]{1,0:T(8,128)}, u32[]{:S(2)}) copy-start(f32[8,128]{1,0:T(8,128)} %constant.33.clone.turn_ref) | copy-start | bytes 12292
  0.7 10.5 %copy-start.5 = (s32[256,1]{0,1:T(1,128)S(1)}, s32[256,1]{0,1:T(1,128)}, u32[]{:S(2)}) copy-start(s32[256,1]{0,1:T(1,128)} %param.17) | copy-start | bytes 3076
  6.0 8.4 %collective-permute-start = (f32[8,640]{1,0:T(8,128)S(1)}, f32[8,640]{1,0:T(8,128)S(1)}, u32[]{:S(2)}, u32[]{:S(2)}) collective-permute-start(f32[8,640]{1,0:T(8,128)S(1)} %get-tuple-element.23), channel_id=1, source_target_pairs={{2,4},{4,2},{6,8},{8,6},{10,12},{12,10},{14,16},{16,14},{18,20},{2... | collective-permute-start | bytes 61448 | tf_op jit(solution)/shard_map/ppermute | solution.py:441
  9.8 4.6 %collective-permute-start.1 = (f32[8,640]{1,0:T(8,128)S(1)}, f32[8,640]{1,0:T(8,128)S(1)}, u32[]{:S(2)}, u32[]{:S(2)}) collective-permute-start(f32[8,640]{1,0:T(8,128)S(1)} %get-tuple-element.24), channel_id=1, source_target_pairs={{0,1},{1,0},{2,3},{3,2},{4,5},{5,4},{6,7},{7,6},{8,9},{9,8},{10,11... | collective-permute-start | bytes 61448 | tf_op jit(solution)/shard_map/ppermute | solution.py:441
  11.2 3.2 %collective-permute-start.2 = (f32[8,640]{1,0:T(8,128)S(1)}, f32[8,640]{1,0:T(8,128)S(1)}, u32[]{:S(2)}, u32[]{:S(2)}) collective-permute-start(f32[8,640]{1,0:T(8,128)S(1)} %get-tuple-element.25), channel_id=1, source_target_pairs={{0,2},{2,0},{4,6},{6,4},{8,10},{10,8},{12,14},{14,12},{16,18},{18,... | collective-permute-start | bytes 61448 | tf_op jit(solution)/shard_map/ppermute | solution.py:441
  16.6 31.0 %all-to-all-start = ((f32[16,128,128]{2,1,0:T(8,128)}), f32[16,128,128]{2,1,0:T(8,128)S(1)}, u32[]{:S(2)}, u32[]{:S(2)}) async-start(f32[16,128,128]{2,1,0:T(8,128)} %bitcast.9), calls=%async_computation | async-start | bytes 2097152 | tf_op jit(solution)/shard_map/all_to_all | solution.py:523
  25.6 18.9 %collective-permute-start.4 = (f32[8,640]{1,0:T(8,128)S(1)}, f32[8,640]{1,0:T(8,128)S(1)}, u32[]{:S(2)}, u32[]{:S(2)}) collective-permute-start(f32[8,640]{1,0:T(8,128)S(1)} %get-tuple-element.35), channel_id=1, source_target_pairs={{0,2},{2,0},{4,6},{6,4},{8,10},{10,8},{12,14},{14,12},{16,18},{18,... | collective-permute-start | bytes 61448 | tf_op jit(solution)/shard_map/ppermute | solution.py:441
  26.1 20.9 %collective-permute-start.5 = (f32[8,640]{1,0:T(8,128)S(1)}, f32[8,640]{1,0:T(8,128)S(1)}, u32[]{:S(2)}, u32[]{:S(2)}) collective-permute-start(f32[8,640]{1,0:T(8,128)S(1)} %get-tuple-element.36), channel_id=1, source_target_pairs={{2,4},{4,2},{6,8},{8,6},{10,12},{12,10},{14,16},{16,14},{18,20},{2... | collective-permute-start | bytes 61448 | tf_op jit(solution)/shard_map/ppermute | solution.py:441
  29.4 15.1 %collective-permute-start.3 = (f32[8,640]{1,0:T(8,128)S(1)}, f32[8,640]{1,0:T(8,128)S(1)}, u32[]{:S(2)}, u32[]{:S(2)}) collective-permute-start(f32[8,640]{1,0:T(8,128)S(1)} %get-tuple-element.34), channel_id=1, source_target_pairs={{0,1},{1,0},{2,3},{3,2},{4,5},{5,4},{6,7},{7,6},{8,9},{9,8},{10,11... | collective-permute-start | bytes 61448 | tf_op jit(solution)/shard_map/ppermute | solution.py:441
